TPU v7x, 256 devices: a whole 4x4x8 slice. The times are simulated.
256 devices in a mesh: outer: 8 (over y, core), rep: 32 (over x, z).
Axes of the slice: x: 4, y: 4, z: 8, core: 2. Of those that a mesh axis runs over, the one named last changes fastest.
Arguments:
- gradients: bfloat16 [8, 4096, 14336], P('outer', 'rep'), may hold values from -12 to 12
- residual: bfloat16 [8, 4096, 14336], P('outer', 'rep'), may hold values from -3 to 3
- sketch: bfloat16 [32, 14336], replicated, may hold values from -0.046875 to 0.046875
Outputs:
- left_basis: float32 [32, 4096], P(None, 'rep')
- right_factor: float32 [32, 14336], P(None, 'rep')
- new_residual: bfloat16 [8, 4096, 14336], P('outer', 'rep')
All inputs are finite; a program needn't handle non-finite values.
Results may differ from a plain program's by a relative error of at most 0.001.
Values sent between devices are 32-bit elements; how exact they have to be, the bound alone decides.
No kernel may reach another device: no remote copies, remote signals or barrier semaphores. Data moves between devices by JAX's collectives and lax.ppermute only.
A program may use at most 64 MiB of HBM per device.

v0:
```python
import jax
import jax.numpy as jnp
from jax import lax
from jax.sharding import PartitionSpec as P


def on_device(gradients, residual, sketch):
    merged = gradients[0].astype(jnp.float32) + residual[0].astype(jnp.float32)
    groups = lax.axis_size("outer")
    probe_rows = sketch.astype(jnp.float32)
    partial_value = lax.dot_general(
        probe_rows, merged, (((1,), (1,)), ((), ())), precision=lax.Precision.HIGHEST
    )
    summed = lax.psum(partial_value, "outer") / groups
    gram_local = jnp.dot(summed, summed.T, precision=lax.Precision.HIGHEST)
    gram_matrix = lax.psum(gram_local, "rep")
    lower_factor = jnp.linalg.cholesky(gram_matrix)
    left_basis = jax.scipy.linalg.solve_triangular(lower_factor, summed, lower=True)
    contrib = jnp.dot(left_basis, merged, precision=lax.Precision.HIGHEST)
    right_factor = lax.psum(contrib, ("outer", "rep")) / groups
    slice_width = right_factor.shape[1] // lax.axis_size("rep")
    own_share = lax.dynamic_slice_in_dim(
        right_factor, lax.axis_index("rep") * slice_width, slice_width, 1
    )
    update = lax.dot_general(
        left_basis, right_factor, (((0,), (0,)), ((), ())), precision=lax.Precision.HIGHEST
    )
    new_residual = (merged - update).astype(jnp.bfloat16)[None]
    return (left_basis, own_share, new_residual)


def solution(mesh):
    return jax.shard_map(
        on_device,
        mesh=mesh,
        in_specs=(P("outer", "rep", None), P("outer", "rep", None), P()),
        out_specs=(P(None, "rep"), P(None, "rep"), P("outer", "rep", None)),
        check_vma=False,
    )
```

profile of v0, /device:TPU:1, one launch (start us, length us, event | category | flops | bytes accessed | tf_op | source)
XLA Modules:
  0.0 471.3 jit_solution(15172546119920418794)
XLA Ops:
  7.2 0.0 copy-start
  7.2 0.0 all-reduce.2.cloned.1.call-start
  7.2 1.1 copy-done
  8.3 6.8 %fusion.6 = f32[32,128]{1,0:T(8,128)S(1)} fusion(bf16[32,14336]{1,0:T(8,128)(2,1)S(1)} %copy-done, bf16[1,128,14336]{2,1,0:T(8,128)(2,1)} %param.4, bf16[1,128,14336]{2,1,0:T(8,128)(2,1)} %param.3), kind=kOutput, calls=%fused_computation.8 | convolution fusion | flops 710148096 | bytes 8273920 | tf_op jit(solution)/shard_map/dot_general | solution.py:11
  15.1 23.8 %psum.21 = f32[32,128]{1,0:T(8,128)S(1)} all-reduce(f32[32,128]{1,0:T(8,128)S(1)} %fusion.6), channel_id=1, replica_groups=mesh['outer'=8,'rep'=32] {'outer'}, use_global_device_ids=true, to_apply=%region_0.0 | all-reduce | flops 4096 | bytes 32768 | tf_op jit(solution)/shard_map/psum | solution.py:14
  38.9 0.1 fusion.14
  39.1 118.1 %psum.22 = f32[32,32]{0,1:T(8,128)S(1)} all-reduce(f32[32,32]{0,1:T(8,128)S(1)} %fusion.14), channel_id=1, replica_groups=mesh['outer'=8,'rep'=32] {'rep'}, use_global_device_ids=true, to_apply=%region_1.0 | all-reduce | flops 1024 | bytes 8192 | tf_op jit(solution)/shard_map/psum | solution.py:16
  157.2 0.1 copy.7
  157.3 2.9 cholesky.16
  160.2 0.6 compare_reduce_fusion
  160.9 0.7 fusion.9
  161.5 2.4 custom-call.7
  164.0 0.2 fusion.10
  164.2 0.0 copy-start.2
  164.2 7.7 %fusion.2 = f32[32,14336]{1,0:T(8,128)} fusion(f32[32,128]{1,0:T(8,128)S(1)} %fusion.10, bf16[1,128,14336]{2,1,0:T(8,128)(2,1)} %param.4, bf16[1,128,14336]{2,1,0:T(8,128)(2,1)} %param.3), kind=kOutput, calls=%fused_computation.3 | convolution fusion | flops 710148096 | bytes 9191424 | tf_op jit(solution)/shard_map/dot_general | solution.py:19
  172.0 0.0 all-reduce.2.cloned.1.call-update
  172.0 280.1 %all-reduce.2.cloned.1.call-done = f32[32,14336]{1,0:T(8,128)} async-done(((f32[32,14336]{1,0:T(8,128)}), f32[32,14336]{1,0:T(8,128)}) %all-reduce.2.cloned.1.call-update) | async-done | bytes 1835024 | tf_op jit(solution)/shard_map/psum | solution.py:20
  452.1 0.0 copy-start.1
  452.1 1.8 broadcast_multiply_fusion
  453.9 0.7 constant_dynamic-slice_fusion
  454.6 0.0 copy-done.2
  454.6 0.1 copy-done.1
  454.7 9.8 %fusion.1 = bf16[1,128,14336]{2,1,0:T(8,128)(2,1)} fusion(f32[32,128]{1,0:T(8,128)S(1)} %fusion.10, bf16[1,128,14336]{2,1,0:T(8,128)(2,1)S(1)} %copy-done.1, bf16[1,128,14336]{2,1,0:T(8,128)(2,1)} %param.3, f32[32,14336]{1,0:T(8,128)} %all-reduce.2.cloned.1.call-done), kind=kOutput, calls=%fused_computation.2 | convolution fusion | flops 714276864 | bytes 12861440 | tf_op jit(solution)/shard_map/dot_general | solution.py:25
  (2 shorter events, 0.0 us)
Async XLA Ops:
  7.2 1.2 copy-start
  7.2 444.9 %all-reduce.2.cloned.1.call-start = ((), (), s32[]{:S(2)}) async-start(), calls=%async_computation | async-start | bytes 3670016 | tf_op jit(solution)/shard_map/psum | solution.py:20
  164.2 290.4 %copy-start.2 = (f32[32,128]{1,0:T(8,128)}, f32[32,128]{1,0:T(8,128)S(1)}, u32[]{:S(2)}) copy-start(f32[32,128]{1,0:T(8,128)S(1)} %fusion.10) | copy-start | bytes 49156
  452.1 2.6 copy-start.1
Sparse Core Ops, SparseCore 0:
  172.1 279.9 all-reduce.1
where the time goes:
time: 472 us; the launch traced here: 471 us
  waiting for transfers between devices  280 us (59%)
  blocking collectives  142 us (30%)
  matrix products  24.6 us (5%)
  between operations  14.1 us (3%)
  other arithmetic  8.46 us (2%)
    psum x1, waiting for transfers between devices, on_device(): right_factor = lax.psum(contrib, ('outer', 'rep')) / groups  280 us
    psum x1, blocking collectives, on_device(): gram_matrix = lax.psum(gram_local, 'rep')  118 us
    psum x1, blocking collectives, on_device(): summed = lax.psum(partial_value, 'outer') / groups  23.8 us
    dot_general x1, matrix products, on_device(): lax.dot_general(left_basis, right_factor, (((0,), (0,)), ((), ())), preci...  9.77 us
  transfers between devices with their start and end apart: 1, of which 1 were waited for; matrix products, arithmetic and copies ran while one was open for 0% of the time, Pallas kernels for 0%

commit v1 on v0

v1 whole, which is shorter than its diff:
```python
import jax
import jax.numpy as jnp
from jax import lax
from jax.experimental import pallas as pl
from jax.experimental.pallas import tpu as pltpu
from jax.sharding import Mesh
from jax.sharding import PartitionSpec as P

AXES = ("y", "c", "x", "z4", "z2", "z1")
SIZES = (4, 2, 4, 2, 2, 2)
SPREAD = ("y", "x", "z1")
ROWS = 128
FF = 14336
RANK = 32
CHUNKS = 16
WIDTH = FF // CHUNKS
TILES = WIDTH // 128
LOADS = 8
LOAD_WIDTH = FF // LOADS
F32 = jnp.float32
BF16 = jnp.bfloat16
MB = 1024 * 1024

ANY = pl.BlockSpec(memory_space=pl.ANY)
VMEM = pl.BlockSpec(memory_space=pltpu.VMEM)
SMEM = pl.BlockSpec(memory_space=pltpu.SMEM)


def params(limit):
    return pltpu.CompilerParams(vmem_limit_bytes=limit)


def three_parts(value):
    first = value.astype(BF16).astype(F32)
    rest = value - first
    second = rest.astype(BF16).astype(F32)
    return first, second, rest - second


def sketch_kernel(grad_hbm, memory_hbm, sketch_hbm, out_ref, grad_ref, memory_ref, sketch_ref, sems):
    copies = []
    for step in range(LOADS):
        cols = pl.ds(step * LOAD_WIDTH, LOAD_WIDTH)
        group = [
            pltpu.make_async_copy(src.at[:, cols], dst.at[:, cols], sems.at[step, which])
            for which, (src, dst) in enumerate(
                ((sketch_hbm, sketch_ref), (grad_hbm, grad_ref), (memory_hbm, memory_ref))
            )
        ]
        for copy in group:
            copy.start()
        copies.append(group)
    total = jnp.zeros((RANK, ROWS), F32)
    for step in range(LOADS):
        for copy in copies[step]:
            copy.wait()
        cols = pl.ds(step * LOAD_WIDTH, LOAD_WIDTH)
        probe = sketch_ref[:, cols]
        for block in (grad_ref, memory_ref):
            total += lax.dot_general(
                probe, block[:, cols], (((1,), (1,)), ((), ())), preferred_element_type=F32
            )
    out_ref[...] = total


def left_sketch(grad, memory, sketch):
    return pl.pallas_call(
        sketch_kernel,
        out_shape=(
            jax.ShapeDtypeStruct((RANK, ROWS), F32),
            pltpu.VMEM((ROWS, FF), BF16),
            pltpu.VMEM((ROWS, FF), BF16),
        ),
        in_specs=[ANY, ANY, ANY],
        out_specs=(VMEM, VMEM, VMEM),
        scratch_shapes=[pltpu.VMEM((RANK, FF), BF16), pltpu.SemaphoreType.DMA((LOADS, 3))],
        compiler_params=params(16 * MB),
        name="left_sketch",
    )(grad, memory, sketch)


def project_kernel(ids_ref, parts_ref, grad_ref, memory_ref, own_ref, other_ref):
    core = ids_ref[0]
    summed = ((parts_ref[0] + parts_ref[1]) + (parts_ref[2] + parts_ref[3])) * (1.0 / 8)
    tiled = jnp.concatenate([summed] * 4, axis=0)
    square = lax.dot_general(
        summed, tiled, (((1,), (1,)), ((), ())), precision=lax.Precision.HIGHEST, preferred_element_type=F32
    )
    lane = lax.broadcasted_iota(jnp.int32, (8, 128), 1) // 32
    gram = jnp.zeros((8, 128), F32)
    for group in range(4):
        gram = jnp.where(lane == group, square[8 * group : 8 * group + 8], gram)
    groups = [summed[8 * q : 8 * q + 8] for q in range(4)]
    even = core == 0
    ordered = jnp.concatenate(
        [
            jnp.where(even, groups[0], groups[1]),
            jnp.where(even, groups[2], groups[3]),
            jnp.where(even, groups[1], groups[0]),
            jnp.where(even, groups[3], groups[2]),
        ],
        axis=0,
    )
    left = jnp.concatenate(three_parts(ordered), axis=0).astype(BF16)
    left = jnp.concatenate([left, left], axis=1)

    @pl.loop(0, CHUNKS)
    def _(chunk):
        cols = pl.ds(pl.multiple_of(chunk * WIDTH, 128), WIDTH)
        both = jnp.concatenate([grad_ref[:, cols], memory_ref[:, cols]], axis=0)
        product = jnp.dot(left, both, preferred_element_type=F32)
        product = product[:32] + (product[32:64] + product[64:])
        for half, ref in enumerate((own_ref, other_ref)):
            for row in range(2):
                base = 16 * half + 8 * row
                for tile in range(TILES):
                    ref[chunk, row, tile] = product[base : base + 8, 128 * tile : 128 * tile + 128]
                ref[chunk, row, TILES] = gram


def project(ids, parts, grad, memory):
    shape = jax.ShapeDtypeStruct((CHUNKS, 2, TILES + 1, 8, 128), F32)
    return pl.pallas_call(
        project_kernel,
        out_shape=(shape, shape),
        in_specs=[SMEM, VMEM, VMEM, VMEM],
        out_specs=(VMEM, VMEM),
        compiler_params=params(24 * MB),
        name="project",
    )(ids, parts, grad, memory)


def factor_kernel(ids_ref, gram_ref, parts_ref, left_ref, inverse_ref, back_ref):
    core = ids_ref[0]
    rows = lax.broadcasted_iota(jnp.int32, (RANK, 128), 0)
    lanes = lax.broadcasted_iota(jnp.int32, (RANK, 128), 1)
    tile = gram_ref[...] * (1.0 / 8)
    packed = jnp.concatenate([tile] + [pltpu.roll(tile, 128 - 32 * q, 1) for q in (1, 2, 3)], axis=0)
    work = jnp.where(lanes < 32, packed, jnp.where(lanes == rows + 32, 1.0, 0.0))
    basis = ((parts_ref[0] + parts_ref[1]) + (parts_ref[2] + parts_ref[3])) * (1.0 / 8)
    scale = jnp.ones((RANK, 128), F32)
    for step in range(RANK):
        column = jnp.broadcast_to(work[:, step : step + 1], (RANK, 128))
        pivot = column[step : step + 1]
        scale = jnp.where(rows == step, pivot, scale)
        factor = jnp.where(rows > step, column / pivot, 0.0)
        work = work - factor * work[step : step + 1]
        basis = basis - factor * basis[step : step + 1]
    scale = lax.rsqrt(scale)
    left = basis * scale
    left_ref[...] = left
    inverse = pltpu.roll(work * scale, 96, 1)
    inverse = jnp.where(lanes < 32, inverse, 0.0)
    inverse_ref[...] = inverse
    solved = lax.dot_general(
        inverse, left, (((0,), (0,)), ((), ())), precision=lax.Precision.HIGHEST, preferred_element_type=F32
    )[:32] * (1.0 / 8)
    even = core == 0
    groups = [solved[8 * q : 8 * q + 8] for q in range(4)]
    ordered = jnp.concatenate(
        [
            jnp.where(even, groups[0], groups[1]),
            jnp.where(even, groups[2], groups[3]),
            jnp.where(even, groups[1], groups[0]),
            jnp.where(even, groups[3], groups[2]),
        ],
        axis=0,
    )
    one, two, three = three_parts(ordered)
    stack = jnp.concatenate([one, two, three, one, two, one, jnp.zeros((64, 128), F32)], axis=0)
    back_ref[...] = stack.T.astype(BF16)


def factor(ids, gram, parts):
    return pl.pallas_call(
        factor_kernel,
        out_shape=(
            jax.ShapeDtypeStruct((RANK, ROWS), F32),
            jax.ShapeDtypeStruct((RANK, 128), F32),
            jax.ShapeDtypeStruct((ROWS, 256), BF16),
        ),
        in_specs=[SMEM, VMEM, VMEM],
        out_specs=(VMEM, VMEM, VMEM),
        compiler_params=params(8 * MB),
        cost_estimate=pl.CostEstimate(flops=10**6, bytes_accessed=10**6, transcendentals=0),
        name="factor",
    )(ids, gram, parts)


def update_kernel(ids_ref, own_ref, other_ref, inverse_ref, back_ref, grad_ref, memory_ref, share_ref, out_hbm, out_ref, sems):
    even = ids_ref[0] == 0
    back = back_ref[:, :192]

    def block(chunk, tile):
        parts = [ref[chunk, row, tile] for ref in (own_ref, other_ref) for row in range(2)]
        return jnp.concatenate(parts, axis=0)

    @pl.loop(0, CHUNKS)
    def _(chunk):
        cols = pl.ds(pl.multiple_of(chunk * WIDTH, 128), WIDTH)
        right = jnp.concatenate([block(chunk, tile) for tile in range(TILES)], axis=1)
        one, two, three = (part.astype(BF16) for part in three_parts(right))
        stack = jnp.concatenate([one, one, one, two, two, three], axis=0)
        update = jnp.dot(back, stack, preferred_element_type=F32)
        merged = grad_ref[:, cols].astype(F32) + memory_ref[:, cols].astype(F32)
        out_ref[:, cols] = (merged - update).astype(BF16)
        pltpu.make_async_copy(out_ref.at[:, cols], out_hbm.at[:, cols], sems.at[chunk]).start()

    mine, odd = ids_ref[1], ids_ref[2]

    def natural(tile):
        own0, own1, other0, other1 = (ref[mine, row, tile] for ref in (own_ref, other_ref) for row in range(2))
        return jnp.concatenate(
            [
                jnp.where(even, own0, other0),
                jnp.where(even, other0, own0),
                jnp.where(even, own1, other1),
                jnp.where(even, other1, own1),
            ],
            axis=0,
        )

    right = jnp.concatenate([natural(tile) for tile in range(TILES)], axis=1)
    share = jnp.dot(
        inverse_ref[:, :32], right, precision=lax.Precision.HIGHEST, preferred_element_type=F32
    ) * (1.0 / 8)
    half = WIDTH // 2
    share_ref[...] = jnp.where(odd == 0, share[:, :half], share[:, half:])

    for chunk in range(CHUNKS):
        cols = pl.ds(chunk * WIDTH, WIDTH)
        pltpu.make_async_copy(out_ref.at[:, cols], out_hbm.at[:, cols], sems.at[chunk]).wait()


def finish(ids, own, other, inverse, back, grad, memory):
    return pl.pallas_call(
        update_kernel,
        out_shape=(
            jax.ShapeDtypeStruct((RANK, WIDTH // 2), F32),
            jax.ShapeDtypeStruct((ROWS, FF), BF16),
        ),
        in_specs=[SMEM] + [VMEM] * 6,
        out_specs=(VMEM, ANY),
        scratch_shapes=[pltpu.VMEM((ROWS, FF), BF16), pltpu.SemaphoreType.DMA((CHUNKS,))],
        compiler_params=params(24 * MB),
        name="finish",
    )(ids, own, other, inverse, back, grad, memory)


def exchange(value, axes):
    return lax.all_to_all(value, axes, 0, 0, tiled=True)


def swap(value):
    return lax.ppermute(value, "c", [(0, 1), (1, 0)])


def spread(value, axes, count):
    return exchange(jnp.broadcast_to(value[None], (count,) + value.shape), axes)


def resident(value):
    return pltpu.with_memory_space_constraint(value, pltpu.VMEM)


def on_device(gradients, residual, sketch):
    core = lax.axis_index("c")
    block = lax.axis_index(("x", "z4", "z2"))
    ids = jnp.stack([core, block, lax.axis_index("z1")]).astype(jnp.int32)
    partial, grad, memory = left_sketch(gradients[0], residual[0], sketch)
    pair = partial + swap(partial)
    parts = spread(pair, "y", 4)
    own, other = project(ids, parts, resident(grad), resident(memory))
    terms = own + swap(other)
    terms = exchange(terms.reshape(32, TILES + 1, 8, 128), SPREAD)
    terms = jnp.sum(terms, axis=0)
    terms = jnp.sum(spread(terms, ("z4", "z2"), 4).reshape((4,) + terms.shape), axis=0)
    gathered = spread(terms[:TILES], SPREAD, 32).reshape(CHUNKS, 2, TILES, 8, 128)
    gathered_other = swap(gathered)
    left, inverse, back = factor(ids, terms[TILES], parts)
    share, fresh = finish(ids, gathered, gathered_other, inverse, back, resident(grad), resident(memory))
    return left, share, fresh[None]


def solution(mesh):
    fine = Mesh(mesh.devices.reshape(SIZES), AXES)
    outer, rep = ("y", "c"), ("x", "z4", "z2", "z1")
    return jax.shard_map(
        on_device,
        mesh=fine,
        in_specs=(P(outer, rep, None), P(outer, rep, None), P()),
        out_specs=(P(None, rep), P(None, rep), P(outer, rep, None)),
        check_vma=False,
    )
```

time: 472 us -> 113 us (0.24)
  waiting for transfers between devices: 280 us -> 7.49 us
  blocking collectives: 142 us -> 54.1 us
  matrix products: 24.6 us -> 0 us
  Pallas kernels: 0 us -> 20.5 us
  local copies, waits for them, and re-layouts: 2.02 us -> 17.7 us
  between operations: 14.1 us -> 0.72 us
  starting transfers between devices: 0.04 us -> 12.1 us
  other arithmetic: 8.46 us -> 0.33 us
    psum x1 -> x0, waiting for transfers between devices: 280 us -> none  [on_device(): right_factor = lax.psum(contrib, ('outer', 'rep')) / groups]
    psum x2 -> x0, blocking collectives: 142 us -> none  [the longest x1 118 us: on_device(): gram_matrix = lax.psum(gram_local, 'rep')]
    all_to_all x0 -> x3, blocking collectives: none -> 54.1 us  [exchange(): return lax.all_to_all(value, axes, 0, 0, tiled=True)]
    dot_general x4 -> x0, matrix products: 24.4 us -> none  [the longest x1 9.77 us: on_device(): lax.dot_general(left_basis, right_factor, (((0,), (0,)), ((), ())), preci...]
    pallas_call x0 -> x4, Pallas kernels: none -> 20.5 us  [the longest x1 5.68 us: finish(): pl.pallas_call(update_kernel, out_shape=(jax.ShapeDtypeStruct((RANK, WIDT...]
    unnamed x6 -> x18, local copies, waits for them, and re-layouts: 1.23 us -> 17 us
    ppermute x0 -> x3, starting transfers between devices: none -> 8.78 us  [swap(): return lax.ppermute(value, 'c', [(0, 1), (1, 0)])]
    another operation x5 -> x1, other arithmetic: 6.68 us -> 0.08 us  [on_device(): ids = jnp.stack([core, block, lax.axis_index('z1')]).astype(jnp.int32)]
  transfers between devices with their start and end apart: 1 -> 4, of which waited for: 1 -> 3; matrix products, arithmetic and copies ran while one was open for 0% -> 0% of each run, Pallas kernels for 0% -> 5%
where the time goes in v1:
time: 113 us
  blocking collectives  54.1 us (48%)
  Pallas kernels  20.5 us (18%)
  local copies, waits for them, and re-layouts  17.7 us (16%)
  starting transfers between devices  12.1 us (11%)
  waiting for transfers between devices  7.49 us (7%)
    all_to_all x3, blocking collectives, exchange(): return lax.all_to_all(value, axes, 0, 0, tiled=True)  54.1 us
    unnamed x18, local copies, waits for them, and re-layouts  17 us
    ppermute x3, starting transfers between devices, swap(): return lax.ppermute(value, 'c', [(0, 1), (1, 0)])  8.78 us
    pallas_call x1, Pallas kernels, finish(): pl.pallas_call(update_kernel, out_shape=(jax.ShapeDtypeStruct((RANK, WIDT...  5.68 us
    pallas_call x1, Pallas kernels, left_sketch(): pl.pallas_call(sketch_kernel, out_shape=(jax.ShapeDtypeStruct((RANK, ROWS...  5.32 us
    pallas_call x1, Pallas kernels, factor(): pl.pallas_call(factor_kernel, out_shape=(jax.ShapeDtypeStruct((RANK, ROWS...  5.11 us
    pallas_call x1, Pallas kernels, project(): pl.pallas_call(project_kernel, out_shape=(shape, shape), in_specs=[SMEM,...  4.36 us
    all_to_all x1, waiting for transfers between devices, exchange(): return lax.all_to_all(value, axes, 0, 0, tiled=True)  4.36 us
  transfers between devices with their start and end apart: 4, of which 3 were waited for; matrix products, arithmetic and copies ran while one was open for 0% of the time, Pallas kernels for 5%

profile of v1, /device:TPU:1, one launch (start us, length us, event | category | flops | bytes accessed | tf_op | source)
XLA Modules:
  0.0 112.9 jit_solution(6301532343080622775)
XLA Ops:
  0.6 0.0 copy-start.6
  0.6 2.0 %copy-done.6 = bf16[1,128,14336]{2,1,0:T(8,128)(2,1)S(1)} copy-done((bf16[1,128,14336]{2,1,0:T(8,128)(2,1)S(1)}, bf16[1,128,14336]{2,1,0:T(8,128)(2,1)}, u32[]{:S(2)}) %copy-start.6) | copy-done | bytes 3670040
  2.7 0.0 copy-start.7
  2.7 2.0 %copy-done.7 = bf16[1,128,14336]{2,1,0:T(8,128)(2,1)S(1)} copy-done((bf16[1,128,14336]{2,1,0:T(8,128)(2,1)S(1)}, bf16[1,128,14336]{2,1,0:T(8,128)(2,1)}, u32[]{:S(2)}) %copy-start.7) | copy-done | bytes 3670040
  4.7 0.0 copy-start.8
  4.7 1.2 %copy-done.8 = bf16[32,14336]{1,0:T(8,128)(2,1)S(1)} copy-done((bf16[32,14336]{1,0:T(8,128)(2,1)S(1)}, bf16[32,14336]{1,0:T(8,128)(2,1)}, u32[]{:S(2)}) %copy-start.8) | copy-done | bytes 917528
  5.9 5.3 %left_sketch.1 = (f32[32,128]{1,0:T(8,128)S(1)}, bf16[128,14336]{1,0:T(8,128)(2,1)S(1)}, bf16[128,14336]{1,0:T(8,128)(2,1)S(1)}) custom-call(bf16[128,14336]{1,0:T(8,128)(2,1)S(1)} %bitcast.12, bf16[128,14336]{1,0:T(8,128)(2,1)S(1)} %bitcast.13, bf16[32,14336]{1,0:T(8,128)(2,1)S(1)} %copy-done.8), custom_call_target="tpu_custom_call" | custom-call | tf_op jit(solution)/shard_map/left_sketch/pallas_call | solution.py:67
  11.2 0.0 copy-start
  11.2 1.8 %copy-done = bf16[128,14336]{1,0:T(8,128)(2,1)} copy-done((bf16[128,14336]{1,0:T(8,128)(2,1)}, bf16[128,14336]{1,0:T(8,128)(2,1)S(1)}, u32[]{:S(2)}) %copy-start) | copy-done | bytes 3670040
  13.1 0.0 copy-start.3
  13.1 1.8 %copy-done.3 = bf16[128,14336]{1,0:T(8,128)(2,1)} copy-done((bf16[128,14336]{1,0:T(8,128)(2,1)}, bf16[128,14336]{1,0:T(8,128)(2,1)S(1)}, u32[]{:S(2)}) %copy-start.3) | copy-done | bytes 3670040
  14.9 3.2 %collective-permute-start = (f32[32,128]{1,0:T(8,128)S(1)}, f32[32,128]{1,0:T(8,128)S(1)}, u32[]{:S(2)}, u32[]{:S(2)}) collective-permute-start(f32[32,128]{1,0:T(8,128)S(1)} %get-tuple-element.13), channel_id=1, source_target_pairs={{0,32},{32,0},{1,33},{33,1},{2,34},{34,2},{3,35},{35,3},{4,36},{36... | collective-permute-start | bytes 49160 | tf_op jit(solution)/shard_map/ppermute | solution.py:255
  18.1 0.8 collective-permute-done
  18.9 0.6 broadcast_in_dim.8
  19.6 3.3 %all-to-all-start = ((f32[4,32,128]{2,1,0:T(8,128)}), f32[4,32,128]{2,1,0:T(8,128)S(1)}, u32[]{:S(2)}, u32[]{:S(2)}) async-start(f32[4,32,128]{2,1,0:T(8,128)} %broadcast_in_dim.8), calls=%async_computation | async-start | bytes 131072 | tf_op jit(solution)/shard_map/all_to_all | solution.py:251
  22.9 0.1 pad_add_fusion.ids_ref
  22.9 4.4 %all-to-all-done.parts_ref = f32[4,32,128]{2,1,0:T(8,128)S(1)} async-done(((f32[4,32,128]{2,1,0:T(8,128)}), f32[4,32,128]{2,1,0:T(8,128)S(1)}, u32[]{:S(2)}, u32[]{:S(2)}) %all-to-all-start) | async-done | bytes 65568 | tf_op jit(solution)/shard_map/all_to_all | solution.py:251
  27.3 0.0 copy-start.1
  27.3 2.0 %copy-done.1 = bf16[128,14336]{1,0:T(8,128)(2,1)S(1)} copy-done((bf16[128,14336]{1,0:T(8,128)(2,1)S(1)}, bf16[128,14336]{1,0:T(8,128)(2,1)}, u32[]{:S(2)}) %copy-start.1) | copy-done | bytes 3670040
  29.3 0.0 copy-start.4
  29.3 2.0 %copy-done.4 = bf16[128,14336]{1,0:T(8,128)(2,1)S(1)} copy-done((bf16[128,14336]{1,0:T(8,128)(2,1)S(1)}, bf16[128,14336]{1,0:T(8,128)(2,1)}, u32[]{:S(2)}) %copy-start.4) | copy-done | bytes 3670040
  31.4 4.4 %project.1 = (f32[16,2,8,8,128]{4,3,2,1,0:T(8,128)S(1)}, f32[16,2,8,8,128]{4,3,2,1,0:T(8,128)S(1)}) custom-call(s32[3]{0:T(128)S(1)} %pad_add_fusion.ids_ref, f32[4,32,128]{2,1,0:T(8,128)S(1)} %all-to-all-done.parts_ref, bf16[128,14336]{1,0:T(8,128)(2,1)S(1)} %copy-done.1, bf16[128,14336]{1,0:T(8,128)(2,1)S(1)} %copy-done.4), custom_call_target="tpu_custom_call" | custom-call | tf_op jit(solution)/shard_map/project/pallas_call | solution.py:123
  35.8 1.6 %collective-permute-start.1 = (f32[16,2,8,8,128]{4,3,2,1,0:T(8,128)S(1)}, f32[16,2,8,8,128]{4,3,2,1,0:T(8,128)S(1)}, u32[]{:S(2)}, u32[]{:S(2)}) collective-permute-start(f32[16,2,8,8,128]{4,3,2,1,0:T(8,128)S(1)} %get-tuple-element.17), channel_id=1, source_target_pairs={{0,32},{32,0},{1,33},{33,1},{2,34},{34,2},{3,35},{35,3},{4,36},{36... | collective-permute-start | bytes 3145736 | tf_op jit(solution)/shard_map/ppermute | solution.py:255
  37.3 2.3 %collective-permute-done.1 = f32[16,2,8,8,128]{4,3,2,1,0:T(8,128)S(1)} collective-permute-done((f32[16,2,8,8,128]{4,3,2,1,0:T(8,128)S(1)}, f32[16,2,8,8,128]{4,3,2,1,0:T(8,128)S(1)}, u32[]{:S(2)}, u32[]{:S(2)}) %collective-permute-start.1) | collective-permute-done | bytes 1048608 | tf_op jit(solution)/shard_map/ppermute | solution.py:255
  39.6 0.2 add.15
  39.8 22.6 %all_to_all.20 = f32[32,8,8,128]{3,2,1,0:T(8,128)S(1)} all-to-all(f32[32,8,8,128]{3,2,1,0:T(8,128)S(1)} %bitcast.14), channel_id=1, replica_groups=mesh['y'=4,'c'=2,'x'=4,'z4'=2,'z2'=2,'z1'=2] {'y','x','z1'}, dimensions={0} | all-to-all | bytes 2097152 | tf_op jit(solution)/shard_map/all_to_all | solution.py:251
  62.4 0.1 reduce_sum.18
  62.5 14.3 %all_to_all.21 = f32[4,8,8,128]{3,2,1,0:T(8,128)S(1)} all-to-all(f32[4,8,8,128]{3,2,1,0:T(8,128)S(1)} %broadcast_in_dim.9), channel_id=1, replica_groups=mesh['y'=4,'c'=2,'x'=4,'z4'=2,'z2'=2,'z1'=2] {'z4','z2'}, dimensions={0} | all-to-all | bytes 262144 | tf_op jit(solution)/shard_map/all_to_all | solution.py:251
  76.8 0.1 broadcast_in_dim.10
  76.9 17.2 %all_to_all.22 = f32[32,7,8,128]{3,2,1,0:T(8,128)S(1)} all-to-all(f32[32,7,8,128]{3,2,1,0:T(8,128)S(1)} %broadcast_in_dim.10), channel_id=1, replica_groups=mesh['y'=4,'c'=2,'x'=4,'z4'=2,'z2'=2,'z1'=2] {'y','x','z1'}, dimensions={0} | all-to-all | bytes 1835008 | tf_op jit(solution)/shard_map/all_to_all | solution.py:251
  94.1 4.0 %collective-permute-start.2 = (f32[16,2,7,8,128]{4,3,2,1,0:T(8,128)S(1)}, f32[16,2,7,8,128]{4,3,2,1,0:T(8,128)S(1)}, u32[]{:S(2)}, u32[]{:S(2)}) collective-permute-start(f32[16,2,7,8,128]{4,3,2,1,0:T(8,128)S(1)} %bitcast.10), channel_id=1, source_target_pairs={{0,32},{32,0},{1,33},{33,1},{2,34},{34,2},{3,35},{35,3},{4,36},{36... | collective-permute-start | bytes 2752520 | tf_op jit(solution)/shard_map/ppermute | solution.py:255
  98.1 5.1 %factor.1 = (f32[32,128]{1,0:T(8,128)}, f32[32,128]{1,0:T(8,128)S(1)}, bf16[128,256]{1,0:T(8,128)(2,1)S(1)}) custom-call(s32[3]{0:T(128)S(1)} %pad_add_fusion.ids_ref, f32[8,128]{1,0:T(8,128)S(1)} %slice_bitcast_fusion.gram_ref, f32[4,32,128]{2,1,0:T(8,128)S(1)} %all-to-all-done.parts_ref), custom_call_target="tpu_custom_call" | custom-call | flops 1000000 | bytes 1000000 | tf_op jit(solution)/shard_map/factor/pallas_call | solution.py:175
  103.2 0.0 collective-permute-done.2.other_ref
  103.2 0.0 copy-start.2
  103.2 2.0 %copy-done.2 = bf16[128,14336]{1,0:T(8,128)(2,1)S(1)} copy-done((bf16[128,14336]{1,0:T(8,128)(2,1)S(1)}, bf16[128,14336]{1,0:T(8,128)(2,1)}, u32[]{:S(2)}) %copy-start.2) | copy-done | bytes 3670040
  105.2 0.0 copy-start.5
  105.2 2.0 %copy-done.5 = bf16[128,14336]{1,0:T(8,128)(2,1)S(1)} copy-done((bf16[128,14336]{1,0:T(8,128)(2,1)S(1)}, bf16[128,14336]{1,0:T(8,128)(2,1)}, u32[]{:S(2)}) %copy-start.5) | copy-done | bytes 3670040
  107.2 5.7 %finish.1 = (f32[32,448]{1,0:T(8,128)}, bf16[128,14336]{1,0:T(8,128)(2,1)}) custom-call(s32[3]{0:T(128)S(1)} %pad_add_fusion.ids_ref, f32[16,2,7,8,128]{4,3,2,1,0:T(8,128)S(1)} %bitcast.11, f32[16,2,7,8,128]{4,3,2,1,0:T(8,128)S(1)} %collective-permute-done.2.other_ref, f32[32,128]{1,0:T(8,128)S(1)} %get-tuple-element.19.inverse_ref, ...), custom_call_target="tpu_custom_call" | custom-call | tf_op jit(solution)/shard_map/finish/pallas_call | solution.py:236
  (5 shorter events, 0.0 us)
Async XLA Ops:
  0.6 2.0 %copy-start.6 = (bf16[1,128,14336]{2,1,0:T(8,128)(2,1)S(1)}, bf16[1,128,14336]{2,1,0:T(8,128)(2,1)}, u32[]{:S(2)}) copy-start(bf16[1,128,14336]{2,1,0:T(8,128)(2,1)} %param.3) | copy-start | bytes 11010052
  2.7 2.0 %copy-start.7 = (bf16[1,128,14336]{2,1,0:T(8,128)(2,1)S(1)}, bf16[1,128,14336]{2,1,0:T(8,128)(2,1)}, u32[]{:S(2)}) copy-start(bf16[1,128,14336]{2,1,0:T(8,128)(2,1)} %param.4) | copy-start | bytes 11010052
  4.7 1.2 %copy-start.8 = (bf16[32,14336]{1,0:T(8,128)(2,1)S(1)}, bf16[32,14336]{1,0:T(8,128)(2,1)}, u32[]{:S(2)}) copy-start(bf16[32,14336]{1,0:T(8,128)(2,1)} %sketch_hbm.1) | copy-start | bytes 2752516
  11.2 1.8 %copy-start = (bf16[128,14336]{1,0:T(8,128)(2,1)}, bf16[128,14336]{1,0:T(8,128)(2,1)S(1)}, u32[]{:S(2)}) copy-start(bf16[128,14336]{1,0:T(8,128)(2,1)S(1)} %get-tuple-element.14.grad_ref) | copy-start | bytes 11010052
  13.1 1.8 %copy-start.3 = (bf16[128,14336]{1,0:T(8,128)(2,1)}, bf16[128,14336]{1,0:T(8,128)(2,1)S(1)}, u32[]{:S(2)}) copy-start(bf16[128,14336]{1,0:T(8,128)(2,1)S(1)} %get-tuple-element.15.memory_ref) | copy-start | bytes 11010052
  14.9 4.1 %collective-permute-start = (f32[32,128]{1,0:T(8,128)S(1)}, f32[32,128]{1,0:T(8,128)S(1)}, u32[]{:S(2)}, u32[]{:S(2)}) collective-permute-start(f32[32,128]{1,0:T(8,128)S(1)} %get-tuple-element.13), channel_id=1, source_target_pairs={{0,32},{32,0},{1,33},{33,1},{2,34},{34,2},{3,35},{35,3},{4,36},{36... | collective-permute-start | bytes 49160 | tf_op jit(solution)/shard_map/ppermute | solution.py:255
  19.6 7.7 %all-to-all-start = ((f32[4,32,128]{2,1,0:T(8,128)}), f32[4,32,128]{2,1,0:T(8,128)S(1)}, u32[]{:S(2)}, u32[]{:S(2)}) async-start(f32[4,32,128]{2,1,0:T(8,128)} %broadcast_in_dim.8), calls=%async_computation | async-start | bytes 131072 | tf_op jit(solution)/shard_map/all_to_all | solution.py:251
  27.3 2.0 %copy-start.1 = (bf16[128,14336]{1,0:T(8,128)(2,1)S(1)}, bf16[128,14336]{1,0:T(8,128)(2,1)}, u32[]{:S(2)}) copy-start(bf16[128,14336]{1,0:T(8,128)(2,1)} %copy-done) | copy-start | bytes 11010052
  29.3 2.0 %copy-start.4 = (bf16[128,14336]{1,0:T(8,128)(2,1)S(1)}, bf16[128,14336]{1,0:T(8,128)(2,1)}, u32[]{:S(2)}) copy-start(bf16[128,14336]{1,0:T(8,128)(2,1)} %copy-done.3) | copy-start | bytes 11010052
  35.8 3.9 %collective-permute-start.1 = (f32[16,2,8,8,128]{4,3,2,1,0:T(8,128)S(1)}, f32[16,2,8,8,128]{4,3,2,1,0:T(8,128)S(1)}, u32[]{:S(2)}, u32[]{:S(2)}) collective-permute-start(f32[16,2,8,8,128]{4,3,2,1,0:T(8,128)S(1)} %get-tuple-element.17), channel_id=1, source_target_pairs={{0,32},{32,0},{1,33},{33,1},{2,34},{34,2},{3,35},{35,3},{4,36},{36... | collective-permute-start | bytes 3145736 | tf_op jit(solution)/shard_map/ppermute | solution.py:255
  94.1 9.1 %collective-permute-start.2 = (f32[16,2,7,8,128]{4,3,2,1,0:T(8,128)S(1)}, f32[16,2,7,8,128]{4,3,2,1,0:T(8,128)S(1)}, u32[]{:S(2)}, u32[]{:S(2)}) collective-permute-start(f32[16,2,7,8,128]{4,3,2,1,0:T(8,128)S(1)} %bitcast.10), channel_id=1, source_target_pairs={{0,32},{32,0},{1,33},{33,1},{2,34},{34,2},{3,35},{35,3},{4,36},{36... | collective-permute-start | bytes 2752520 | tf_op jit(solution)/shard_map/ppermute | solution.py:255
  103.2 2.0 %copy-start.2 = (bf16[128,14336]{1,0:T(8,128)(2,1)S(1)}, bf16[128,14336]{1,0:T(8,128)(2,1)}, u32[]{:S(2)}) copy-start(bf16[128,14336]{1,0:T(8,128)(2,1)} %copy-done) | copy-start | bytes 11010052
  105.2 2.0 %copy-start.5 = (bf16[128,14336]{1,0:T(8,128)(2,1)S(1)}, bf16[128,14336]{1,0:T(8,128)(2,1)}, u32[]{:S(2)}) copy-start(bf16[128,14336]{1,0:T(8,128)(2,1)} %copy-done.3) | copy-start | bytes 11010052

commit v2 on v1

--- a/solution.py
+++ b/solution.py
@@ -24,6 +24,7 @@
 ANY = pl.BlockSpec(memory_space=pl.ANY)
 VMEM = pl.BlockSpec(memory_space=pltpu.VMEM)
 SMEM = pl.BlockSpec(memory_space=pltpu.SMEM)
+BLOCKS = [pltpu.VMEM((ROWS, FF), BF16), pltpu.VMEM((ROWS, FF), BF16), pltpu.SemaphoreType.DMA((CHUNKS, 2))]
 
 
 def params(limit):
@@ -35,6 +36,17 @@
     rest = value - first
     second = rest.astype(BF16).astype(F32)
     return first, second, rest - second
+
+
+def loads(grad_hbm, memory_hbm, grad_ref, memory_ref, sems):
+    def copies(chunk):
+        cols = pl.ds(pl.multiple_of(chunk * WIDTH, 128), WIDTH)
+        return (
+            pltpu.make_async_copy(grad_hbm.at[:, cols], grad_ref.at[:, cols], sems.at[chunk, 0]),
+            pltpu.make_async_copy(memory_hbm.at[:, cols], memory_ref.at[:, cols], sems.at[chunk, 1]),
+        )
+
+    return copies
 
 
 def sketch_kernel(grad_hbm, memory_hbm, sketch_hbm, out_ref, grad_ref, memory_ref, sketch_ref, sems):
@@ -66,20 +78,25 @@
 def left_sketch(grad, memory, sketch):
     return pl.pallas_call(
         sketch_kernel,
-        out_shape=(
-            jax.ShapeDtypeStruct((RANK, ROWS), F32),
+        out_shape=jax.ShapeDtypeStruct((RANK, ROWS), F32),
+        in_specs=[ANY, ANY, ANY],
+        out_specs=VMEM,
+        scratch_shapes=[
             pltpu.VMEM((ROWS, FF), BF16),
             pltpu.VMEM((ROWS, FF), BF16),
-        ),
-        in_specs=[ANY, ANY, ANY],
-        out_specs=(VMEM, VMEM, VMEM),
-        scratch_shapes=[pltpu.VMEM((RANK, FF), BF16), pltpu.SemaphoreType.DMA((LOADS, 3))],
-        compiler_params=params(16 * MB),
+            pltpu.VMEM((RANK, FF), BF16),
+            pltpu.SemaphoreType.DMA((LOADS, 3)),
+        ],
+        compiler_params=params(24 * MB),
         name="left_sketch",
     )(grad, memory, sketch)
 
 
-def project_kernel(ids_ref, parts_ref, grad_ref, memory_ref, own_ref, other_ref):
+def project_kernel(ids_ref, parts_ref, grad_hbm, memory_hbm, own_ref, other_ref, grad_ref, memory_ref, sems):
+    copies = loads(grad_hbm, memory_hbm, grad_ref, memory_ref, sems)
+    for chunk in range(CHUNKS):
+        for copy in copies(chunk):
+            copy.start()
     core = ids_ref[0]
     summed = ((parts_ref[0] + parts_ref[1]) + (parts_ref[2] + parts_ref[3])) * (1.0 / 8)
     tiled = jnp.concatenate([summed] * 4, axis=0)
@@ -106,6 +123,8 @@
 
     @pl.loop(0, CHUNKS)
     def _(chunk):
+        for copy in copies(chunk):
+            copy.wait()
         cols = pl.ds(pl.multiple_of(chunk * WIDTH, 128), WIDTH)
         both = jnp.concatenate([grad_ref[:, cols], memory_ref[:, cols]], axis=0)
         product = jnp.dot(left, both, preferred_element_type=F32)
@@ -123,14 +142,21 @@
     return pl.pallas_call(
         project_kernel,
         out_shape=(shape, shape),
-        in_specs=[SMEM, VMEM, VMEM, VMEM],
+        in_specs=[SMEM, VMEM, ANY, ANY],
         out_specs=(VMEM, VMEM),
+        scratch_shapes=BLOCKS,
         compiler_params=params(24 * MB),
         name="project",
     )(ids, parts, grad, memory)
 
 
-def factor_kernel(ids_ref, gram_ref, parts_ref, left_ref, inverse_ref, back_ref):
+def factor_kernel(
+    ids_ref, gram_ref, parts_ref, grad_hbm, memory_hbm, left_ref, inverse_ref, back_ref, grad_ref, memory_ref, sems
+):
+    copies = loads(grad_hbm, memory_hbm, grad_ref, memory_ref, sems)
+    for chunk in range(CHUNKS):
+        for copy in copies(chunk):
+            copy.start()
     core = ids_ref[0]
     rows = lax.broadcasted_iota(jnp.int32, (RANK, 128), 0)
     lanes = lax.broadcasted_iota(jnp.int32, (RANK, 128), 1)
@@ -169,22 +195,28 @@
     one, two, three = three_parts(ordered)
     stack = jnp.concatenate([one, two, three, one, two, one, jnp.zeros((64, 128), F32)], axis=0)
     back_ref[...] = stack.T.astype(BF16)
-
-
-def factor(ids, gram, parts):
+    for chunk in range(CHUNKS):
+        for copy in copies(chunk):
+            copy.wait()
+
+
+def factor(ids, gram, parts, grad, memory):
     return pl.pallas_call(
         factor_kernel,
         out_shape=(
             jax.ShapeDtypeStruct((RANK, ROWS), F32),
             jax.ShapeDtypeStruct((RANK, 128), F32),
             jax.ShapeDtypeStruct((ROWS, 256), BF16),
+            pltpu.VMEM((ROWS, FF), BF16),
+            pltpu.VMEM((ROWS, FF), BF16),
         ),
-        in_specs=[SMEM, VMEM, VMEM],
-        out_specs=(VMEM, VMEM, VMEM),
+        in_specs=[SMEM, VMEM, VMEM, ANY, ANY],
+        out_specs=(VMEM,) * 5,
+        scratch_shapes=[pltpu.SemaphoreType.DMA((CHUNKS, 2))],
         compiler_params=params(8 * MB),
         cost_estimate=pl.CostEstimate(flops=10**6, bytes_accessed=10**6, transcendentals=0),
         name="factor",
-    )(ids, gram, parts)
+    )(ids, gram, parts, grad, memory)
 
 
 def update_kernel(ids_ref, own_ref, other_ref, inverse_ref, back_ref, grad_ref, memory_ref, share_ref, out_hbm, out_ref, sems):
@@ -263,22 +295,27 @@
     return pltpu.with_memory_space_constraint(value, pltpu.VMEM)
 
 
+def far(value):
+    return pltpu.with_memory_space_constraint(value, pltpu.HBM)
+
+
 def on_device(gradients, residual, sketch):
     core = lax.axis_index("c")
     block = lax.axis_index(("x", "z4", "z2"))
     ids = jnp.stack([core, block, lax.axis_index("z1")]).astype(jnp.int32)
-    partial, grad, memory = left_sketch(gradients[0], residual[0], sketch)
+    grad, memory = far(gradients[0]), far(residual[0])
+    partial = left_sketch(grad, memory, far(sketch))
     pair = partial + swap(partial)
     parts = spread(pair, "y", 4)
-    own, other = project(ids, parts, resident(grad), resident(memory))
+    own, other = project(ids, parts, grad, memory)
     terms = own + swap(other)
     terms = exchange(terms.reshape(32, TILES + 1, 8, 128), SPREAD)
     terms = jnp.sum(terms, axis=0)
     terms = jnp.sum(spread(terms, ("z4", "z2"), 4).reshape((4,) + terms.shape), axis=0)
     gathered = spread(terms[:TILES], SPREAD, 32).reshape(CHUNKS, 2, TILES, 8, 128)
     gathered_other = swap(gathered)
-    left, inverse, back = factor(ids, terms[TILES], parts)
-    share, fresh = finish(ids, gathered, gathered_other, inverse, back, resident(grad), resident(memory))
+    left, inverse, back, near_grad, near_memory = factor(ids, terms[TILES], parts, grad, memory)
+    share, fresh = finish(ids, gathered, gathered_other, inverse, back, resident(near_grad), resident(near_memory))
     return left, share, fresh[None]
 
 

time: 113 us -> 101 us (0.89)
  local copies, waits for them, and re-layouts: 17.7 us -> 0.71 us
  Pallas kernels: 20.5 us -> 25.2 us
    unnamed x18 -> x0, local copies, waits for them, and re-layouts: 17 us -> none
    pallas_call x1, Pallas kernels: 5.11 us -> 8.51 us  [factor(): pl.pallas_call(factor_kernel, out_shape=(jax.ShapeDtypeStruct((RANK, ROWS...]
    pallas_call x1, Pallas kernels: 4.36 us -> 5.51 us  [project(): pl.pallas_call(project_kernel, out_shape=(shape, shape), in_specs=[SMEM,...]
  transfers between devices with their start and end apart: 4 -> 4, of which waited for: 3 -> 3; matrix products, arithmetic and copies ran while one was open for 0% -> 0% of each run, Pallas kernels for 5% -> 8%
where the time goes in v2:
time: 101 us
  blocking collectives  54.1 us (54%)
  Pallas kernels  25.2 us (25%)
  starting transfers between devices  12.2 us (12%)
  waiting for transfers between devices  7.49 us (7%)
    all_to_all x3, blocking collectives, exchange(): return lax.all_to_all(value, axes, 0, 0, tiled=True)  54.1 us
    ppermute x3, starting transfers between devices, swap(): return lax.ppermute(value, 'c', [(0, 1), (1, 0)])  8.87 us
    pallas_call x1, Pallas kernels, factor(): pl.pallas_call(factor_kernel, out_shape=(jax.ShapeDtypeStruct((RANK, ROWS...  8.51 us
    pallas_call x1, Pallas kernels, finish(): pl.pallas_call(update_kernel, out_shape=(jax.ShapeDtypeStruct((RANK, WIDT...  5.67 us
    pallas_call x1, Pallas kernels, left_sketch(): pl.pallas_call(sketch_kernel, out_shape=jax.ShapeDtypeStruct((RANK, ROWS)...  5.52 us
    pallas_call x1, Pallas kernels, project(): pl.pallas_call(project_kernel, out_shape=(shape, shape), in_specs=[SMEM,...  5.51 us
    all_to_all x1, waiting for transfers between devices, exchange(): return lax.all_to_all(value, axes, 0, 0, tiled=True)  4.36 us
    all_to_all x1, starting transfers between devices, exchange(): return lax.all_to_all(value, axes, 0, 0, tiled=True)  3.28 us
  transfers between devices with their start and end apart: 4, of which 3 were waited for; matrix products, arithmetic and copies ran while one was open for 0% of the time, Pallas kernels for 8%

profile of v2, /device:TPU:1, one launch (start us, length us, event | category | flops | bytes accessed | tf_op | source)
XLA Modules:
  0.0 100.7 jit_solution(17525856713348120050)
XLA Ops:
  0.6 5.5 %left_sketch.1 = f32[32,128]{1,0:T(8,128)S(1)} custom-call(bf16[128,14336]{1,0:T(8,128)(2,1)} %bitcast.12, bf16[128,14336]{1,0:T(8,128)(2,1)} %bitcast.15, bf16[32,14336]{1,0:T(8,128)(2,1)} %sketch_hbm.1), custom_call_target="tpu_custom_call" | custom-call | tf_op jit(solution)/shard_map/left_sketch/pallas_call | solution.py:79
  6.2 3.3 %collective-permute-start = (f32[32,128]{1,0:T(8,128)S(1)}, f32[32,128]{1,0:T(8,128)S(1)}, u32[]{:S(2)}, u32[]{:S(2)}) collective-permute-start(f32[32,128]{1,0:T(8,128)S(1)} %left_sketch.1), channel_id=1, source_target_pairs={{0,32},{32,0},{1,33},{33,1},{2,34},{34,2},{3,35},{35,3},{4,36},{36... | collective-permute-start | bytes 49160 | tf_op jit(solution)/shard_map/ppermute | solution.py:287
  9.5 0.8 collective-permute-done
  10.3 0.6 broadcast_in_dim.8
  11.0 3.3 %all-to-all-start = ((f32[4,32,128]{2,1,0:T(8,128)}), f32[4,32,128]{2,1,0:T(8,128)S(1)}, u32[]{:S(2)}, u32[]{:S(2)}) async-start(f32[4,32,128]{2,1,0:T(8,128)} %broadcast_in_dim.8), calls=%async_computation | async-start | bytes 131072 | tf_op jit(solution)/shard_map/all_to_all | solution.py:283
  14.3 0.1 pad_add_fusion.ids_ref
  14.3 4.4 %all-to-all-done.parts_ref = f32[4,32,128]{2,1,0:T(8,128)S(1)} async-done(((f32[4,32,128]{2,1,0:T(8,128)}), f32[4,32,128]{2,1,0:T(8,128)S(1)}, u32[]{:S(2)}, u32[]{:S(2)}) %all-to-all-start) | async-done | bytes 65568 | tf_op jit(solution)/shard_map/all_to_all | solution.py:283
  18.7 5.5 %project.1 = (f32[16,2,8,8,128]{4,3,2,1,0:T(8,128)S(1)}, f32[16,2,8,8,128]{4,3,2,1,0:T(8,128)S(1)}) custom-call(s32[3]{0:T(128)S(1)} %pad_add_fusion.ids_ref, f32[4,32,128]{2,1,0:T(8,128)S(1)} %all-to-all-done.parts_ref, bf16[128,14336]{1,0:T(8,128)(2,1)} %bitcast.13, bf16[128,14336]{1,0:T(8,128)(2,1)} %bitcast.16), custom_call_target="tpu_custom_call" | custom-call | tf_op jit(solution)/shard_map/project/pallas_call | solution.py:142
  24.2 1.6 %collective-permute-start.1 = (f32[16,2,8,8,128]{4,3,2,1,0:T(8,128)S(1)}, f32[16,2,8,8,128]{4,3,2,1,0:T(8,128)S(1)}, u32[]{:S(2)}, u32[]{:S(2)}) collective-permute-start(f32[16,2,8,8,128]{4,3,2,1,0:T(8,128)S(1)} %get-tuple-element.13), channel_id=1, source_target_pairs={{0,32},{32,0},{1,33},{33,1},{2,34},{34,2},{3,35},{35,3},{4,36},{36... | collective-permute-start | bytes 3145736 | tf_op jit(solution)/shard_map/ppermute | solution.py:287
  25.8 2.3 %collective-permute-done.1 = f32[16,2,8,8,128]{4,3,2,1,0:T(8,128)S(1)} collective-permute-done((f32[16,2,8,8,128]{4,3,2,1,0:T(8,128)S(1)}, f32[16,2,8,8,128]{4,3,2,1,0:T(8,128)S(1)}, u32[]{:S(2)}, u32[]{:S(2)}) %collective-permute-start.1) | collective-permute-done | bytes 1048608 | tf_op jit(solution)/shard_map/ppermute | solution.py:287
  28.1 0.2 add.15
  28.3 22.6 %all_to_all.20 = f32[32,8,8,128]{3,2,1,0:T(8,128)S(1)} all-to-all(f32[32,8,8,128]{3,2,1,0:T(8,128)S(1)} %bitcast.18), channel_id=1, replica_groups=mesh['y'=4,'c'=2,'x'=4,'z4'=2,'z2'=2,'z1'=2] {'y','x','z1'}, dimensions={0} | all-to-all | bytes 2097152 | tf_op jit(solution)/shard_map/all_to_all | solution.py:283
  50.9 0.1 reduce_sum.18
  50.9 14.3 %all_to_all.21 = f32[4,8,8,128]{3,2,1,0:T(8,128)S(1)} all-to-all(f32[4,8,8,128]{3,2,1,0:T(8,128)S(1)} %broadcast_in_dim.9), channel_id=1, replica_groups=mesh['y'=4,'c'=2,'x'=4,'z4'=2,'z2'=2,'z1'=2] {'z4','z2'}, dimensions={0} | all-to-all | bytes 262144 | tf_op jit(solution)/shard_map/all_to_all | solution.py:283
  65.3 0.1 broadcast_in_dim.10
  65.4 17.2 %all_to_all.22 = f32[32,7,8,128]{3,2,1,0:T(8,128)S(1)} all-to-all(f32[32,7,8,128]{3,2,1,0:T(8,128)S(1)} %broadcast_in_dim.10), channel_id=1, replica_groups=mesh['y'=4,'c'=2,'x'=4,'z4'=2,'z2'=2,'z1'=2] {'y','x','z1'}, dimensions={0} | all-to-all | bytes 1835008 | tf_op jit(solution)/shard_map/all_to_all | solution.py:283
  82.5 4.0 %collective-permute-start.2 = (f32[16,2,7,8,128]{4,3,2,1,0:T(8,128)S(1)}, f32[16,2,7,8,128]{4,3,2,1,0:T(8,128)S(1)}, u32[]{:S(2)}, u32[]{:S(2)}) collective-permute-start(f32[16,2,7,8,128]{4,3,2,1,0:T(8,128)S(1)} %bitcast.10), channel_id=1, source_target_pairs={{0,32},{32,0},{1,33},{33,1},{2,34},{34,2},{3,35},{35,3},{4,36},{36... | collective-permute-start | bytes 2752520 | tf_op jit(solution)/shard_map/ppermute | solution.py:287
  86.5 8.5 %factor.1 = (f32[32,128]{1,0:T(8,128)}, f32[32,128]{1,0:T(8,128)S(1)}, bf16[128,256]{1,0:T(8,128)(2,1)S(1)}, bf16[128,14336]{1,0:T(8,128)(2,1)S(1)}, bf16[128,14336]{1,0:T(8,128)(2,1)S(1)}) custom-call(s32[3]{0:T(128)S(1)} %pad_add_fusion.ids_ref, f32[8,128]{1,0:T(8,128)S(1)} %slice_bitcast_fusion.gram_ref, f32[4,32,128]{2,1,0:T(8,128)S(1)} %all-to-all-done.parts_ref, ...), custom_call_target="tpu_custom_call" | custom-call | flops 1000000 | bytes 1000000 | tf_op jit(solution)/shard_map/factor/pallas_call | solution.py:204
  95.0 0.0 collective-permute-done.2.other_ref
  95.0 5.7 %finish.1 = (f32[32,448]{1,0:T(8,128)}, bf16[128,14336]{1,0:T(8,128)(2,1)}) custom-call(s32[3]{0:T(128)S(1)} %pad_add_fusion.ids_ref, f32[16,2,7,8,128]{4,3,2,1,0:T(8,128)S(1)} %bitcast.11, f32[16,2,7,8,128]{4,3,2,1,0:T(8,128)S(1)} %collective-permute-done.2.other_ref, f32[32,128]{1,0:T(8,128)S(1)} %get-tuple-element.15.inverse_ref, ...), custom_call_target="tpu_custom_call" | custom-call | tf_op jit(solution)/shard_map/finish/pallas_call | solution.py:268
  (5 shorter events, 0.0 us)
Async XLA Ops:
  6.2 4.2 %collective-permute-start = (f32[32,128]{1,0:T(8,128)S(1)}, f32[32,128]{1,0:T(8,128)S(1)}, u32[]{:S(2)}, u32[]{:S(2)}) collective-permute-start(f32[32,128]{1,0:T(8,128)S(1)} %left_sketch.1), channel_id=1, source_target_pairs={{0,32},{32,0},{1,33},{33,1},{2,34},{34,2},{3,35},{35,3},{4,36},{36... | collective-permute-start | bytes 49160 | tf_op jit(solution)/shard_map/ppermute | solution.py:287
  11.0 7.7 %all-to-all-start = ((f32[4,32,128]{2,1,0:T(8,128)}), f32[4,32,128]{2,1,0:T(8,128)S(1)}, u32[]{:S(2)}, u32[]{:S(2)}) async-start(f32[4,32,128]{2,1,0:T(8,128)} %broadcast_in_dim.8), calls=%async_computation | async-start | bytes 131072 | tf_op jit(solution)/shard_map/all_to_all | solution.py:283
  24.2 3.9 %collective-permute-start.1 = (f32[16,2,8,8,128]{4,3,2,1,0:T(8,128)S(1)}, f32[16,2,8,8,128]{4,3,2,1,0:T(8,128)S(1)}, u32[]{:S(2)}, u32[]{:S(2)}) collective-permute-start(f32[16,2,8,8,128]{4,3,2,1,0:T(8,128)S(1)} %get-tuple-element.13), channel_id=1, source_target_pairs={{0,32},{32,0},{1,33},{33,1},{2,34},{34,2},{3,35},{35,3},{4,36},{36... | collective-permute-start | bytes 3145736 | tf_op jit(solution)/shard_map/ppermute | solution.py:287
  82.5 12.5 %collective-permute-start.2 = (f32[16,2,7,8,128]{4,3,2,1,0:T(8,128)S(1)}, f32[16,2,7,8,128]{4,3,2,1,0:T(8,128)S(1)}, u32[]{:S(2)}, u32[]{:S(2)}) collective-permute-start(f32[16,2,7,8,128]{4,3,2,1,0:T(8,128)S(1)} %bitcast.10), channel_id=1, source_target_pairs={{0,32},{32,0},{1,33},{33,1},{2,34},{34,2},{3,35},{35,3},{4,36},{36... | collective-permute-start | bytes 2752520 | tf_op jit(solution)/shard_map/ppermute | solution.py:287

commit v3 on v1

--- a/solution.py
+++ b/solution.py
@@ -17,6 +17,9 @@
 TILES = WIDTH // 128
 LOADS = 8
 LOAD_WIDTH = FF // LOADS
+GROUP = 4
+STEPS = CHUNKS // GROUP
+STEP_WIDTH = GROUP * WIDTH
 F32 = jnp.float32
 BF16 = jnp.bfloat16
 MB = 1024 * 1024
@@ -79,9 +82,15 @@
     )(grad, memory, sketch)
 
 
-def project_kernel(ids_ref, parts_ref, grad_ref, memory_ref, own_ref, other_ref):
+def mean_of(part_refs):
+    one, two, three, four = (ref[...] for ref in part_refs)
+    return ((one + two) + (three + four)) * (1.0 / 8)
+
+
+def project_kernel(ids_ref, *refs):
+    part_refs, (grad_ref, memory_ref, own_ref, other_ref) = refs[:4], refs[4:]
     core = ids_ref[0]
-    summed = ((parts_ref[0] + parts_ref[1]) + (parts_ref[2] + parts_ref[3])) * (1.0 / 8)
+    summed = mean_of(part_refs)
     tiled = jnp.concatenate([summed] * 4, axis=0)
     square = lax.dot_general(
         summed, tiled, (((1,), (1,)), ((), ())), precision=lax.Precision.HIGHEST, preferred_element_type=F32
@@ -104,18 +113,21 @@
     left = jnp.concatenate(three_parts(ordered), axis=0).astype(BF16)
     left = jnp.concatenate([left, left], axis=1)
 
-    @pl.loop(0, CHUNKS)
-    def _(chunk):
-        cols = pl.ds(pl.multiple_of(chunk * WIDTH, 128), WIDTH)
+    @pl.loop(0, STEPS, unroll=2)
+    def _(step):
+        cols = pl.ds(pl.multiple_of(step * STEP_WIDTH, 128), STEP_WIDTH)
         both = jnp.concatenate([grad_ref[:, cols], memory_ref[:, cols]], axis=0)
         product = jnp.dot(left, both, preferred_element_type=F32)
         product = product[:32] + (product[32:64] + product[64:])
-        for half, ref in enumerate((own_ref, other_ref)):
-            for row in range(2):
-                base = 16 * half + 8 * row
-                for tile in range(TILES):
-                    ref[chunk, row, tile] = product[base : base + 8, 128 * tile : 128 * tile + 128]
-                ref[chunk, row, TILES] = gram
+        for member in range(GROUP):
+            chunk = step * GROUP + member
+            for half, ref in enumerate((own_ref, other_ref)):
+                for row in range(2):
+                    base = 16 * half + 8 * row
+                    for tile in range(TILES):
+                        left_edge = WIDTH * member + 128 * tile
+                        ref[chunk, row, tile] = product[base : base + 8, left_edge : left_edge + 128]
+                    ref[chunk, row, TILES] = gram
 
 
 def project(ids, parts, grad, memory):
@@ -123,21 +135,22 @@
     return pl.pallas_call(
         project_kernel,
         out_shape=(shape, shape),
-        in_specs=[SMEM, VMEM, VMEM, VMEM],
+        in_specs=[SMEM] + [VMEM] * 6,
         out_specs=(VMEM, VMEM),
-        compiler_params=params(24 * MB),
+        compiler_params=params(16 * MB),
         name="project",
-    )(ids, parts, grad, memory)
-
-
-def factor_kernel(ids_ref, gram_ref, parts_ref, left_ref, inverse_ref, back_ref):
+    )(ids, *parts, grad, memory)
+
+
+def factor_kernel(ids_ref, gram_ref, *refs):
+    part_refs, (left_ref, inverse_ref, back_ref) = refs[:4], refs[4:]
     core = ids_ref[0]
     rows = lax.broadcasted_iota(jnp.int32, (RANK, 128), 0)
     lanes = lax.broadcasted_iota(jnp.int32, (RANK, 128), 1)
     tile = gram_ref[...] * (1.0 / 8)
     packed = jnp.concatenate([tile] + [pltpu.roll(tile, 128 - 32 * q, 1) for q in (1, 2, 3)], axis=0)
     work = jnp.where(lanes < 32, packed, jnp.where(lanes == rows + 32, 1.0, 0.0))
-    basis = ((parts_ref[0] + parts_ref[1]) + (parts_ref[2] + parts_ref[3])) * (1.0 / 8)
+    basis = mean_of(part_refs)
     scale = jnp.ones((RANK, 128), F32)
     for step in range(RANK):
         column = jnp.broadcast_to(work[:, step : step + 1], (RANK, 128))
@@ -179,15 +192,25 @@
             jax.ShapeDtypeStruct((RANK, 128), F32),
             jax.ShapeDtypeStruct((ROWS, 256), BF16),
         ),
-        in_specs=[SMEM, VMEM, VMEM],
+        in_specs=[SMEM] + [VMEM] * 5,
         out_specs=(VMEM, VMEM, VMEM),
-        compiler_params=params(8 * MB),
-        cost_estimate=pl.CostEstimate(flops=10**6, bytes_accessed=10**6, transcendentals=0),
+        compiler_params=params(16 * MB),
+        cost_estimate=pl.CostEstimate(flops=10**9, bytes_accessed=10**7, transcendentals=0),
         name="factor",
-    )(ids, gram, parts)
-
-
-def update_kernel(ids_ref, own_ref, other_ref, inverse_ref, back_ref, grad_ref, memory_ref, share_ref, out_hbm, out_ref, sems):
+    )(ids, gram, *parts)
+
+
+def update_kernel(
+    ids_ref, own_ref, other_ref, inverse_ref, back_ref, grad_ref, memory_ref,
+    share_ref, out_hbm, out_ref, store_sems,
+):
+    def columns(step):
+        return pl.ds(step * STEP_WIDTH, STEP_WIDTH)
+
+    def store(step):
+        cols = columns(step)
+        return pltpu.make_async_copy(out_ref.at[:, cols], out_hbm.at[:, cols], store_sems.at[step])
+
     even = ids_ref[0] == 0
     back = back_ref[:, :192]
 
@@ -195,16 +218,16 @@
         parts = [ref[chunk, row, tile] for ref in (own_ref, other_ref) for row in range(2)]
         return jnp.concatenate(parts, axis=0)
 
-    @pl.loop(0, CHUNKS)
-    def _(chunk):
-        cols = pl.ds(pl.multiple_of(chunk * WIDTH, 128), WIDTH)
-        right = jnp.concatenate([block(chunk, tile) for tile in range(TILES)], axis=1)
+    for step in range(STEPS):
+        tiles = [block(step * GROUP + member, tile) for member in range(GROUP) for tile in range(TILES)]
+        right = jnp.concatenate(tiles, axis=1)
         one, two, three = (part.astype(BF16) for part in three_parts(right))
         stack = jnp.concatenate([one, one, one, two, two, three], axis=0)
         update = jnp.dot(back, stack, preferred_element_type=F32)
+        cols = columns(step)
         merged = grad_ref[:, cols].astype(F32) + memory_ref[:, cols].astype(F32)
         out_ref[:, cols] = (merged - update).astype(BF16)
-        pltpu.make_async_copy(out_ref.at[:, cols], out_hbm.at[:, cols], sems.at[chunk]).start()
+        store(step).start()
 
     mine, odd = ids_ref[1], ids_ref[2]
 
@@ -227,9 +250,8 @@
     half = WIDTH // 2
     share_ref[...] = jnp.where(odd == 0, share[:, :half], share[:, half:])
 
-    for chunk in range(CHUNKS):
-        cols = pl.ds(chunk * WIDTH, WIDTH)
-        pltpu.make_async_copy(out_ref.at[:, cols], out_hbm.at[:, cols], sems.at[chunk]).wait()
+    for step in range(STEPS):
+        store(step).wait()
 
 
 def finish(ids, own, other, inverse, back, grad, memory):
@@ -241,12 +263,36 @@
         ),
         in_specs=[SMEM] + [VMEM] * 6,
         out_specs=(VMEM, ANY),
-        scratch_shapes=[pltpu.VMEM((ROWS, FF), BF16), pltpu.SemaphoreType.DMA((CHUNKS,))],
-        compiler_params=params(24 * MB),
+        scratch_shapes=[pltpu.VMEM((ROWS, FF), BF16), pltpu.SemaphoreType.DMA((STEPS,))],
+        compiler_params=params(16 * MB),
         name="finish",
     )(ids, own, other, inverse, back, grad, memory)
 
 
+def fetch_kernel(after_ref, grad_hbm, memory_hbm, grad_ref, memory_ref, sems):
+    copies = [
+        pltpu.make_async_copy(grad_hbm, grad_ref, sems.at[0]),
+        pltpu.make_async_copy(memory_hbm, memory_ref, sems.at[1]),
+    ]
+    for copy in copies:
+        copy.start()
+    for copy in copies:
+        copy.wait()
+
+
+def fetch(after, grad, memory):
+    return pl.pallas_call(
+        fetch_kernel,
+        out_shape=(pltpu.VMEM((ROWS, FF), BF16), pltpu.VMEM((ROWS, FF), BF16)),
+        in_specs=[ANY, ANY, ANY],
+        out_specs=(VMEM, VMEM),
+        scratch_shapes=[pltpu.SemaphoreType.DMA((2,))],
+        compiler_params=params(16 * MB),
+        cost_estimate=pl.CostEstimate(flops=10**8, bytes_accessed=14 * 10**6, transcendentals=0),
+        name="fetch",
+    )(after, grad, memory)
+
+
 def exchange(value, axes):
     return lax.all_to_all(value, axes, 0, 0, tiled=True)
 
@@ -261,24 +307,33 @@
 
 def resident(value):
     return pltpu.with_memory_space_constraint(value, pltpu.VMEM)
+
+
+def far(value):
+    return pltpu.with_memory_space_constraint(value, pltpu.HBM)
 
 
 def on_device(gradients, residual, sketch):
     core = lax.axis_index("c")
     block = lax.axis_index(("x", "z4", "z2"))
     ids = jnp.stack([core, block, lax.axis_index("z1")]).astype(jnp.int32)
-    partial, grad, memory = left_sketch(gradients[0], residual[0], sketch)
+    far_grad, far_memory = far(gradients[0]), far(residual[0])
+    partial, grad, memory = left_sketch(far_grad, far_memory, far(sketch))
+    ids, partial = lax.optimization_barrier((ids, partial))
     pair = partial + swap(partial)
-    parts = spread(pair, "y", 4)
+    parts = [pair] + [lax.ppermute(pair, "y", [(i, i ^ k) for i in range(4)]) for k in (1, 2, 3)]
     own, other = project(ids, parts, resident(grad), resident(memory))
     terms = own + swap(other)
     terms = exchange(terms.reshape(32, TILES + 1, 8, 128), SPREAD)
     terms = jnp.sum(terms, axis=0)
     terms = jnp.sum(spread(terms, ("z4", "z2"), 4).reshape((4,) + terms.shape), axis=0)
     gathered = spread(terms[:TILES], SPREAD, 32).reshape(CHUNKS, 2, TILES, 8, 128)
-    gathered_other = swap(gathered)
     left, inverse, back = factor(ids, terms[TILES], parts)
-    share, fresh = finish(ids, gathered, gathered_other, inverse, back, resident(grad), resident(memory))
+    gathered, inverse = lax.optimization_barrier((gathered, inverse))
+    near_grad, near_memory = fetch(inverse, far_grad, far_memory)
+    share, fresh = finish(
+        ids, gathered, swap(gathered), inverse, back, resident(near_grad), resident(near_memory)
+    )
     return left, share, fresh[None]
 
 

time: 113 us -> 90.5 us (0.80)
  local copies, waits for them, and re-layouts: 17.7 us -> 1 us
  blocking collectives: 54.1 us -> 38.3 us
  waiting for transfers between devices: 7.49 us -> 13.3 us
  starting transfers between devices: 12.1 us -> 16.4 us
    unnamed x18 -> x0, local copies, waits for them, and re-layouts: 17 us -> none
    all_to_all x3 -> x2, blocking collectives: 54.1 us -> 38.3 us  [exchange(): return lax.all_to_all(value, axes, 0, 0, tiled=True)]
    all_to_all x1, waiting for transfers between devices: 4.36 us -> 8.32 us  [exchange(): return lax.all_to_all(value, axes, 0, 0, tiled=True)]
    ppermute x0 -> x3, starting transfers between devices: none -> 3.25 us  [on_device(): lax.ppermute(pair, 'y', [(i, i ^ k) for i in range(4)])]
    ppermute x0 -> x3, waiting for transfers between devices: none -> 1.84 us  [on_device(): lax.ppermute(pair, 'y', [(i, i ^ k) for i in range(4)])]
    pallas_call x1, Pallas kernels: 5.68 us -> 4.11 us  [finish(): pl.pallas_call(update_kernel, out_shape=(jax.ShapeDtypeStruct((RANK, WIDT...]
    pallas_call x1 -> x2, Pallas kernels: 4.36 us -> 5.48 us  [the longest x1 3.17 us: fetch(): pl.pallas_call(fetch_kernel, out_shape=(pltpu.VMEM((ROWS, FF), BF16), plt...]
  transfers between devices with their start and end apart: 4 -> 7, of which waited for: 3 -> 5; matrix products, arithmetic and copies ran while one was open for 0% -> 0% of each run, Pallas kernels for 5% -> 9%
where the time goes in v3:
time: 90.5 us; the launch traced here: 90.2 us
  blocking collectives  38.3 us (42%)
  Pallas kernels  20.2 us (22%)
  starting transfers between devices  16.4 us (18%)
  waiting for transfers between devices  13.3 us (15%)
  local copies, waits for them, and re-layouts  1 us (1%)
    all_to_all x2, blocking collectives, exchange(): return lax.all_to_all(value, axes, 0, 0, tiled=True)  38.3 us
    ppermute x3, starting transfers between devices, swap(): return lax.ppermute(value, 'c', [(0, 1), (1, 0)])  9.2 us
    all_to_all x1, waiting for transfers between devices, exchange(): return lax.all_to_all(value, axes, 0, 0, tiled=True)  8.32 us
    pallas_call x1, Pallas kernels, left_sketch(): pl.pallas_call(sketch_kernel, out_shape=(jax.ShapeDtypeStruct((RANK, ROWS...  5.53 us
    pallas_call x1, Pallas kernels, factor(): pl.pallas_call(factor_kernel, out_shape=(jax.ShapeDtypeStruct((RANK, ROWS...  5.11 us
    pallas_call x1, Pallas kernels, finish(): pl.pallas_call(update_kernel, out_shape=(jax.ShapeDtypeStruct((RANK, WIDT...  4.11 us
    all_to_all x1, starting transfers between devices, exchange(): return lax.all_to_all(value, axes, 0, 0, tiled=True)  3.92 us
    ppermute x3, starting transfers between devices, on_device(): lax.ppermute(pair, 'y', [(i, i ^ k) for i in range(4)])  3.25 us
  transfers between devices with their start and end apart: 7, of which 5 were waited for; matrix products, arithmetic and copies ran while one was open for 0% of the time, Pallas kernels for 9%

profile of v3, /device:TPU:1, one launch (start us, length us, event | category | flops | bytes accessed | tf_op | source)
XLA Modules:
  0.0 90.2 jit_solution(13978687858008090355)
XLA Ops:
  0.6 0.1 pad_add_fusion.ids_ref
  0.7 5.5 %left_sketch.1 = (f32[32,128]{1,0:T(8,128)S(1)}, bf16[128,14336]{1,0:T(8,128)(2,1)S(1)}, bf16[128,14336]{1,0:T(8,128)(2,1)S(1)}) custom-call(bf16[128,14336]{1,0:T(8,128)(2,1)} %bitcast.12, bf16[128,14336]{1,0:T(8,128)(2,1)} %bitcast.14, bf16[32,14336]{1,0:T(8,128)(2,1)} %sketch_hbm.1), custom_call_target="tpu_custom_call" | custom-call | tf_op jit(solution)/shard_map/left_sketch/pallas_call | solution.py:70
  6.3 3.3 %collective-permute-start = (f32[32,128]{1,0:T(8,128)S(1)}, f32[32,128]{1,0:T(8,128)S(1)}, u32[]{:S(2)}, u32[]{:S(2)}) collective-permute-start(f32[32,128]{1,0:T(8,128)S(1)} %get-tuple-element.21), channel_id=1, source_target_pairs={{0,32},{32,0},{1,33},{33,1},{2,34},{34,2},{3,35},{35,3},{4,36},{36... | collective-permute-start | bytes 49160 | tf_op jit(solution)/shard_map/ppermute | solution.py:301
  9.6 0.8 collective-permute-done
  10.4 1.0 %collective-permute-start.3 = (f32[32,128]{1,0:T(8,128)S(1)}, f32[32,128]{1,0:T(8,128)S(1)}, u32[]{:S(2)}, u32[]{:S(2)}) collective-permute-start(f32[32,128]{1,0:T(8,128)S(1)} %add.14.refs_0_), channel_id=1, source_target_pairs={{0,192},{64,128},{128,64},{192,0},{1,193},{65,129},{129,65},{193,1... | collective-permute-start | bytes 49160 | tf_op jit(solution)/shard_map/ppermute | solution.py:324
  11.4 0.3 collective-permute-start.2
  11.8 1.9 %collective-permute-start.1 = (f32[32,128]{1,0:T(8,128)S(1)}, f32[32,128]{1,0:T(8,128)S(1)}, u32[]{:S(2)}, u32[]{:S(2)}) collective-permute-start(f32[32,128]{1,0:T(8,128)S(1)} %add.14.refs_0_), channel_id=1, source_target_pairs={{0,64},{64,0},{128,192},{192,128},{1,65},{65,1},{129,193},{193,129... | collective-permute-start | bytes 49160 | tf_op jit(solution)/shard_map/ppermute | solution.py:324
  13.7 0.5 collective-permute-done.3.refs_3_
  14.2 1.3 %collective-permute-done.2.refs_2_ = f32[32,128]{1,0:T(8,128)S(1)} collective-permute-done((f32[32,128]{1,0:T(8,128)S(1)}, f32[32,128]{1,0:T(8,128)S(1)}, u32[]{:S(2)}, u32[]{:S(2)}) %collective-permute-start.2) | collective-permute-done | bytes 16416 | tf_op jit(solution)/shard_map/ppermute | solution.py:324
  15.5 0.0 collective-permute-done.1.refs_1_
  15.5 2.3 %project.1 = (f32[16,2,8,8,128]{4,3,2,1,0:T(8,128)S(1)}, f32[16,2,8,8,128]{4,3,2,1,0:T(8,128)S(1)}) custom-call(s32[3]{0:T(128)S(1)} %pad_add_fusion.ids_ref, f32[32,128]{1,0:T(8,128)S(1)} %add.14.refs_0_, f32[32,128]{1,0:T(8,128)S(1)} %collective-permute-done.1.refs_1_, f32[32,128]{1,0:T(8,128)S(1)} %collective-permute-done.2.refs_2_, ...), custom_call_target="tpu_custom_call" | custom-call | tf_op jit(solution)/shard_map/project/pallas_call | solution.py:135
  17.8 1.8 %collective-permute-start.4 = (f32[16,2,8,8,128]{4,3,2,1,0:T(8,128)S(1)}, f32[16,2,8,8,128]{4,3,2,1,0:T(8,128)S(1)}, u32[]{:S(2)}, u32[]{:S(2)}) collective-permute-start(f32[16,2,8,8,128]{4,3,2,1,0:T(8,128)S(1)} %get-tuple-element.25), channel_id=1, source_target_pairs={{0,32},{32,0},{1,33},{33,1},{2,34},{34,2},{3,35},{35,3},{4,36},{36... | collective-permute-start | bytes 3145736 | tf_op jit(solution)/shard_map/ppermute | solution.py:301
  19.7 2.3 %collective-permute-done.4 = f32[16,2,8,8,128]{4,3,2,1,0:T(8,128)S(1)} collective-permute-done((f32[16,2,8,8,128]{4,3,2,1,0:T(8,128)S(1)}, f32[16,2,8,8,128]{4,3,2,1,0:T(8,128)S(1)}, u32[]{:S(2)}, u32[]{:S(2)}) %collective-permute-start.4) | collective-permute-done | bytes 1048608 | tf_op jit(solution)/shard_map/ppermute | solution.py:301
  22.0 0.2 add.15
  22.1 24.0 %all_to_all.15 = f32[32,8,8,128]{3,2,1,0:T(8,128)S(1)} all-to-all(f32[32,8,8,128]{3,2,1,0:T(8,128)S(1)} %bitcast.16), channel_id=1, replica_groups=mesh['y'=4,'c'=2,'x'=4,'z4'=2,'z2'=2,'z1'=2] {'y','x','z1'}, dimensions={0} | all-to-all | bytes 2097152 | tf_op jit(solution)/shard_map/all_to_all | solution.py:297
  46.1 0.1 reduce_sum.18
  46.2 14.3 %all_to_all.16 = f32[4,8,8,128]{3,2,1,0:T(8,128)S(1)} all-to-all(f32[4,8,8,128]{3,2,1,0:T(8,128)S(1)} %broadcast_in_dim.6), channel_id=1, replica_groups=mesh['y'=4,'c'=2,'x'=4,'z4'=2,'z2'=2,'z1'=2] {'z4','z2'}, dimensions={0} | all-to-all | bytes 262144 | tf_op jit(solution)/shard_map/all_to_all | solution.py:297
  60.5 1.0 %broadcast_in_dim.7 = f32[32,7,8,128]{3,2,1,0:T(8,128)} broadcast(f32[7,8,128]{2,1,0:T(8,128)S(1)} %slice.9), dimensions={1,2,3} | broadcast | bytes 946176 | tf_op jit(solution)/shard_map/broadcast_in_dim | solution.py:305
  61.5 3.9 %all-to-all-start.2 = ((f32[32,7,8,128]{3,2,1,0:T(8,128)}), f32[32,7,8,128]{3,2,1,0:T(8,128)S(1)}, u32[]{:S(2)}, u32[]{:S(2)}) async-start(f32[32,7,8,128]{3,2,1,0:T(8,128)} %broadcast_in_dim.7), calls=%async_computation.2 | async-start | bytes 1835008 | tf_op jit(solution)/shard_map/all_to_all | solution.py:297
  65.5 5.1 %factor.1 = (f32[32,128]{1,0:T(8,128)}, f32[32,128]{1,0:T(8,128)S(1)}, bf16[128,256]{1,0:T(8,128)(2,1)S(1)}) custom-call(s32[3]{0:T(128)S(1)} %pad_add_fusion.ids_ref, f32[8,128]{1,0:T(8,128)S(1)} %slice_bitcast_fusion.gram_ref, f32[32,128]{1,0:T(8,128)S(1)} %add.14.refs_0_, f32[32,128]{1,0:T(8,128)S(1)} %collective-permute-done.1.refs_1_, ...), custom_call_target="tpu_custom_call" | custom-call | flops 1000000000 | bytes 10000000 | tf_op jit(solution)/shard_map/factor/pallas_call | solution.py:188
  70.6 8.3 %all-to-all-done.2 = f32[32,7,8,128]{3,2,1,0:T(8,128)S(1)} async-done(((f32[32,7,8,128]{3,2,1,0:T(8,128)}), f32[32,7,8,128]{3,2,1,0:T(8,128)S(1)}, u32[]{:S(2)}, u32[]{:S(2)}) %all-to-all-start.2) | async-done | bytes 917536 | tf_op jit(solution)/shard_map/all_to_all | solution.py:297
  78.9 4.0 %collective-permute-start.5 = (f32[16,2,7,8,128]{4,3,2,1,0:T(8,128)S(1)}, f32[16,2,7,8,128]{4,3,2,1,0:T(8,128)S(1)}, u32[]{:S(2)}, u32[]{:S(2)}) collective-permute-start(f32[16,2,7,8,128]{4,3,2,1,0:T(8,128)S(1)} %bitcast.10), channel_id=1, source_target_pairs={{0,32},{32,0},{1,33},{33,1},{2,34},{34,2},{3,35},{35,3},{4,36},{36... | collective-permute-start | bytes 2752520 | tf_op jit(solution)/shard_map/ppermute | solution.py:301
  82.9 3.2 %fetch.1 = (bf16[128,14336]{1,0:T(8,128)(2,1)S(1)}, bf16[128,14336]{1,0:T(8,128)(2,1)S(1)}) custom-call(f32[32,128]{1,0:T(8,128)S(1)} %get-tuple-element.29.after_ref.inverse_ref, bf16[128,14336]{1,0:T(8,128)(2,1)} %bitcast.13, bf16[128,14336]{1,0:T(8,128)(2,1)} %bitcast.15), custom_call_target="tpu_custom_call" | custom-call | flops 100000000 | bytes 14000000 | tf_op jit(solution)/shard_map/fetch/pallas_call | solution.py:284
  86.1 0.0 collective-permute-done.5.other_ref
  86.1 4.1 %finish.1 = (f32[32,448]{1,0:T(8,128)}, bf16[128,14336]{1,0:T(8,128)(2,1)}) custom-call(s32[3]{0:T(128)S(1)} %pad_add_fusion.ids_ref, f32[16,2,7,8,128]{4,3,2,1,0:T(8,128)S(1)} %bitcast.11, f32[16,2,7,8,128]{4,3,2,1,0:T(8,128)S(1)} %collective-permute-done.5.other_ref, f32[32,128]{1,0:T(8,128)S(1)} %get-tuple-element.29.after_ref.inverse_ref, ...), custom_call_target="tpu_custom_call" | custom-call | tf_op jit(solution)/shard_map/finish/pallas_call | solution.py:258
  (5 shorter events, 0.0 us)
Async XLA Ops:
  6.3 4.2 %collective-permute-start = (f32[32,128]{1,0:T(8,128)S(1)}, f32[32,128]{1,0:T(8,128)S(1)}, u32[]{:S(2)}, u32[]{:S(2)}) collective-permute-start(f32[32,128]{1,0:T(8,128)S(1)} %get-tuple-element.21), channel_id=1, source_target_pairs={{0,32},{32,0},{1,33},{33,1},{2,34},{34,2},{3,35},{35,3},{4,36},{36... | collective-permute-start | bytes 49160 | tf_op jit(solution)/shard_map/ppermute | solution.py:301
  10.4 3.8 %collective-permute-start.3 = (f32[32,128]{1,0:T(8,128)S(1)}, f32[32,128]{1,0:T(8,128)S(1)}, u32[]{:S(2)}, u32[]{:S(2)}) collective-permute-start(f32[32,128]{1,0:T(8,128)S(1)} %add.14.refs_0_), channel_id=1, source_target_pairs={{0,192},{64,128},{128,64},{192,0},{1,193},{65,129},{129,65},{193,1... | collective-permute-start | bytes 49160 | tf_op jit(solution)/shard_map/ppermute | solution.py:324
  11.4 4.1 %collective-permute-start.2 = (f32[32,128]{1,0:T(8,128)S(1)}, f32[32,128]{1,0:T(8,128)S(1)}, u32[]{:S(2)}, u32[]{:S(2)}) collective-permute-start(f32[32,128]{1,0:T(8,128)S(1)} %add.14.refs_0_), channel_id=1, source_target_pairs={{0,128},{64,192},{128,0},{192,64},{1,129},{65,193},{129,1},{193,65... | collective-permute-start | bytes 49160 | tf_op jit(solution)/shard_map/ppermute | solution.py:324
  11.8 3.7 %collective-permute-start.1 = (f32[32,128]{1,0:T(8,128)S(1)}, f32[32,128]{1,0:T(8,128)S(1)}, u32[]{:S(2)}, u32[]{:S(2)}) collective-permute-start(f32[32,128]{1,0:T(8,128)S(1)} %add.14.refs_0_), channel_id=1, source_target_pairs={{0,64},{64,0},{128,192},{192,128},{1,65},{65,1},{129,193},{193,129... | collective-permute-start | bytes 49160 | tf_op jit(solution)/shard_map/ppermute | solution.py:324
  17.8 4.1 %collective-permute-start.4 = (f32[16,2,8,8,128]{4,3,2,1,0:T(8,128)S(1)}, f32[16,2,8,8,128]{4,3,2,1,0:T(8,128)S(1)}, u32[]{:S(2)}, u32[]{:S(2)}) collective-permute-start(f32[16,2,8,8,128]{4,3,2,1,0:T(8,128)S(1)} %get-tuple-element.25), channel_id=1, source_target_pairs={{0,32},{32,0},{1,33},{33,1},{2,34},{34,2},{3,35},{35,3},{4,36},{36... | collective-permute-start | bytes 3145736 | tf_op jit(solution)/shard_map/ppermute | solution.py:301
  61.5 17.4 %all-to-all-start.2 = ((f32[32,7,8,128]{3,2,1,0:T(8,128)}), f32[32,7,8,128]{3,2,1,0:T(8,128)S(1)}, u32[]{:S(2)}, u32[]{:S(2)}) async-start(f32[32,7,8,128]{3,2,1,0:T(8,128)} %broadcast_in_dim.7), calls=%async_computation.2 | async-start | bytes 1835008 | tf_op jit(solution)/shard_map/all_to_all | solution.py:297
  78.9 7.2 %collective-permute-start.5 = (f32[16,2,7,8,128]{4,3,2,1,0:T(8,128)S(1)}, f32[16,2,7,8,128]{4,3,2,1,0:T(8,128)S(1)}, u32[]{:S(2)}, u32[]{:S(2)}) collective-permute-start(f32[16,2,7,8,128]{4,3,2,1,0:T(8,128)S(1)} %bitcast.10), channel_id=1, source_target_pairs={{0,32},{32,0},{1,33},{33,1},{2,34},{34,2},{3,35},{35,3},{4,36},{36... | collective-permute-start | bytes 2752520 | tf_op jit(solution)/shard_map/ppermute | solution.py:301

commit v4 on v3

--- a/solution.py
+++ b/solution.py
@@ -301,6 +301,11 @@
     return lax.ppermute(value, "c", [(0, 1), (1, 0)])
 
 
+def four(value, axes):
+    one, three, two = (lax.ppermute(value, axes, [(i, i ^ k) for i in range(4)]) for k in (1, 3, 2))
+    return value, one, two, three
+
+
 def spread(value, axes, count):
     return exchange(jnp.broadcast_to(value[None], (count,) + value.shape), axes)
 
@@ -321,12 +326,13 @@
     partial, grad, memory = left_sketch(far_grad, far_memory, far(sketch))
     ids, partial = lax.optimization_barrier((ids, partial))
     pair = partial + swap(partial)
-    parts = [pair] + [lax.ppermute(pair, "y", [(i, i ^ k) for i in range(4)]) for k in (1, 2, 3)]
+    parts = four(pair, "y")
     own, other = project(ids, parts, resident(grad), resident(memory))
     terms = own + swap(other)
     terms = exchange(terms.reshape(32, TILES + 1, 8, 128), SPREAD)
     terms = jnp.sum(terms, axis=0)
-    terms = jnp.sum(spread(terms, ("z4", "z2"), 4).reshape((4,) + terms.shape), axis=0)
+    one, two, three, last = four(terms, ("z4", "z2"))
+    terms = (one + two) + (three + last)
     gathered = spread(terms[:TILES], SPREAD, 32).reshape(CHUNKS, 2, TILES, 8, 128)
     left, inverse, back = factor(ids, terms[TILES], parts)
     gathered, inverse = lax.optimization_barrier((gathered, inverse))

time: 90.5 us -> 88.5 us (0.978)
  blocking collectives: 38.3 us -> 24 us
  starting transfers between devices: 16.4 us -> 23.2 us
  waiting for transfers between devices: 13.3 us -> 18.9 us
    all_to_all x2 -> x1, blocking collectives: 38.3 us -> 24 us  [exchange(): return lax.all_to_all(value, axes, 0, 0, tiled=True)]
    ppermute x3 -> x6, starting transfers between devices: 3.25 us -> 10.6 us  [four(): lax.ppermute(value, axes, [(i, i ^ k) for i in range(4)])]
    ppermute x3 -> x6, waiting for transfers between devices: 1.84 us -> 6.85 us  [four(): lax.ppermute(value, axes, [(i, i ^ k) for i in range(4)])]
  transfers between devices with their start and end apart: 7 -> 10, of which waited for: 5 -> 6; matrix products, arithmetic and copies ran while one was open for 0% -> 0% of each run, Pallas kernels for 9% -> 9%
where the time goes in v4:
time: 88.5 us; the launch traced here: 88.3 us
  blocking collectives  24 us (27%)
  starting transfers between devices  23.2 us (26%)
  Pallas kernels  20.2 us (23%)
  waiting for transfers between devices  18.9 us (21%)
  local copies, waits for them, and re-layouts  0.99 us (1%)
    all_to_all x1, blocking collectives, exchange(): return lax.all_to_all(value, axes, 0, 0, tiled=True)  24 us
    ppermute x6, starting transfers between devices, four(): lax.ppermute(value, axes, [(i, i ^ k) for i in range(4)])  10.6 us
    all_to_all x1, waiting for transfers between devices, exchange(): return lax.all_to_all(value, axes, 0, 0, tiled=True)  8.93 us
    ppermute x3, starting transfers between devices, swap(): return lax.ppermute(value, 'c', [(0, 1), (1, 0)])  8.6 us
    ppermute x6, waiting for transfers between devices, four(): lax.ppermute(value, axes, [(i, i ^ k) for i in range(4)])  6.85 us
    pallas_call x1, Pallas kernels, left_sketch(): pl.pallas_call(sketch_kernel, out_shape=(jax.ShapeDtypeStruct((RANK, ROWS...  5.53 us
    pallas_call x1, Pallas kernels, factor(): pl.pallas_call(factor_kernel, out_shape=(jax.ShapeDtypeStruct((RANK, ROWS...  5.11 us
    pallas_call x1, Pallas kernels, finish(): pl.pallas_call(update_kernel, out_shape=(jax.ShapeDtypeStruct((RANK, WIDT...  4.09 us
  transfers between devices with their start and end apart: 10, of which 6 were waited for; matrix products, arithmetic and copies ran while one was open for 0% of the time, Pallas kernels for 9%

profile of v4, /device:TPU:1, one launch (start us, length us, event | category | flops | bytes accessed | tf_op | source)
XLA Modules:
  0.0 88.3 jit_solution(1672684197088785154)
XLA Ops:
  0.6 0.1 pad_add_fusion.ids_ref
  0.7 5.5 %left_sketch.1 = (f32[32,128]{1,0:T(8,128)S(1)}, bf16[128,14336]{1,0:T(8,128)(2,1)S(1)}, bf16[128,14336]{1,0:T(8,128)(2,1)S(1)}) custom-call(bf16[128,14336]{1,0:T(8,128)(2,1)} %bitcast.12, bf16[128,14336]{1,0:T(8,128)(2,1)} %bitcast.14, bf16[32,14336]{1,0:T(8,128)(2,1)} %sketch_hbm.1), custom_call_target="tpu_custom_call" | custom-call | tf_op jit(solution)/shard_map/left_sketch/pallas_call | solution.py:70
  6.3 3.3 %collective-permute-start = (f32[32,128]{1,0:T(8,128)S(1)}, f32[32,128]{1,0:T(8,128)S(1)}, u32[]{:S(2)}, u32[]{:S(2)}) collective-permute-start(f32[32,128]{1,0:T(8,128)S(1)} %get-tuple-element.21), channel_id=1, source_target_pairs={{0,32},{32,0},{1,33},{33,1},{2,34},{34,2},{3,35},{35,3},{4,36},{36... | collective-permute-start | bytes 49160 | tf_op jit(solution)/shard_map/ppermute | solution.py:301
  9.6 0.8 collective-permute-done
  10.4 1.0 %collective-permute-start.3 = (f32[32,128]{1,0:T(8,128)S(1)}, f32[32,128]{1,0:T(8,128)S(1)}, u32[]{:S(2)}, u32[]{:S(2)}) collective-permute-start(f32[32,128]{1,0:T(8,128)S(1)} %add.23.refs_0_), channel_id=1, source_target_pairs={{0,192},{64,128},{128,64},{192,0},{1,193},{65,129},{129,65},{193,1... | collective-permute-start | bytes 49160 | tf_op jit(solution)/shard_map/ppermute | solution.py:305
  11.4 0.3 collective-permute-start.2
  11.8 1.9 %collective-permute-start.1 = (f32[32,128]{1,0:T(8,128)S(1)}, f32[32,128]{1,0:T(8,128)S(1)}, u32[]{:S(2)}, u32[]{:S(2)}) collective-permute-start(f32[32,128]{1,0:T(8,128)S(1)} %add.23.refs_0_), channel_id=1, source_target_pairs={{0,64},{64,0},{128,192},{192,128},{1,65},{65,1},{129,193},{193,129... | collective-permute-start | bytes 49160 | tf_op jit(solution)/shard_map/ppermute | solution.py:305
  13.7 0.5 collective-permute-done.3.refs_3_
  14.2 1.3 %collective-permute-done.2.refs_2_ = f32[32,128]{1,0:T(8,128)S(1)} collective-permute-done((f32[32,128]{1,0:T(8,128)S(1)}, f32[32,128]{1,0:T(8,128)S(1)}, u32[]{:S(2)}, u32[]{:S(2)}) %collective-permute-start.2) | collective-permute-done | bytes 16416 | tf_op jit(solution)/shard_map/ppermute | solution.py:305
  15.5 0.0 collective-permute-done.1.refs_1_
  15.5 2.3 %project.1 = (f32[16,2,8,8,128]{4,3,2,1,0:T(8,128)S(1)}, f32[16,2,8,8,128]{4,3,2,1,0:T(8,128)S(1)}) custom-call(s32[3]{0:T(128)S(1)} %pad_add_fusion.ids_ref, f32[32,128]{1,0:T(8,128)S(1)} %add.23.refs_0_, f32[32,128]{1,0:T(8,128)S(1)} %collective-permute-done.1.refs_1_, f32[32,128]{1,0:T(8,128)S(1)} %collective-permute-done.2.refs_2_, ...), custom_call_target="tpu_custom_call" | custom-call | tf_op jit(solution)/shard_map/project/pallas_call | solution.py:135
  17.8 1.8 %collective-permute-start.4 = (f32[16,2,8,8,128]{4,3,2,1,0:T(8,128)S(1)}, f32[16,2,8,8,128]{4,3,2,1,0:T(8,128)S(1)}, u32[]{:S(2)}, u32[]{:S(2)}) collective-permute-start(f32[16,2,8,8,128]{4,3,2,1,0:T(8,128)S(1)} %get-tuple-element.25), channel_id=1, source_target_pairs={{0,32},{32,0},{1,33},{33,1},{2,34},{34,2},{3,35},{35,3},{4,36},{36... | collective-permute-start | bytes 3145736 | tf_op jit(solution)/shard_map/ppermute | solution.py:301
  19.7 2.3 %collective-permute-done.4 = f32[16,2,8,8,128]{4,3,2,1,0:T(8,128)S(1)} collective-permute-done((f32[16,2,8,8,128]{4,3,2,1,0:T(8,128)S(1)}, f32[16,2,8,8,128]{4,3,2,1,0:T(8,128)S(1)}, u32[]{:S(2)}, u32[]{:S(2)}) %collective-permute-start.4) | collective-permute-done | bytes 1048608 | tf_op jit(solution)/shard_map/ppermute | solution.py:301
  22.0 0.2 add.24
  22.1 24.0 %all_to_all.10 = f32[32,8,8,128]{3,2,1,0:T(8,128)S(1)} all-to-all(f32[32,8,8,128]{3,2,1,0:T(8,128)S(1)} %bitcast.16), channel_id=1, replica_groups=mesh['y'=4,'c'=2,'x'=4,'z4'=2,'z2'=2,'z1'=2] {'y','x','z1'}, dimensions={0} | all-to-all | bytes 2097152 | tf_op jit(solution)/shard_map/all_to_all | solution.py:297
  46.1 0.1 reduce_sum.9
  46.2 5.2 %collective-permute-start.7 = (f32[8,8,128]{2,1,0:T(8,128)S(1)}, f32[8,8,128]{2,1,0:T(8,128)S(1)}, u32[]{:S(2)}, u32[]{:S(2)}) collective-permute-start(f32[8,8,128]{2,1,0:T(8,128)S(1)} %reduce_sum.9), channel_id=1, source_target_pairs={{0,6},{2,4},{4,2},{6,0},{1,7},{3,5},{5,3},{7,1},{8,14},{10,12},{12... | collective-permute-start | bytes 98312 | tf_op jit(solution)/shard_map/ppermute | solution.py:305
  51.4 1.2 %collective-permute-start.6 = (f32[8,8,128]{2,1,0:T(8,128)S(1)}, f32[8,8,128]{2,1,0:T(8,128)S(1)}, u32[]{:S(2)}, u32[]{:S(2)}) collective-permute-start(f32[8,8,128]{2,1,0:T(8,128)S(1)} %reduce_sum.9), channel_id=1, source_target_pairs={{0,4},{2,6},{4,0},{6,2},{1,5},{3,7},{5,1},{7,3},{8,12},{10,14},{12... | collective-permute-start | bytes 98312 | tf_op jit(solution)/shard_map/ppermute | solution.py:305
  52.6 1.0 %collective-permute-start.5 = (f32[8,8,128]{2,1,0:T(8,128)S(1)}, f32[8,8,128]{2,1,0:T(8,128)S(1)}, u32[]{:S(2)}, u32[]{:S(2)}) collective-permute-start(f32[8,8,128]{2,1,0:T(8,128)S(1)} %reduce_sum.9), channel_id=1, source_target_pairs={{0,2},{2,0},{4,6},{6,4},{1,3},{3,1},{5,7},{7,5},{8,10},{10,8},{12,... | collective-permute-start | bytes 98312 | tf_op jit(solution)/shard_map/ppermute | solution.py:305
  53.6 0.0 collective-permute-done.7
  53.6 5.0 %collective-permute-done.6 = f32[8,8,128]{2,1,0:T(8,128)S(1)} collective-permute-done((f32[8,8,128]{2,1,0:T(8,128)S(1)}, f32[8,8,128]{2,1,0:T(8,128)S(1)}, u32[]{:S(2)}, u32[]{:S(2)}) %collective-permute-start.6) | collective-permute-done | bytes 32800 | tf_op jit(solution)/shard_map/ppermute | solution.py:305
  58.6 0.0 collective-permute-done.5
  58.6 1.0 %broadcast_in_dim.4 = f32[32,7,8,128]{3,2,1,0:T(8,128)} broadcast(f32[7,8,128]{2,1,0:T(8,128)S(1)} %slice.9), dimensions={1,2,3} | broadcast | bytes 946176 | tf_op jit(solution)/shard_map/broadcast_in_dim | solution.py:310
  59.6 3.9 %all-to-all-start.1 = ((f32[32,7,8,128]{3,2,1,0:T(8,128)}), f32[32,7,8,128]{3,2,1,0:T(8,128)S(1)}, u32[]{:S(2)}, u32[]{:S(2)}) async-start(f32[32,7,8,128]{3,2,1,0:T(8,128)} %broadcast_in_dim.4), calls=%async_computation.1 | async-start | bytes 1835008 | tf_op jit(solution)/shard_map/all_to_all | solution.py:297
  63.5 5.1 %factor.1 = (f32[32,128]{1,0:T(8,128)}, f32[32,128]{1,0:T(8,128)S(1)}, bf16[128,256]{1,0:T(8,128)(2,1)S(1)}) custom-call(s32[3]{0:T(128)S(1)} %pad_add_fusion.ids_ref, f32[8,128]{1,0:T(8,128)S(1)} %slice_bitcast_fusion.gram_ref, f32[32,128]{1,0:T(8,128)S(1)} %add.23.refs_0_, f32[32,128]{1,0:T(8,128)S(1)} %collective-permute-done.1.refs_1_, ...), custom_call_target="tpu_custom_call" | custom-call | flops 1000000000 | bytes 10000000 | tf_op jit(solution)/shard_map/factor/pallas_call | solution.py:188
  68.6 8.9 %all-to-all-done.1 = f32[32,7,8,128]{3,2,1,0:T(8,128)S(1)} async-done(((f32[32,7,8,128]{3,2,1,0:T(8,128)}), f32[32,7,8,128]{3,2,1,0:T(8,128)S(1)}, u32[]{:S(2)}, u32[]{:S(2)}) %all-to-all-start.1) | async-done | bytes 917536 | tf_op jit(solution)/shard_map/all_to_all | solution.py:297
  77.6 3.4 %collective-permute-start.8 = (f32[16,2,7,8,128]{4,3,2,1,0:T(8,128)S(1)}, f32[16,2,7,8,128]{4,3,2,1,0:T(8,128)S(1)}, u32[]{:S(2)}, u32[]{:S(2)}) collective-permute-start(f32[16,2,7,8,128]{4,3,2,1,0:T(8,128)S(1)} %bitcast.10), channel_id=1, source_target_pairs={{0,32},{32,0},{1,33},{33,1},{2,34},{34,2},{3,35},{35,3},{4,36},{36... | collective-permute-start | bytes 2752520 | tf_op jit(solution)/shard_map/ppermute | solution.py:301
  81.0 3.2 %fetch.1 = (bf16[128,14336]{1,0:T(8,128)(2,1)S(1)}, bf16[128,14336]{1,0:T(8,128)(2,1)S(1)}) custom-call(f32[32,128]{1,0:T(8,128)S(1)} %get-tuple-element.29.after_ref.inverse_ref, bf16[128,14336]{1,0:T(8,128)(2,1)} %bitcast.13, bf16[128,14336]{1,0:T(8,128)(2,1)} %bitcast.15), custom_call_target="tpu_custom_call" | custom-call | flops 100000000 | bytes 14000000 | tf_op jit(solution)/shard_map/fetch/pallas_call | solution.py:284
  84.2 0.0 collective-permute-done.8.other_ref
  84.2 4.1 %finish.1 = (f32[32,448]{1,0:T(8,128)}, bf16[128,14336]{1,0:T(8,128)(2,1)}) custom-call(s32[3]{0:T(128)S(1)} %pad_add_fusion.ids_ref, f32[16,2,7,8,128]{4,3,2,1,0:T(8,128)S(1)} %bitcast.11, f32[16,2,7,8,128]{4,3,2,1,0:T(8,128)S(1)} %collective-permute-done.8.other_ref, f32[32,128]{1,0:T(8,128)S(1)} %get-tuple-element.29.after_ref.inverse_ref, ...), custom_call_target="tpu_custom_call" | custom-call | tf_op jit(solution)/shard_map/finish/pallas_call | solution.py:258
  (4 shorter events, 0.0 us)
Async XLA Ops:
  6.3 4.2 %collective-permute-start = (f32[32,128]{1,0:T(8,128)S(1)}, f32[32,128]{1,0:T(8,128)S(1)}, u32[]{:S(2)}, u32[]{:S(2)}) collective-permute-start(f32[32,128]{1,0:T(8,128)S(1)} %get-tuple-element.21), channel_id=1, source_target_pairs={{0,32},{32,0},{1,33},{33,1},{2,34},{34,2},{3,35},{35,3},{4,36},{36... | collective-permute-start | bytes 49160 | tf_op jit(solution)/shard_map/ppermute | solution.py:301
  10.4 3.8 %collective-permute-start.3 = (f32[32,128]{1,0:T(8,128)S(1)}, f32[32,128]{1,0:T(8,128)S(1)}, u32[]{:S(2)}, u32[]{:S(2)}) collective-permute-start(f32[32,128]{1,0:T(8,128)S(1)} %add.23.refs_0_), channel_id=1, source_target_pairs={{0,192},{64,128},{128,64},{192,0},{1,193},{65,129},{129,65},{193,1... | collective-permute-start | bytes 49160 | tf_op jit(solution)/shard_map/ppermute | solution.py:305
  11.4 4.1 %collective-permute-start.2 = (f32[32,128]{1,0:T(8,128)S(1)}, f32[32,128]{1,0:T(8,128)S(1)}, u32[]{:S(2)}, u32[]{:S(2)}) collective-permute-start(f32[32,128]{1,0:T(8,128)S(1)} %add.23.refs_0_), channel_id=1, source_target_pairs={{0,128},{64,192},{128,0},{192,64},{1,129},{65,193},{129,1},{193,65... | collective-permute-start | bytes 49160 | tf_op jit(solution)/shard_map/ppermute | solution.py:305
  11.8 3.7 %collective-permute-start.1 = (f32[32,128]{1,0:T(8,128)S(1)}, f32[32,128]{1,0:T(8,128)S(1)}, u32[]{:S(2)}, u32[]{:S(2)}) collective-permute-start(f32[32,128]{1,0:T(8,128)S(1)} %add.23.refs_0_), channel_id=1, source_target_pairs={{0,64},{64,0},{128,192},{192,128},{1,65},{65,1},{129,193},{193,129... | collective-permute-start | bytes 49160 | tf_op jit(solution)/shard_map/ppermute | solution.py:305
  17.8 4.1 %collective-permute-start.4 = (f32[16,2,8,8,128]{4,3,2,1,0:T(8,128)S(1)}, f32[16,2,8,8,128]{4,3,2,1,0:T(8,128)S(1)}, u32[]{:S(2)}, u32[]{:S(2)}) collective-permute-start(f32[16,2,8,8,128]{4,3,2,1,0:T(8,128)S(1)} %get-tuple-element.25), channel_id=1, source_target_pairs={{0,32},{32,0},{1,33},{33,1},{2,34},{34,2},{3,35},{35,3},{4,36},{36... | collective-permute-start | bytes 3145736 | tf_op jit(solution)/shard_map/ppermute | solution.py:301
  46.2 7.4 %collective-permute-start.7 = (f32[8,8,128]{2,1,0:T(8,128)S(1)}, f32[8,8,128]{2,1,0:T(8,128)S(1)}, u32[]{:S(2)}, u32[]{:S(2)}) collective-permute-start(f32[8,8,128]{2,1,0:T(8,128)S(1)} %reduce_sum.9), channel_id=1, source_target_pairs={{0,6},{2,4},{4,2},{6,0},{1,7},{3,5},{5,3},{7,1},{8,14},{10,12},{12... | collective-permute-start | bytes 98312 | tf_op jit(solution)/shard_map/ppermute | solution.py:305
  51.4 7.2 %collective-permute-start.6 = (f32[8,8,128]{2,1,0:T(8,128)S(1)}, f32[8,8,128]{2,1,0:T(8,128)S(1)}, u32[]{:S(2)}, u32[]{:S(2)}) collective-permute-start(f32[8,8,128]{2,1,0:T(8,128)S(1)} %reduce_sum.9), channel_id=1, source_target_pairs={{0,4},{2,6},{4,0},{6,2},{1,5},{3,7},{5,1},{7,3},{8,12},{10,14},{12... | collective-permute-start | bytes 98312 | tf_op jit(solution)/shard_map/ppermute | solution.py:305
  52.6 6.0 %collective-permute-start.5 = (f32[8,8,128]{2,1,0:T(8,128)S(1)}, f32[8,8,128]{2,1,0:T(8,128)S(1)}, u32[]{:S(2)}, u32[]{:S(2)}) collective-permute-start(f32[8,8,128]{2,1,0:T(8,128)S(1)} %reduce_sum.9), channel_id=1, source_target_pairs={{0,2},{2,0},{4,6},{6,4},{1,3},{3,1},{5,7},{7,5},{8,10},{10,8},{12,... | collective-permute-start | bytes 98312 | tf_op jit(solution)/shard_map/ppermute | solution.py:305
  59.6 18.0 %all-to-all-start.1 = ((f32[32,7,8,128]{3,2,1,0:T(8,128)}), f32[32,7,8,128]{3,2,1,0:T(8,128)S(1)}, u32[]{:S(2)}, u32[]{:S(2)}) async-start(f32[32,7,8,128]{3,2,1,0:T(8,128)} %broadcast_in_dim.4), calls=%async_computation.1 | async-start | bytes 1835008 | tf_op jit(solution)/shard_map/all_to_all | solution.py:297
  77.6 6.6 %collective-permute-start.8 = (f32[16,2,7,8,128]{4,3,2,1,0:T(8,128)S(1)}, f32[16,2,7,8,128]{4,3,2,1,0:T(8,128)S(1)}, u32[]{:S(2)}, u32[]{:S(2)}) collective-permute-start(f32[16,2,7,8,128]{4,3,2,1,0:T(8,128)S(1)} %bitcast.10), channel_id=1, source_target_pairs={{0,32},{32,0},{1,33},{33,1},{2,34},{34,2},{3,35},{35,3},{4,36},{36... | collective-permute-start | bytes 2752520 | tf_op jit(solution)/shard_map/ppermute | solution.py:301

commit v5 on v4

--- a/solution.py
+++ b/solution.py
@@ -145,21 +145,39 @@
 def factor_kernel(ids_ref, gram_ref, *refs):
     part_refs, (left_ref, inverse_ref, back_ref) = refs[:4], refs[4:]
     core = ids_ref[0]
-    rows = lax.broadcasted_iota(jnp.int32, (RANK, 128), 0)
+    row = lax.broadcasted_iota(jnp.int32, (8, 128), 0)
+    lane = lax.broadcasted_iota(jnp.int32, (8, 128), 1)
+    tile = gram_ref[...] * (1.0 / 8)
+    work, scales = [], []
+    for q in range(4):
+        part = pltpu.roll(tile, 128 - 32 * q, 1) if q else tile
+        work.append(jnp.where(lane < 32, part, jnp.where(lane == row + (32 + 8 * q), 1.0, 0.0)))
+    summed = mean_of(part_refs)
+    basis = [summed[8 * q : 8 * q + 8] for q in range(4)]
+    for p in range(4):
+        below = range(p, 4)
+        columns = [
+            {g: jnp.broadcast_to(work[g][:, 8 * p + q : 8 * p + q + 1], (8, 128)) for g in below} for q in range(8)
+        ]
+        scale = jnp.ones((8, 128), F32)
+        for q in range(8):
+            pivot = columns[q][p][q : q + 1]
+            scale = jnp.where(row == q, pivot, scale)
+            ratio = 1.0 / pivot
+            factors = {g: columns[q][g] * ratio for g in below}
+            factors[p] = jnp.where(row > q, factors[p], 0.0)
+            for later in range(q + 1, 8):
+                edge = columns[later][p][q : q + 1]
+                for g in below:
+                    columns[later][g] = columns[later][g] - factors[g] * edge
+            work_row, basis_row = work[p][q : q + 1], basis[p][q : q + 1]
+            for g in below:
+                work[g] = work[g] - factors[g] * work_row
+                basis[g] = basis[g] - factors[g] * basis_row
+        scales.append(lax.rsqrt(scale))
+    scale = jnp.concatenate(scales, axis=0)
+    work, basis = jnp.concatenate(work, axis=0), jnp.concatenate(basis, axis=0)
     lanes = lax.broadcasted_iota(jnp.int32, (RANK, 128), 1)
-    tile = gram_ref[...] * (1.0 / 8)
-    packed = jnp.concatenate([tile] + [pltpu.roll(tile, 128 - 32 * q, 1) for q in (1, 2, 3)], axis=0)
-    work = jnp.where(lanes < 32, packed, jnp.where(lanes == rows + 32, 1.0, 0.0))
-    basis = mean_of(part_refs)
-    scale = jnp.ones((RANK, 128), F32)
-    for step in range(RANK):
-        column = jnp.broadcast_to(work[:, step : step + 1], (RANK, 128))
-        pivot = column[step : step + 1]
-        scale = jnp.where(rows == step, pivot, scale)
-        factor = jnp.where(rows > step, column / pivot, 0.0)
-        work = work - factor * work[step : step + 1]
-        basis = basis - factor * basis[step : step + 1]
-    scale = lax.rsqrt(scale)
     left = basis * scale
     left_ref[...] = left
     inverse = pltpu.roll(work * scale, 96, 1)
@@ -195,7 +213,7 @@
         in_specs=[SMEM] + [VMEM] * 5,
         out_specs=(VMEM, VMEM, VMEM),
         compiler_params=params(16 * MB),
-        cost_estimate=pl.CostEstimate(flops=10**9, bytes_accessed=10**7, transcendentals=0),
+        cost_estimate=pl.CostEstimate(flops=2 * 10**10, bytes_accessed=10**7, transcendentals=0),
         name="factor",
     )(ids, gram, *parts)
 
@@ -267,30 +285,6 @@
         compiler_params=params(16 * MB),
         name="finish",
     )(ids, own, other, inverse, back, grad, memory)
-
-
-def fetch_kernel(after_ref, grad_hbm, memory_hbm, grad_ref, memory_ref, sems):
-    copies = [
-        pltpu.make_async_copy(grad_hbm, grad_ref, sems.at[0]),
-        pltpu.make_async_copy(memory_hbm, memory_ref, sems.at[1]),
-    ]
-    for copy in copies:
-        copy.start()
-    for copy in copies:
-        copy.wait()
-
-
-def fetch(after, grad, memory):
-    return pl.pallas_call(
-        fetch_kernel,
-        out_shape=(pltpu.VMEM((ROWS, FF), BF16), pltpu.VMEM((ROWS, FF), BF16)),
-        in_specs=[ANY, ANY, ANY],
-        out_specs=(VMEM, VMEM),
-        scratch_shapes=[pltpu.SemaphoreType.DMA((2,))],
-        compiler_params=params(16 * MB),
-        cost_estimate=pl.CostEstimate(flops=10**8, bytes_accessed=14 * 10**6, transcendentals=0),
-        name="fetch",
-    )(after, grad, memory)
 
 
 def exchange(value, axes):
@@ -334,11 +328,10 @@
     one, two, three, last = four(terms, ("z4", "z2"))
     terms = (one + two) + (three + last)
     gathered = spread(terms[:TILES], SPREAD, 32).reshape(CHUNKS, 2, TILES, 8, 128)
-    left, inverse, back = factor(ids, terms[TILES], parts)
-    gathered, inverse = lax.optimization_barrier((gathered, inverse))
-    near_grad, near_memory = fetch(inverse, far_grad, far_memory)
+    gathered, gram = lax.optimization_barrier((gathered, terms[TILES]))
+    left, inverse, back = factor(ids, gram, parts)
     share, fresh = finish(
-        ids, gathered, swap(gathered), inverse, back, resident(near_grad), resident(near_memory)
+        ids, gathered, swap(gathered), inverse, back, resident(gradients[0]), resident(residual[0])
     )
     return left, share, fresh[None]
 

time: 88.5 us -> 87.5 us (0.989)
  Pallas kernels: 20.2 us -> 13.9 us
  waiting for transfers between devices: 18.9 us -> 24.2 us
    all_to_all x1, waiting for transfers between devices: 8.93 us -> 14 us  [exchange(): return lax.all_to_all(value, axes, 0, 0, tiled=True)]
    pallas_call x1, Pallas kernels: 5.11 us -> 1.92 us  [factor(): pl.pallas_call(factor_kernel, out_shape=(jax.ShapeDtypeStruct((RANK, ROWS...]
    pallas_call x1 -> x0, Pallas kernels: 3.17 us -> none  [fetch(): pl.pallas_call(fetch_kernel, out_shape=(pltpu.VMEM((ROWS, FF), BF16), plt...]
  transfers between devices with their start and end apart: 10 -> 10, of which waited for: 6 -> 7; matrix products, arithmetic and copies ran while one was open for 0% -> 0% of each run, Pallas kernels for 9% -> 2%
where the time goes in v5:
time: 87.5 us; the launch traced here: 87.2 us
  waiting for transfers between devices  24.2 us (28%)
  blocking collectives  24 us (27%)
  starting transfers between devices  23.2 us (27%)
  Pallas kernels  13.9 us (16%)
  local copies, waits for them, and re-layouts  1 us (1%)
    all_to_all x1, blocking collectives, exchange(): return lax.all_to_all(value, axes, 0, 0, tiled=True)  24 us
    all_to_all x1, waiting for transfers between devices, exchange(): return lax.all_to_all(value, axes, 0, 0, tiled=True)  14 us
    ppermute x6, starting transfers between devices, four(): lax.ppermute(value, axes, [(i, i ^ k) for i in range(4)])  10.6 us
    ppermute x3, starting transfers between devices, swap(): return lax.ppermute(value, 'c', [(0, 1), (1, 0)])  8.6 us
    ppermute x6, waiting for transfers between devices, four(): lax.ppermute(value, axes, [(i, i ^ k) for i in range(4)])  6.85 us
    pallas_call x1, Pallas kernels, left_sketch(): pl.pallas_call(sketch_kernel, out_shape=(jax.ShapeDtypeStruct((RANK, ROWS...  5.53 us
    pallas_call x1, Pallas kernels, finish(): pl.pallas_call(update_kernel, out_shape=(jax.ShapeDtypeStruct((RANK, WIDT...  4.14 us
    all_to_all x1, starting transfers between devices, exchange(): return lax.all_to_all(value, axes, 0, 0, tiled=True)  3.92 us
  transfers between devices with their start and end apart: 10, of which 7 were waited for; matrix products, arithmetic and copies ran while one was open for 0% of the time, Pallas kernels for 2%

profile of v5, /device:TPU:1, one launch (start us, length us, event | category | flops | bytes accessed | tf_op | source)
XLA Modules:
  0.0 87.2 jit_solution(6577739500989490896)
XLA Ops:
  0.6 0.1 pad_add_fusion.ids_ref
  0.7 5.5 %left_sketch.1 = (f32[32,128]{1,0:T(8,128)S(1)}, bf16[128,14336]{1,0:T(8,128)(2,1)S(1)}, bf16[128,14336]{1,0:T(8,128)(2,1)S(1)}) custom-call(bf16[128,14336]{1,0:T(8,128)(2,1)} %bitcast.10, bf16[128,14336]{1,0:T(8,128)(2,1)} %bitcast.12, bf16[32,14336]{1,0:T(8,128)(2,1)} %sketch_hbm.1), custom_call_target="tpu_custom_call" | custom-call | tf_op jit(solution)/shard_map/left_sketch/pallas_call | solution.py:70
  6.3 3.3 %collective-permute-start = (f32[32,128]{1,0:T(8,128)S(1)}, f32[32,128]{1,0:T(8,128)S(1)}, u32[]{:S(2)}, u32[]{:S(2)}) collective-permute-start(f32[32,128]{1,0:T(8,128)S(1)} %get-tuple-element.19), channel_id=1, source_target_pairs={{0,32},{32,0},{1,33},{33,1},{2,34},{34,2},{3,35},{35,3},{4,36},{36... | collective-permute-start | bytes 49160 | tf_op jit(solution)/shard_map/ppermute | solution.py:295
  9.6 0.8 collective-permute-done
  10.4 1.0 %collective-permute-start.3 = (f32[32,128]{1,0:T(8,128)S(1)}, f32[32,128]{1,0:T(8,128)S(1)}, u32[]{:S(2)}, u32[]{:S(2)}) collective-permute-start(f32[32,128]{1,0:T(8,128)S(1)} %add.23.refs_0_), channel_id=1, source_target_pairs={{0,192},{64,128},{128,64},{192,0},{1,193},{65,129},{129,65},{193,1... | collective-permute-start | bytes 49160 | tf_op jit(solution)/shard_map/ppermute | solution.py:299
  11.4 0.3 collective-permute-start.2
  11.8 1.9 %collective-permute-start.1 = (f32[32,128]{1,0:T(8,128)S(1)}, f32[32,128]{1,0:T(8,128)S(1)}, u32[]{:S(2)}, u32[]{:S(2)}) collective-permute-start(f32[32,128]{1,0:T(8,128)S(1)} %add.23.refs_0_), channel_id=1, source_target_pairs={{0,64},{64,0},{128,192},{192,128},{1,65},{65,1},{129,193},{193,129... | collective-permute-start | bytes 49160 | tf_op jit(solution)/shard_map/ppermute | solution.py:299
  13.7 0.5 collective-permute-done.3.refs_3_
  14.2 1.3 %collective-permute-done.2.refs_2_ = f32[32,128]{1,0:T(8,128)S(1)} collective-permute-done((f32[32,128]{1,0:T(8,128)S(1)}, f32[32,128]{1,0:T(8,128)S(1)}, u32[]{:S(2)}, u32[]{:S(2)}) %collective-permute-start.2) | collective-permute-done | bytes 16416 | tf_op jit(solution)/shard_map/ppermute | solution.py:299
  15.5 0.0 collective-permute-done.1.refs_1_
  15.5 2.3 %project.1 = (f32[16,2,8,8,128]{4,3,2,1,0:T(8,128)S(1)}, f32[16,2,8,8,128]{4,3,2,1,0:T(8,128)S(1)}) custom-call(s32[3]{0:T(128)S(1)} %pad_add_fusion.ids_ref, f32[32,128]{1,0:T(8,128)S(1)} %add.23.refs_0_, f32[32,128]{1,0:T(8,128)S(1)} %collective-permute-done.1.refs_1_, f32[32,128]{1,0:T(8,128)S(1)} %collective-permute-done.2.refs_2_, ...), custom_call_target="tpu_custom_call" | custom-call | tf_op jit(solution)/shard_map/project/pallas_call | solution.py:135
  17.8 1.8 %collective-permute-start.4 = (f32[16,2,8,8,128]{4,3,2,1,0:T(8,128)S(1)}, f32[16,2,8,8,128]{4,3,2,1,0:T(8,128)S(1)}, u32[]{:S(2)}, u32[]{:S(2)}) collective-permute-start(f32[16,2,8,8,128]{4,3,2,1,0:T(8,128)S(1)} %get-tuple-element.23), channel_id=1, source_target_pairs={{0,32},{32,0},{1,33},{33,1},{2,34},{34,2},{3,35},{35,3},{4,36},{36... | collective-permute-start | bytes 3145736 | tf_op jit(solution)/shard_map/ppermute | solution.py:295
  19.7 2.3 %collective-permute-done.4 = f32[16,2,8,8,128]{4,3,2,1,0:T(8,128)S(1)} collective-permute-done((f32[16,2,8,8,128]{4,3,2,1,0:T(8,128)S(1)}, f32[16,2,8,8,128]{4,3,2,1,0:T(8,128)S(1)}, u32[]{:S(2)}, u32[]{:S(2)}) %collective-permute-start.4) | collective-permute-done | bytes 1048608 | tf_op jit(solution)/shard_map/ppermute | solution.py:295
  22.0 0.2 add.24
  22.1 24.0 %all_to_all.10 = f32[32,8,8,128]{3,2,1,0:T(8,128)S(1)} all-to-all(f32[32,8,8,128]{3,2,1,0:T(8,128)S(1)} %bitcast.16), channel_id=1, replica_groups=mesh['y'=4,'c'=2,'x'=4,'z4'=2,'z2'=2,'z1'=2] {'y','x','z1'}, dimensions={0} | all-to-all | bytes 2097152 | tf_op jit(solution)/shard_map/all_to_all | solution.py:291
  46.1 0.1 reduce_sum.9
  46.2 5.2 %collective-permute-start.7 = (f32[8,8,128]{2,1,0:T(8,128)S(1)}, f32[8,8,128]{2,1,0:T(8,128)S(1)}, u32[]{:S(2)}, u32[]{:S(2)}) collective-permute-start(f32[8,8,128]{2,1,0:T(8,128)S(1)} %reduce_sum.9), channel_id=1, source_target_pairs={{0,6},{2,4},{4,2},{6,0},{1,7},{3,5},{5,3},{7,1},{8,14},{10,12},{12... | collective-permute-start | bytes 98312 | tf_op jit(solution)/shard_map/ppermute | solution.py:299
  51.4 1.2 %collective-permute-start.6 = (f32[8,8,128]{2,1,0:T(8,128)S(1)}, f32[8,8,128]{2,1,0:T(8,128)S(1)}, u32[]{:S(2)}, u32[]{:S(2)}) collective-permute-start(f32[8,8,128]{2,1,0:T(8,128)S(1)} %reduce_sum.9), channel_id=1, source_target_pairs={{0,4},{2,6},{4,0},{6,2},{1,5},{3,7},{5,1},{7,3},{8,12},{10,14},{12... | collective-permute-start | bytes 98312 | tf_op jit(solution)/shard_map/ppermute | solution.py:299
  52.6 1.0 %collective-permute-start.5 = (f32[8,8,128]{2,1,0:T(8,128)S(1)}, f32[8,8,128]{2,1,0:T(8,128)S(1)}, u32[]{:S(2)}, u32[]{:S(2)}) collective-permute-start(f32[8,8,128]{2,1,0:T(8,128)S(1)} %reduce_sum.9), channel_id=1, source_target_pairs={{0,2},{2,0},{4,6},{6,4},{1,3},{3,1},{5,7},{7,5},{8,10},{10,8},{12,... | collective-permute-start | bytes 98312 | tf_op jit(solution)/shard_map/ppermute | solution.py:299
  53.6 0.0 collective-permute-done.7
  53.6 5.0 %collective-permute-done.6 = f32[8,8,128]{2,1,0:T(8,128)S(1)} collective-permute-done((f32[8,8,128]{2,1,0:T(8,128)S(1)}, f32[8,8,128]{2,1,0:T(8,128)S(1)}, u32[]{:S(2)}, u32[]{:S(2)}) %collective-permute-start.6) | collective-permute-done | bytes 32800 | tf_op jit(solution)/shard_map/ppermute | solution.py:299
  58.6 0.0 collective-permute-done.5
  58.6 1.0 %broadcast_in_dim.4 = f32[32,7,8,128]{3,2,1,0:T(8,128)} broadcast(f32[7,8,128]{2,1,0:T(8,128)S(1)} %slice.8), dimensions={1,2,3} | broadcast | bytes 946176 | tf_op jit(solution)/shard_map/broadcast_in_dim | solution.py:304
  59.6 3.9 %all-to-all-start.1 = ((f32[32,7,8,128]{3,2,1,0:T(8,128)}), f32[32,7,8,128]{3,2,1,0:T(8,128)S(1)}, u32[]{:S(2)}, u32[]{:S(2)}) async-start(f32[32,7,8,128]{3,2,1,0:T(8,128)} %broadcast_in_dim.4), calls=%async_computation.1 | async-start | bytes 1835008 | tf_op jit(solution)/shard_map/all_to_all | solution.py:291
  63.5 14.0 %all-to-all-done.1 = f32[32,7,8,128]{3,2,1,0:T(8,128)S(1)} async-done(((f32[32,7,8,128]{3,2,1,0:T(8,128)}), f32[32,7,8,128]{3,2,1,0:T(8,128)S(1)}, u32[]{:S(2)}, u32[]{:S(2)}) %all-to-all-start.1) | async-done | bytes 917536 | tf_op jit(solution)/shard_map/all_to_all | solution.py:291
  77.6 0.0 copy-start
  77.6 0.0 copy-start.1
  77.6 3.4 %collective-permute-start.8 = (f32[16,2,7,8,128]{4,3,2,1,0:T(8,128)S(1)}, f32[16,2,7,8,128]{4,3,2,1,0:T(8,128)S(1)}, u32[]{:S(2)}, u32[]{:S(2)}) collective-permute-start(f32[16,2,7,8,128]{4,3,2,1,0:T(8,128)S(1)} %bitcast.14), channel_id=1, source_target_pairs={{0,32},{32,0},{1,33},{33,1},{2,34},{34,2},{3,35},{35,3},{4,36},{36... | collective-permute-start | bytes 2752520 | tf_op jit(solution)/shard_map/ppermute | solution.py:295
  81.0 1.9 %factor.1 = (f32[32,128]{1,0:T(8,128)}, f32[32,128]{1,0:T(8,128)S(1)}, bf16[128,256]{1,0:T(8,128)(2,1)S(1)}) custom-call(s32[3]{0:T(128)S(1)} %pad_add_fusion.ids_ref, f32[8,128]{1,0:T(8,128)S(1)} %slice_bitcast_fusion.gram_ref, f32[32,128]{1,0:T(8,128)S(1)} %add.23.refs_0_, f32[32,128]{1,0:T(8,128)S(1)} %collective-permute-done.1.refs_1_, ...), custom_call_target="tpu_custom_call" | custom-call | flops 20000000000 | bytes 10000000 | tf_op jit(solution)/shard_map/factor/pallas_call | solution.py:206
  82.9 0.2 collective-permute-done.8.other_ref
  83.1 0.0 copy-done
  83.1 0.0 copy-done.1
  83.1 4.1 %finish.1 = (f32[32,448]{1,0:T(8,128)}, bf16[128,14336]{1,0:T(8,128)(2,1)}) custom-call(s32[3]{0:T(128)S(1)} %pad_add_fusion.ids_ref, f32[16,2,7,8,128]{4,3,2,1,0:T(8,128)S(1)} %bitcast.15, f32[16,2,7,8,128]{4,3,2,1,0:T(8,128)S(1)} %collective-permute-done.8.other_ref, f32[32,128]{1,0:T(8,128)S(1)} %get-tuple-element.27.inverse_ref, ...), custom_call_target="tpu_custom_call" | custom-call | tf_op jit(solution)/shard_map/finish/pallas_call | solution.py:276
  (4 shorter events, 0.0 us)
Async XLA Ops:
  6.3 4.2 %collective-permute-start = (f32[32,128]{1,0:T(8,128)S(1)}, f32[32,128]{1,0:T(8,128)S(1)}, u32[]{:S(2)}, u32[]{:S(2)}) collective-permute-start(f32[32,128]{1,0:T(8,128)S(1)} %get-tuple-element.19), channel_id=1, source_target_pairs={{0,32},{32,0},{1,33},{33,1},{2,34},{34,2},{3,35},{35,3},{4,36},{36... | collective-permute-start | bytes 49160 | tf_op jit(solution)/shard_map/ppermute | solution.py:295
  10.4 3.8 %collective-permute-start.3 = (f32[32,128]{1,0:T(8,128)S(1)}, f32[32,128]{1,0:T(8,128)S(1)}, u32[]{:S(2)}, u32[]{:S(2)}) collective-permute-start(f32[32,128]{1,0:T(8,128)S(1)} %add.23.refs_0_), channel_id=1, source_target_pairs={{0,192},{64,128},{128,64},{192,0},{1,193},{65,129},{129,65},{193,1... | collective-permute-start | bytes 49160 | tf_op jit(solution)/shard_map/ppermute | solution.py:299
  11.4 4.1 %collective-permute-start.2 = (f32[32,128]{1,0:T(8,128)S(1)}, f32[32,128]{1,0:T(8,128)S(1)}, u32[]{:S(2)}, u32[]{:S(2)}) collective-permute-start(f32[32,128]{1,0:T(8,128)S(1)} %add.23.refs_0_), channel_id=1, source_target_pairs={{0,128},{64,192},{128,0},{192,64},{1,129},{65,193},{129,1},{193,65... | collective-permute-start | bytes 49160 | tf_op jit(solution)/shard_map/ppermute | solution.py:299
  11.8 3.7 %collective-permute-start.1 = (f32[32,128]{1,0:T(8,128)S(1)}, f32[32,128]{1,0:T(8,128)S(1)}, u32[]{:S(2)}, u32[]{:S(2)}) collective-permute-start(f32[32,128]{1,0:T(8,128)S(1)} %add.23.refs_0_), channel_id=1, source_target_pairs={{0,64},{64,0},{128,192},{192,128},{1,65},{65,1},{129,193},{193,129... | collective-permute-start | bytes 49160 | tf_op jit(solution)/shard_map/ppermute | solution.py:299
  17.8 4.1 %collective-permute-start.4 = (f32[16,2,8,8,128]{4,3,2,1,0:T(8,128)S(1)}, f32[16,2,8,8,128]{4,3,2,1,0:T(8,128)S(1)}, u32[]{:S(2)}, u32[]{:S(2)}) collective-permute-start(f32[16,2,8,8,128]{4,3,2,1,0:T(8,128)S(1)} %get-tuple-element.23), channel_id=1, source_target_pairs={{0,32},{32,0},{1,33},{33,1},{2,34},{34,2},{3,35},{35,3},{4,36},{36... | collective-permute-start | bytes 3145736 | tf_op jit(solution)/shard_map/ppermute | solution.py:295
  46.2 7.4 %collective-permute-start.7 = (f32[8,8,128]{2,1,0:T(8,128)S(1)}, f32[8,8,128]{2,1,0:T(8,128)S(1)}, u32[]{:S(2)}, u32[]{:S(2)}) collective-permute-start(f32[8,8,128]{2,1,0:T(8,128)S(1)} %reduce_sum.9), channel_id=1, source_target_pairs={{0,6},{2,4},{4,2},{6,0},{1,7},{3,5},{5,3},{7,1},{8,14},{10,12},{12... | collective-permute-start | bytes 98312 | tf_op jit(solution)/shard_map/ppermute | solution.py:299
  51.4 7.2 %collective-permute-start.6 = (f32[8,8,128]{2,1,0:T(8,128)S(1)}, f32[8,8,128]{2,1,0:T(8,128)S(1)}, u32[]{:S(2)}, u32[]{:S(2)}) collective-permute-start(f32[8,8,128]{2,1,0:T(8,128)S(1)} %reduce_sum.9), channel_id=1, source_target_pairs={{0,4},{2,6},{4,0},{6,2},{1,5},{3,7},{5,1},{7,3},{8,12},{10,14},{12... | collective-permute-start | bytes 98312 | tf_op jit(solution)/shard_map/ppermute | solution.py:299
  52.6 6.0 %collective-permute-start.5 = (f32[8,8,128]{2,1,0:T(8,128)S(1)}, f32[8,8,128]{2,1,0:T(8,128)S(1)}, u32[]{:S(2)}, u32[]{:S(2)}) collective-permute-start(f32[8,8,128]{2,1,0:T(8,128)S(1)} %reduce_sum.9), channel_id=1, source_target_pairs={{0,2},{2,0},{4,6},{6,4},{1,3},{3,1},{5,7},{7,5},{8,10},{10,8},{12,... | collective-permute-start | bytes 98312 | tf_op jit(solution)/shard_map/ppermute | solution.py:299
  59.6 18.0 %all-to-all-start.1 = ((f32[32,7,8,128]{3,2,1,0:T(8,128)}), f32[32,7,8,128]{3,2,1,0:T(8,128)S(1)}, u32[]{:S(2)}, u32[]{:S(2)}) async-start(f32[32,7,8,128]{3,2,1,0:T(8,128)} %broadcast_in_dim.4), calls=%async_computation.1 | async-start | bytes 1835008 | tf_op jit(solution)/shard_map/all_to_all | solution.py:291
  77.6 5.5 %copy-start = (bf16[1,128,14336]{2,1,0:T(8,128)(2,1)S(1)}, bf16[1,128,14336]{2,1,0:T(8,128)(2,1)}, u32[]{:S(2)}) copy-start(bf16[1,128,14336]{2,1,0:T(8,128)(2,1)} %param.3) | copy-start | bytes 11010052
  77.6 5.5 %copy-start.1 = (bf16[1,128,14336]{2,1,0:T(8,128)(2,1)S(1)}, bf16[1,128,14336]{2,1,0:T(8,128)(2,1)}, u32[]{:S(2)}) copy-start(bf16[1,128,14336]{2,1,0:T(8,128)(2,1)} %param.4) | copy-start | bytes 11010052
  77.6 5.5 %collective-permute-start.8 = (f32[16,2,7,8,128]{4,3,2,1,0:T(8,128)S(1)}, f32[16,2,7,8,128]{4,3,2,1,0:T(8,128)S(1)}, u32[]{:S(2)}, u32[]{:S(2)}) collective-permute-start(f32[16,2,7,8,128]{4,3,2,1,0:T(8,128)S(1)} %bitcast.14), channel_id=1, source_target_pairs={{0,32},{32,0},{1,33},{33,1},{2,34},{34,2},{3,35},{35,3},{4,36},{36... | collective-permute-start | bytes 2752520 | tf_op jit(solution)/shard_map/ppermute | solution.py:295

commit v6 on v5

--- a/solution.py
+++ b/solution.py
@@ -40,15 +40,17 @@
     return first, second, rest - second
 
 
-def sketch_kernel(grad_hbm, memory_hbm, sketch_hbm, out_ref, grad_ref, memory_ref, sketch_ref, sems):
+def product(sketch, block):
+    return lax.dot_general(sketch, block, (((1,), (1,)), ((), ())), preferred_element_type=F32)
+
+
+def first_kernel(grad_hbm, sketch_hbm, out_ref, grad_ref, sketch_ref, sems):
     copies = []
     for step in range(LOADS):
         cols = pl.ds(step * LOAD_WIDTH, LOAD_WIDTH)
         group = [
             pltpu.make_async_copy(src.at[:, cols], dst.at[:, cols], sems.at[step, which])
-            for which, (src, dst) in enumerate(
-                ((sketch_hbm, sketch_ref), (grad_hbm, grad_ref), (memory_hbm, memory_ref))
-            )
+            for which, (src, dst) in enumerate(((sketch_hbm, sketch_ref), (grad_hbm, grad_ref)))
         ]
         for copy in group:
             copy.start()
@@ -58,28 +60,38 @@
         for copy in copies[step]:
             copy.wait()
         cols = pl.ds(step * LOAD_WIDTH, LOAD_WIDTH)
-        probe = sketch_ref[:, cols]
-        for block in (grad_ref, memory_ref):
-            total += lax.dot_general(
-                probe, block[:, cols], (((1,), (1,)), ((), ())), preferred_element_type=F32
-            )
+        total += product(sketch_ref[:, cols], grad_ref[:, cols])
     out_ref[...] = total
 
 
+def second_kernel(first_ref, sketch_ref, memory_ref, out_ref):
+    out_ref[...] = first_ref[...] + product(sketch_ref[...], memory_ref[...])
+
+
 def left_sketch(grad, memory, sketch):
-    return pl.pallas_call(
-        sketch_kernel,
+    first, near_grad, near_sketch = pl.pallas_call(
+        first_kernel,
         out_shape=(
             jax.ShapeDtypeStruct((RANK, ROWS), F32),
             pltpu.VMEM((ROWS, FF), BF16),
-            pltpu.VMEM((ROWS, FF), BF16),
+            pltpu.VMEM((RANK, FF), BF16),
         ),
-        in_specs=[ANY, ANY, ANY],
-        out_specs=(VMEM, VMEM, VMEM),
-        scratch_shapes=[pltpu.VMEM((RANK, FF), BF16), pltpu.SemaphoreType.DMA((LOADS, 3))],
-        compiler_params=params(16 * MB),
-        name="left_sketch",
-    )(grad, memory, sketch)
+        in_specs=[ANY, ANY],
+        out_specs=(VMEM,) * 3,
+        scratch_shapes=[pltpu.SemaphoreType.DMA((LOADS, 2))],
+        compiler_params=params(16 * MB),
+        cost_estimate=pl.CostEstimate(flops=2 * 10**10, bytes_accessed=10**7, transcendentals=0),
+        name="left_first",
+    )(grad, sketch)
+    total = pl.pallas_call(
+        second_kernel,
+        out_shape=jax.ShapeDtypeStruct((RANK, ROWS), F32),
+        in_specs=[VMEM] * 3,
+        out_specs=VMEM,
+        compiler_params=params(16 * MB),
+        name="left_second",
+    )(first, resident(near_sketch), resident(memory))
+    return total, near_grad
 
 
 def mean_of(part_refs):
@@ -296,7 +308,7 @@
 
 
 def four(value, axes):
-    one, three, two = (lax.ppermute(value, axes, [(i, i ^ k) for i in range(4)]) for k in (1, 3, 2))
+    three, two, one = (lax.ppermute(value, axes, [(i, i ^ k) for i in range(4)]) for k in (3, 2, 1))
     return value, one, two, three
 
 
@@ -316,12 +328,12 @@
     core = lax.axis_index("c")
     block = lax.axis_index(("x", "z4", "z2"))
     ids = jnp.stack([core, block, lax.axis_index("z1")]).astype(jnp.int32)
-    far_grad, far_memory = far(gradients[0]), far(residual[0])
-    partial, grad, memory = left_sketch(far_grad, far_memory, far(sketch))
+    far_grad = far(gradients[0])
+    partial, grad = left_sketch(far_grad, residual[0], far(sketch))
     ids, partial = lax.optimization_barrier((ids, partial))
     pair = partial + swap(partial)
     parts = four(pair, "y")
-    own, other = project(ids, parts, resident(grad), resident(memory))
+    own, other = project(ids, parts, resident(grad), resident(residual[0]))
     terms = own + swap(other)
     terms = exchange(terms.reshape(32, TILES + 1, 8, 128), SPREAD)
     terms = jnp.sum(terms, axis=0)

time: 87.5 us -> 86.9 us (level)
    pallas_call x1 -> x2, Pallas kernels: 5.53 us -> 5.09 us  [the longest x1 3.73 us: left_sketch(): pl.pallas_call(first_kernel, out_shape=(jax.ShapeDtypeStruct((RANK, ROWS)...]
where the time goes in v6:
time: 86.9 us; the launch traced here: 86.6 us
  waiting for transfers between devices  24.2 us (28%)
  blocking collectives  24 us (28%)
  starting transfers between devices  23.2 us (27%)
  Pallas kernels  13.3 us (15%)
  local copies, waits for them, and re-layouts  1 us (1%)
    all_to_all x1, blocking collectives, exchange(): return lax.all_to_all(value, axes, 0, 0, tiled=True)  24 us
    all_to_all x1, waiting for transfers between devices, exchange(): return lax.all_to_all(value, axes, 0, 0, tiled=True)  14 us
    ppermute x6, starting transfers between devices, four(): lax.ppermute(value, axes, [(i, i ^ k) for i in range(4)])  10.6 us
    ppermute x3, starting transfers between devices, swap(): return lax.ppermute(value, 'c', [(0, 1), (1, 0)])  8.59 us
    ppermute x6, waiting for transfers between devices, four(): lax.ppermute(value, axes, [(i, i ^ k) for i in range(4)])  6.85 us
    pallas_call x1, Pallas kernels, finish(): pl.pallas_call(update_kernel, out_shape=(jax.ShapeDtypeStruct((RANK, WIDT...  4.06 us
    all_to_all x1, starting transfers between devices, exchange(): return lax.all_to_all(value, axes, 0, 0, tiled=True)  3.92 us
    pallas_call x1, Pallas kernels, left_sketch(): pl.pallas_call(first_kernel, out_shape=(jax.ShapeDtypeStruct((RANK, ROWS)...  3.73 us
  transfers between devices with their start and end apart: 10, of which 7 were waited for; matrix products, arithmetic and copies ran while one was open for 0% of the time, Pallas kernels for 2%

profile of v6, /device:TPU:1, one launch (start us, length us, event | category | flops | bytes accessed | tf_op | source)
XLA Modules:
  0.0 86.6 jit_solution(4785322215107933233)
XLA Ops:
  0.6 0.0 copy-start
  0.7 3.7 %left_first.1 = (f32[32,128]{1,0:T(8,128)S(1)}, bf16[128,14336]{1,0:T(8,128)(2,1)S(1)}, bf16[32,14336]{1,0:T(8,128)(2,1)S(1)}) custom-call(bf16[128,14336]{1,0:T(8,128)(2,1)} %bitcast.15, bf16[32,14336]{1,0:T(8,128)(2,1)} %sketch_hbm.1), custom_call_target="tpu_custom_call" | custom-call | flops 20000000000 | bytes 10000000 | tf_op jit(solution)/shard_map/left_first/pallas_call | solution.py:72
  4.4 0.1 pad_add_fusion.ids_ref
  4.5 0.0 copy-done
  4.5 1.4 %left_second.1 = f32[32,128]{1,0:T(8,128)S(1)} custom-call(f32[32,128]{1,0:T(8,128)S(1)} %get-tuple-element.17.first_ref, bf16[32,14336]{1,0:T(8,128)(2,1)S(1)} %get-tuple-element.18.sketch_ref, bf16[128,14336]{1,0:T(8,128)(2,1)S(1)} %bitcast.10), custom_call_target="tpu_custom_call" | custom-call | tf_op jit(solution)/shard_map/left_second/pallas_call | solution.py:86
  5.8 3.3 %collective-permute-start = (f32[32,128]{1,0:T(8,128)S(1)}, f32[32,128]{1,0:T(8,128)S(1)}, u32[]{:S(2)}, u32[]{:S(2)}) collective-permute-start(f32[32,128]{1,0:T(8,128)S(1)} %left_second.1), channel_id=1, source_target_pairs={{0,32},{32,0},{1,33},{33,1},{2,34},{34,2},{3,35},{35,3},{4,36},{36... | collective-permute-start | bytes 49160 | tf_op jit(solution)/shard_map/ppermute | solution.py:307
  9.1 0.8 collective-permute-done
  10.0 1.0 %collective-permute-start.3 = (f32[32,128]{1,0:T(8,128)S(1)}, f32[32,128]{1,0:T(8,128)S(1)}, u32[]{:S(2)}, u32[]{:S(2)}) collective-permute-start(f32[32,128]{1,0:T(8,128)S(1)} %add.23.refs_0_), channel_id=1, source_target_pairs={{0,192},{64,128},{128,64},{192,0},{1,193},{65,129},{129,65},{193,1... | collective-permute-start | bytes 49160 | tf_op jit(solution)/shard_map/ppermute | solution.py:311
  11.0 0.3 collective-permute-start.2
  11.3 1.9 %collective-permute-start.1 = (f32[32,128]{1,0:T(8,128)S(1)}, f32[32,128]{1,0:T(8,128)S(1)}, u32[]{:S(2)}, u32[]{:S(2)}) collective-permute-start(f32[32,128]{1,0:T(8,128)S(1)} %add.23.refs_0_), channel_id=1, source_target_pairs={{0,64},{64,0},{128,192},{192,128},{1,65},{65,1},{129,193},{193,129... | collective-permute-start | bytes 49160 | tf_op jit(solution)/shard_map/ppermute | solution.py:311
  13.2 0.5 collective-permute-done.3.refs_3_
  13.8 1.3 %collective-permute-done.2.refs_2_ = f32[32,128]{1,0:T(8,128)S(1)} collective-permute-done((f32[32,128]{1,0:T(8,128)S(1)}, f32[32,128]{1,0:T(8,128)S(1)}, u32[]{:S(2)}, u32[]{:S(2)}) %collective-permute-start.2) | collective-permute-done | bytes 16416 | tf_op jit(solution)/shard_map/ppermute | solution.py:311
  15.1 0.0 collective-permute-done.1.refs_1_
  15.1 2.2 %project.1 = (f32[16,2,8,8,128]{4,3,2,1,0:T(8,128)S(1)}, f32[16,2,8,8,128]{4,3,2,1,0:T(8,128)S(1)}) custom-call(s32[3]{0:T(128)S(1)} %pad_add_fusion.ids_ref, f32[32,128]{1,0:T(8,128)S(1)} %add.23.refs_0_, f32[32,128]{1,0:T(8,128)S(1)} %collective-permute-done.1.refs_1_, f32[32,128]{1,0:T(8,128)S(1)} %collective-permute-done.2.refs_2_, ...), custom_call_target="tpu_custom_call" | custom-call | tf_op jit(solution)/shard_map/project/pallas_call | solution.py:147
  17.3 1.9 %collective-permute-start.4 = (f32[16,2,8,8,128]{4,3,2,1,0:T(8,128)S(1)}, f32[16,2,8,8,128]{4,3,2,1,0:T(8,128)S(1)}, u32[]{:S(2)}, u32[]{:S(2)}) collective-permute-start(f32[16,2,8,8,128]{4,3,2,1,0:T(8,128)S(1)} %get-tuple-element.23), channel_id=1, source_target_pairs={{0,32},{32,0},{1,33},{33,1},{2,34},{34,2},{3,35},{35,3},{4,36},{36... | collective-permute-start | bytes 3145736 | tf_op jit(solution)/shard_map/ppermute | solution.py:307
  19.1 2.3 %collective-permute-done.4 = f32[16,2,8,8,128]{4,3,2,1,0:T(8,128)S(1)} collective-permute-done((f32[16,2,8,8,128]{4,3,2,1,0:T(8,128)S(1)}, f32[16,2,8,8,128]{4,3,2,1,0:T(8,128)S(1)}, u32[]{:S(2)}, u32[]{:S(2)}) %collective-permute-start.4) | collective-permute-done | bytes 1048608 | tf_op jit(solution)/shard_map/ppermute | solution.py:307
  21.4 0.2 add.24
  21.6 24.0 %all_to_all.10 = f32[32,8,8,128]{3,2,1,0:T(8,128)S(1)} all-to-all(f32[32,8,8,128]{3,2,1,0:T(8,128)S(1)} %bitcast.17), channel_id=1, replica_groups=mesh['y'=4,'c'=2,'x'=4,'z4'=2,'z2'=2,'z1'=2] {'y','x','z1'}, dimensions={0} | all-to-all | bytes 2097152 | tf_op jit(solution)/shard_map/all_to_all | solution.py:303
  45.6 0.1 reduce_sum.9
  45.6 5.2 %collective-permute-start.7 = (f32[8,8,128]{2,1,0:T(8,128)S(1)}, f32[8,8,128]{2,1,0:T(8,128)S(1)}, u32[]{:S(2)}, u32[]{:S(2)}) collective-permute-start(f32[8,8,128]{2,1,0:T(8,128)S(1)} %reduce_sum.9), channel_id=1, source_target_pairs={{0,6},{2,4},{4,2},{6,0},{1,7},{3,5},{5,3},{7,1},{8,14},{10,12},{12... | collective-permute-start | bytes 98312 | tf_op jit(solution)/shard_map/ppermute | solution.py:311
  50.9 1.2 %collective-permute-start.6 = (f32[8,8,128]{2,1,0:T(8,128)S(1)}, f32[8,8,128]{2,1,0:T(8,128)S(1)}, u32[]{:S(2)}, u32[]{:S(2)}) collective-permute-start(f32[8,8,128]{2,1,0:T(8,128)S(1)} %reduce_sum.9), channel_id=1, source_target_pairs={{0,4},{2,6},{4,0},{6,2},{1,5},{3,7},{5,1},{7,3},{8,12},{10,14},{12... | collective-permute-start | bytes 98312 | tf_op jit(solution)/shard_map/ppermute | solution.py:311
  52.0 1.0 %collective-permute-start.5 = (f32[8,8,128]{2,1,0:T(8,128)S(1)}, f32[8,8,128]{2,1,0:T(8,128)S(1)}, u32[]{:S(2)}, u32[]{:S(2)}) collective-permute-start(f32[8,8,128]{2,1,0:T(8,128)S(1)} %reduce_sum.9), channel_id=1, source_target_pairs={{0,2},{2,0},{4,6},{6,4},{1,3},{3,1},{5,7},{7,5},{8,10},{10,8},{12,... | collective-permute-start | bytes 98312 | tf_op jit(solution)/shard_map/ppermute | solution.py:311
  53.0 0.0 collective-permute-done.7
  53.0 5.0 %collective-permute-done.6 = f32[8,8,128]{2,1,0:T(8,128)S(1)} collective-permute-done((f32[8,8,128]{2,1,0:T(8,128)S(1)}, f32[8,8,128]{2,1,0:T(8,128)S(1)}, u32[]{:S(2)}, u32[]{:S(2)}) %collective-permute-start.6) | collective-permute-done | bytes 32800 | tf_op jit(solution)/shard_map/ppermute | solution.py:311
  58.0 0.0 collective-permute-done.5
  58.1 1.0 %broadcast_in_dim.4 = f32[32,7,8,128]{3,2,1,0:T(8,128)} broadcast(f32[7,8,128]{2,1,0:T(8,128)S(1)} %slice.8), dimensions={1,2,3} | broadcast | bytes 946176 | tf_op jit(solution)/shard_map/broadcast_in_dim | solution.py:316
  59.1 3.9 %all-to-all-start.1 = ((f32[32,7,8,128]{3,2,1,0:T(8,128)}), f32[32,7,8,128]{3,2,1,0:T(8,128)S(1)}, u32[]{:S(2)}, u32[]{:S(2)}) async-start(f32[32,7,8,128]{3,2,1,0:T(8,128)} %broadcast_in_dim.4), calls=%async_computation.1 | async-start | bytes 1835008 | tf_op jit(solution)/shard_map/all_to_all | solution.py:303
  63.0 14.0 %all-to-all-done.1 = f32[32,7,8,128]{3,2,1,0:T(8,128)S(1)} async-done(((f32[32,7,8,128]{3,2,1,0:T(8,128)}), f32[32,7,8,128]{3,2,1,0:T(8,128)S(1)}, u32[]{:S(2)}, u32[]{:S(2)}) %all-to-all-start.1) | async-done | bytes 917536 | tf_op jit(solution)/shard_map/all_to_all | solution.py:303
  77.0 0.0 copy-start.1
  77.0 0.0 copy-start.2
  77.0 3.4 %collective-permute-start.8 = (f32[16,2,7,8,128]{4,3,2,1,0:T(8,128)S(1)}, f32[16,2,7,8,128]{4,3,2,1,0:T(8,128)S(1)}, u32[]{:S(2)}, u32[]{:S(2)}) collective-permute-start(f32[16,2,7,8,128]{4,3,2,1,0:T(8,128)S(1)} %bitcast.13), channel_id=1, source_target_pairs={{0,32},{32,0},{1,33},{33,1},{2,34},{34,2},{3,35},{35,3},{4,36},{36... | collective-permute-start | bytes 2752520 | tf_op jit(solution)/shard_map/ppermute | solution.py:307
  80.5 1.9 %factor.1 = (f32[32,128]{1,0:T(8,128)}, f32[32,128]{1,0:T(8,128)S(1)}, bf16[128,256]{1,0:T(8,128)(2,1)S(1)}) custom-call(s32[3]{0:T(128)S(1)} %pad_add_fusion.ids_ref, f32[8,128]{1,0:T(8,128)S(1)} %slice_bitcast_fusion.gram_ref, f32[32,128]{1,0:T(8,128)S(1)} %add.23.refs_0_, f32[32,128]{1,0:T(8,128)S(1)} %collective-permute-done.1.refs_1_, ...), custom_call_target="tpu_custom_call" | custom-call | flops 20000000000 | bytes 10000000 | tf_op jit(solution)/shard_map/factor/pallas_call | solution.py:218
  82.4 0.2 collective-permute-done.8.other_ref
  82.6 0.0 copy-done.1
  82.6 0.0 copy-done.2
  82.6 4.1 %finish.1 = (f32[32,448]{1,0:T(8,128)}, bf16[128,14336]{1,0:T(8,128)(2,1)}) custom-call(s32[3]{0:T(128)S(1)} %pad_add_fusion.ids_ref, f32[16,2,7,8,128]{4,3,2,1,0:T(8,128)S(1)} %bitcast.14, f32[16,2,7,8,128]{4,3,2,1,0:T(8,128)S(1)} %collective-permute-done.8.other_ref, f32[32,128]{1,0:T(8,128)S(1)} %get-tuple-element.27.inverse_ref, ...), custom_call_target="tpu_custom_call" | custom-call | tf_op jit(solution)/shard_map/finish/pallas_call | solution.py:288
  (4 shorter events, 0.0 us)
Async XLA Ops:
  0.6 3.8 %copy-start = (bf16[1,128,14336]{2,1,0:T(8,128)(2,1)S(1)}, bf16[1,128,14336]{2,1,0:T(8,128)(2,1)}, u32[]{:S(2)}) copy-start(bf16[1,128,14336]{2,1,0:T(8,128)(2,1)} %param.4) | copy-start | bytes 11010052
  5.8 4.1 %collective-permute-start = (f32[32,128]{1,0:T(8,128)S(1)}, f32[32,128]{1,0:T(8,128)S(1)}, u32[]{:S(2)}, u32[]{:S(2)}) collective-permute-start(f32[32,128]{1,0:T(8,128)S(1)} %left_second.1), channel_id=1, source_target_pairs={{0,32},{32,0},{1,33},{33,1},{2,34},{34,2},{3,35},{35,3},{4,36},{36... | collective-permute-start | bytes 49160 | tf_op jit(solution)/shard_map/ppermute | solution.py:307
  10.0 3.8 %collective-permute-start.3 = (f32[32,128]{1,0:T(8,128)S(1)}, f32[32,128]{1,0:T(8,128)S(1)}, u32[]{:S(2)}, u32[]{:S(2)}) collective-permute-start(f32[32,128]{1,0:T(8,128)S(1)} %add.23.refs_0_), channel_id=1, source_target_pairs={{0,192},{64,128},{128,64},{192,0},{1,193},{65,129},{129,65},{193,1... | collective-permute-start | bytes 49160 | tf_op jit(solution)/shard_map/ppermute | solution.py:311
  11.0 4.1 %collective-permute-start.2 = (f32[32,128]{1,0:T(8,128)S(1)}, f32[32,128]{1,0:T(8,128)S(1)}, u32[]{:S(2)}, u32[]{:S(2)}) collective-permute-start(f32[32,128]{1,0:T(8,128)S(1)} %add.23.refs_0_), channel_id=1, source_target_pairs={{0,128},{64,192},{128,0},{192,64},{1,129},{65,193},{129,1},{193,65... | collective-permute-start | bytes 49160 | tf_op jit(solution)/shard_map/ppermute | solution.py:311
  11.3 3.7 %collective-permute-start.1 = (f32[32,128]{1,0:T(8,128)S(1)}, f32[32,128]{1,0:T(8,128)S(1)}, u32[]{:S(2)}, u32[]{:S(2)}) collective-permute-start(f32[32,128]{1,0:T(8,128)S(1)} %add.23.refs_0_), channel_id=1, source_target_pairs={{0,64},{64,0},{128,192},{192,128},{1,65},{65,1},{129,193},{193,129... | collective-permute-start | bytes 49160 | tf_op jit(solution)/shard_map/ppermute | solution.py:311
  17.3 4.1 %collective-permute-start.4 = (f32[16,2,8,8,128]{4,3,2,1,0:T(8,128)S(1)}, f32[16,2,8,8,128]{4,3,2,1,0:T(8,128)S(1)}, u32[]{:S(2)}, u32[]{:S(2)}) collective-permute-start(f32[16,2,8,8,128]{4,3,2,1,0:T(8,128)S(1)} %get-tuple-element.23), channel_id=1, source_target_pairs={{0,32},{32,0},{1,33},{33,1},{2,34},{34,2},{3,35},{35,3},{4,36},{36... | collective-permute-start | bytes 3145736 | tf_op jit(solution)/shard_map/ppermute | solution.py:307
  45.6 7.4 %collective-permute-start.7 = (f32[8,8,128]{2,1,0:T(8,128)S(1)}, f32[8,8,128]{2,1,0:T(8,128)S(1)}, u32[]{:S(2)}, u32[]{:S(2)}) collective-permute-start(f32[8,8,128]{2,1,0:T(8,128)S(1)} %reduce_sum.9), channel_id=1, source_target_pairs={{0,6},{2,4},{4,2},{6,0},{1,7},{3,5},{5,3},{7,1},{8,14},{10,12},{12... | collective-permute-start | bytes 98312 | tf_op jit(solution)/shard_map/ppermute | solution.py:311
  50.9 7.2 %collective-permute-start.6 = (f32[8,8,128]{2,1,0:T(8,128)S(1)}, f32[8,8,128]{2,1,0:T(8,128)S(1)}, u32[]{:S(2)}, u32[]{:S(2)}) collective-permute-start(f32[8,8,128]{2,1,0:T(8,128)S(1)} %reduce_sum.9), channel_id=1, source_target_pairs={{0,4},{2,6},{4,0},{6,2},{1,5},{3,7},{5,1},{7,3},{8,12},{10,14},{12... | collective-permute-start | bytes 98312 | tf_op jit(solution)/shard_map/ppermute | solution.py:311
  52.0 6.0 %collective-permute-start.5 = (f32[8,8,128]{2,1,0:T(8,128)S(1)}, f32[8,8,128]{2,1,0:T(8,128)S(1)}, u32[]{:S(2)}, u32[]{:S(2)}) collective-permute-start(f32[8,8,128]{2,1,0:T(8,128)S(1)} %reduce_sum.9), channel_id=1, source_target_pairs={{0,2},{2,0},{4,6},{6,4},{1,3},{3,1},{5,7},{7,5},{8,10},{10,8},{12,... | collective-permute-start | bytes 98312 | tf_op jit(solution)/shard_map/ppermute | solution.py:311
  59.1 18.0 %all-to-all-start.1 = ((f32[32,7,8,128]{3,2,1,0:T(8,128)}), f32[32,7,8,128]{3,2,1,0:T(8,128)S(1)}, u32[]{:S(2)}, u32[]{:S(2)}) async-start(f32[32,7,8,128]{3,2,1,0:T(8,128)} %broadcast_in_dim.4), calls=%async_computation.1 | async-start | bytes 1835008 | tf_op jit(solution)/shard_map/all_to_all | solution.py:303
  77.0 5.5 %copy-start.1 = (bf16[1,128,14336]{2,1,0:T(8,128)(2,1)S(1)}, bf16[1,128,14336]{2,1,0:T(8,128)(2,1)}, u32[]{:S(2)}) copy-start(bf16[1,128,14336]{2,1,0:T(8,128)(2,1)} %param.4) | copy-start | bytes 11010052
  77.0 5.5 %copy-start.2 = (bf16[1,128,14336]{2,1,0:T(8,128)(2,1)S(1)}, bf16[1,128,14336]{2,1,0:T(8,128)(2,1)}, u32[]{:S(2)}) copy-start(bf16[1,128,14336]{2,1,0:T(8,128)(2,1)} %param.3) | copy-start | bytes 11010052
  77.0 5.5 %collective-permute-start.8 = (f32[16,2,7,8,128]{4,3,2,1,0:T(8,128)S(1)}, f32[16,2,7,8,128]{4,3,2,1,0:T(8,128)S(1)}, u32[]{:S(2)}, u32[]{:S(2)}) collective-permute-start(f32[16,2,7,8,128]{4,3,2,1,0:T(8,128)S(1)} %bitcast.13), channel_id=1, source_target_pairs={{0,32},{32,0},{1,33},{33,1},{2,34},{34,2},{3,35},{35,3},{4,36},{36... | collective-permute-start | bytes 2752520 | tf_op jit(solution)/shard_map/ppermute | solution.py:307

commit v7 on v6

--- a/solution.py
+++ b/solution.py
@@ -20,6 +20,9 @@
 GROUP = 4
 STEPS = CHUNKS // GROUP
 STEP_WIDTH = GROUP * WIDTH
+LAST_GROUP = 2
+LAST_STEPS = CHUNKS // LAST_GROUP
+LAST_WIDTH = LAST_GROUP * WIDTH
 F32 = jnp.float32
 BF16 = jnp.bfloat16
 MB = 1024 * 1024
@@ -235,7 +238,7 @@
     share_ref, out_hbm, out_ref, store_sems,
 ):
     def columns(step):
-        return pl.ds(step * STEP_WIDTH, STEP_WIDTH)
+        return pl.ds(step * LAST_WIDTH, LAST_WIDTH)
 
     def store(step):
         cols = columns(step)
@@ -248,8 +251,8 @@
         parts = [ref[chunk, row, tile] for ref in (own_ref, other_ref) for row in range(2)]
         return jnp.concatenate(parts, axis=0)
 
-    for step in range(STEPS):
-        tiles = [block(step * GROUP + member, tile) for member in range(GROUP) for tile in range(TILES)]
+    for step in range(LAST_STEPS):
+        tiles = [block(step * LAST_GROUP + member, tile) for member in range(LAST_GROUP) for tile in range(TILES)]
         right = jnp.concatenate(tiles, axis=1)
         one, two, three = (part.astype(BF16) for part in three_parts(right))
         stack = jnp.concatenate([one, one, one, two, two, three], axis=0)
@@ -280,7 +283,7 @@
     half = WIDTH // 2
     share_ref[...] = jnp.where(odd == 0, share[:, :half], share[:, half:])
 
-    for step in range(STEPS):
+    for step in range(LAST_STEPS):
         store(step).wait()
 
 
@@ -293,7 +296,7 @@
         ),
         in_specs=[SMEM] + [VMEM] * 6,
         out_specs=(VMEM, ANY),
-        scratch_shapes=[pltpu.VMEM((ROWS, FF), BF16), pltpu.SemaphoreType.DMA((STEPS,))],
+        scratch_shapes=[pltpu.VMEM((ROWS, FF), BF16), pltpu.SemaphoreType.DMA((LAST_STEPS,))],
         compiler_params=params(16 * MB),
         name="finish",
     )(ids, own, other, inverse, back, grad, memory)

time: 86.9 us -> 86.8 us (level)
  no operation moved by 1% of the time
where the time goes in v7:
time: 86.8 us; the launch traced here: 86.5 us
  waiting for transfers between devices  24.2 us (28%)
  blocking collectives  24 us (28%)
  starting transfers between devices  23.2 us (27%)
  Pallas kernels  13.2 us (15%)
  local copies, waits for them, and re-layouts  1 us (1%)
    all_to_all x1, blocking collectives, exchange(): return lax.all_to_all(value, axes, 0, 0, tiled=True)  24 us
    all_to_all x1, waiting for transfers between devices, exchange(): return lax.all_to_all(value, axes, 0, 0, tiled=True)  14 us
    ppermute x6, starting transfers between devices, four(): lax.ppermute(value, axes, [(i, i ^ k) for i in range(4)])  10.6 us
    ppermute x3, starting transfers between devices, swap(): return lax.ppermute(value, 'c', [(0, 1), (1, 0)])  8.59 us
    ppermute x6, waiting for transfers between devices, four(): lax.ppermute(value, axes, [(i, i ^ k) for i in range(4)])  6.85 us
    pallas_call x1, Pallas kernels, finish(): pl.pallas_call(update_kernel, out_shape=(jax.ShapeDtypeStruct((RANK, WIDT...  3.96 us
    all_to_all x1, starting transfers between devices, exchange(): return lax.all_to_all(value, axes, 0, 0, tiled=True)  3.92 us
    pallas_call x1, Pallas kernels, left_sketch(): pl.pallas_call(first_kernel, out_shape=(jax.ShapeDtypeStruct((RANK, ROWS)...  3.73 us
  transfers between devices with their start and end apart: 10, of which 7 were waited for; matrix products, arithmetic and copies ran while one was open for 0% of the time, Pallas kernels for 2%

profile of v7, /device:TPU:1, one launch (start us, length us, event | category | flops | bytes accessed | tf_op | source)
XLA Modules:
  0.0 86.5 jit_solution(14966320427265154312)
XLA Ops:
  0.6 0.0 copy-start
  0.7 3.7 %left_first.1 = (f32[32,128]{1,0:T(8,128)S(1)}, bf16[128,14336]{1,0:T(8,128)(2,1)S(1)}, bf16[32,14336]{1,0:T(8,128)(2,1)S(1)}) custom-call(bf16[128,14336]{1,0:T(8,128)(2,1)} %bitcast.15, bf16[32,14336]{1,0:T(8,128)(2,1)} %sketch_hbm.1), custom_call_target="tpu_custom_call" | custom-call | flops 20000000000 | bytes 10000000 | tf_op jit(solution)/shard_map/left_first/pallas_call | solution.py:75
  4.4 0.1 pad_add_fusion.ids_ref
  4.5 0.0 copy-done
  4.5 1.4 %left_second.1 = f32[32,128]{1,0:T(8,128)S(1)} custom-call(f32[32,128]{1,0:T(8,128)S(1)} %get-tuple-element.17.first_ref, bf16[32,14336]{1,0:T(8,128)(2,1)S(1)} %get-tuple-element.18.sketch_ref, bf16[128,14336]{1,0:T(8,128)(2,1)S(1)} %bitcast.10), custom_call_target="tpu_custom_call" | custom-call | tf_op jit(solution)/shard_map/left_second/pallas_call | solution.py:89
  5.8 3.3 %collective-permute-start = (f32[32,128]{1,0:T(8,128)S(1)}, f32[32,128]{1,0:T(8,128)S(1)}, u32[]{:S(2)}, u32[]{:S(2)}) collective-permute-start(f32[32,128]{1,0:T(8,128)S(1)} %left_second.1), channel_id=1, source_target_pairs={{0,32},{32,0},{1,33},{33,1},{2,34},{34,2},{3,35},{35,3},{4,36},{36... | collective-permute-start | bytes 49160 | tf_op jit(solution)/shard_map/ppermute | solution.py:310
  9.1 0.8 collective-permute-done
  10.0 1.0 %collective-permute-start.3 = (f32[32,128]{1,0:T(8,128)S(1)}, f32[32,128]{1,0:T(8,128)S(1)}, u32[]{:S(2)}, u32[]{:S(2)}) collective-permute-start(f32[32,128]{1,0:T(8,128)S(1)} %add.23.refs_0_), channel_id=1, source_target_pairs={{0,192},{64,128},{128,64},{192,0},{1,193},{65,129},{129,65},{193,1... | collective-permute-start | bytes 49160 | tf_op jit(solution)/shard_map/ppermute | solution.py:314
  11.0 0.3 collective-permute-start.2
  11.3 1.9 %collective-permute-start.1 = (f32[32,128]{1,0:T(8,128)S(1)}, f32[32,128]{1,0:T(8,128)S(1)}, u32[]{:S(2)}, u32[]{:S(2)}) collective-permute-start(f32[32,128]{1,0:T(8,128)S(1)} %add.23.refs_0_), channel_id=1, source_target_pairs={{0,64},{64,0},{128,192},{192,128},{1,65},{65,1},{129,193},{193,129... | collective-permute-start | bytes 49160 | tf_op jit(solution)/shard_map/ppermute | solution.py:314
  13.2 0.5 collective-permute-done.3.refs_3_
  13.8 1.3 %collective-permute-done.2.refs_2_ = f32[32,128]{1,0:T(8,128)S(1)} collective-permute-done((f32[32,128]{1,0:T(8,128)S(1)}, f32[32,128]{1,0:T(8,128)S(1)}, u32[]{:S(2)}, u32[]{:S(2)}) %collective-permute-start.2) | collective-permute-done | bytes 16416 | tf_op jit(solution)/shard_map/ppermute | solution.py:314
  15.1 0.0 collective-permute-done.1.refs_1_
  15.1 2.2 %project.1 = (f32[16,2,8,8,128]{4,3,2,1,0:T(8,128)S(1)}, f32[16,2,8,8,128]{4,3,2,1,0:T(8,128)S(1)}) custom-call(s32[3]{0:T(128)S(1)} %pad_add_fusion.ids_ref, f32[32,128]{1,0:T(8,128)S(1)} %add.23.refs_0_, f32[32,128]{1,0:T(8,128)S(1)} %collective-permute-done.1.refs_1_, f32[32,128]{1,0:T(8,128)S(1)} %collective-permute-done.2.refs_2_, ...), custom_call_target="tpu_custom_call" | custom-call | tf_op jit(solution)/shard_map/project/pallas_call | solution.py:150
  17.3 1.9 %collective-permute-start.4 = (f32[16,2,8,8,128]{4,3,2,1,0:T(8,128)S(1)}, f32[16,2,8,8,128]{4,3,2,1,0:T(8,128)S(1)}, u32[]{:S(2)}, u32[]{:S(2)}) collective-permute-start(f32[16,2,8,8,128]{4,3,2,1,0:T(8,128)S(1)} %get-tuple-element.23), channel_id=1, source_target_pairs={{0,32},{32,0},{1,33},{33,1},{2,34},{34,2},{3,35},{35,3},{4,36},{36... | collective-permute-start | bytes 3145736 | tf_op jit(solution)/shard_map/ppermute | solution.py:310
  19.1 2.3 %collective-permute-done.4 = f32[16,2,8,8,128]{4,3,2,1,0:T(8,128)S(1)} collective-permute-done((f32[16,2,8,8,128]{4,3,2,1,0:T(8,128)S(1)}, f32[16,2,8,8,128]{4,3,2,1,0:T(8,128)S(1)}, u32[]{:S(2)}, u32[]{:S(2)}) %collective-permute-start.4) | collective-permute-done | bytes 1048608 | tf_op jit(solution)/shard_map/ppermute | solution.py:310
  21.4 0.2 add.24
  21.6 24.0 %all_to_all.10 = f32[32,8,8,128]{3,2,1,0:T(8,128)S(1)} all-to-all(f32[32,8,8,128]{3,2,1,0:T(8,128)S(1)} %bitcast.17), channel_id=1, replica_groups=mesh['y'=4,'c'=2,'x'=4,'z4'=2,'z2'=2,'z1'=2] {'y','x','z1'}, dimensions={0} | all-to-all | bytes 2097152 | tf_op jit(solution)/shard_map/all_to_all | solution.py:306
  45.6 0.1 reduce_sum.9
  45.6 5.2 %collective-permute-start.7 = (f32[8,8,128]{2,1,0:T(8,128)S(1)}, f32[8,8,128]{2,1,0:T(8,128)S(1)}, u32[]{:S(2)}, u32[]{:S(2)}) collective-permute-start(f32[8,8,128]{2,1,0:T(8,128)S(1)} %reduce_sum.9), channel_id=1, source_target_pairs={{0,6},{2,4},{4,2},{6,0},{1,7},{3,5},{5,3},{7,1},{8,14},{10,12},{12... | collective-permute-start | bytes 98312 | tf_op jit(solution)/shard_map/ppermute | solution.py:314
  50.9 1.2 %collective-permute-start.6 = (f32[8,8,128]{2,1,0:T(8,128)S(1)}, f32[8,8,128]{2,1,0:T(8,128)S(1)}, u32[]{:S(2)}, u32[]{:S(2)}) collective-permute-start(f32[8,8,128]{2,1,0:T(8,128)S(1)} %reduce_sum.9), channel_id=1, source_target_pairs={{0,4},{2,6},{4,0},{6,2},{1,5},{3,7},{5,1},{7,3},{8,12},{10,14},{12... | collective-permute-start | bytes 98312 | tf_op jit(solution)/shard_map/ppermute | solution.py:314
  52.0 1.0 %collective-permute-start.5 = (f32[8,8,128]{2,1,0:T(8,128)S(1)}, f32[8,8,128]{2,1,0:T(8,128)S(1)}, u32[]{:S(2)}, u32[]{:S(2)}) collective-permute-start(f32[8,8,128]{2,1,0:T(8,128)S(1)} %reduce_sum.9), channel_id=1, source_target_pairs={{0,2},{2,0},{4,6},{6,4},{1,3},{3,1},{5,7},{7,5},{8,10},{10,8},{12,... | collective-permute-start | bytes 98312 | tf_op jit(solution)/shard_map/ppermute | solution.py:314
  53.0 0.0 collective-permute-done.7
  53.0 5.0 %collective-permute-done.6 = f32[8,8,128]{2,1,0:T(8,128)S(1)} collective-permute-done((f32[8,8,128]{2,1,0:T(8,128)S(1)}, f32[8,8,128]{2,1,0:T(8,128)S(1)}, u32[]{:S(2)}, u32[]{:S(2)}) %collective-permute-start.6) | collective-permute-done | bytes 32800 | tf_op jit(solution)/shard_map/ppermute | solution.py:314
  58.0 0.0 collective-permute-done.5
  58.1 1.0 %broadcast_in_dim.4 = f32[32,7,8,128]{3,2,1,0:T(8,128)} broadcast(f32[7,8,128]{2,1,0:T(8,128)S(1)} %slice.8), dimensions={1,2,3} | broadcast | bytes 946176 | tf_op jit(solution)/shard_map/broadcast_in_dim | solution.py:319
  59.1 3.9 %all-to-all-start.1 = ((f32[32,7,8,128]{3,2,1,0:T(8,128)}), f32[32,7,8,128]{3,2,1,0:T(8,128)S(1)}, u32[]{:S(2)}, u32[]{:S(2)}) async-start(f32[32,7,8,128]{3,2,1,0:T(8,128)} %broadcast_in_dim.4), calls=%async_computation.1 | async-start | bytes 1835008 | tf_op jit(solution)/shard_map/all_to_all | solution.py:306
  63.0 14.0 %all-to-all-done.1 = f32[32,7,8,128]{3,2,1,0:T(8,128)S(1)} async-done(((f32[32,7,8,128]{3,2,1,0:T(8,128)}), f32[32,7,8,128]{3,2,1,0:T(8,128)S(1)}, u32[]{:S(2)}, u32[]{:S(2)}) %all-to-all-start.1) | async-done | bytes 917536 | tf_op jit(solution)/shard_map/all_to_all | solution.py:306
  77.0 0.0 copy-start.1
  77.0 0.0 copy-start.2
  77.0 3.4 %collective-permute-start.8 = (f32[16,2,7,8,128]{4,3,2,1,0:T(8,128)S(1)}, f32[16,2,7,8,128]{4,3,2,1,0:T(8,128)S(1)}, u32[]{:S(2)}, u32[]{:S(2)}) collective-permute-start(f32[16,2,7,8,128]{4,3,2,1,0:T(8,128)S(1)} %bitcast.13), channel_id=1, source_target_pairs={{0,32},{32,0},{1,33},{33,1},{2,34},{34,2},{3,35},{35,3},{4,36},{36... | collective-permute-start | bytes 2752520 | tf_op jit(solution)/shard_map/ppermute | solution.py:310
  80.5 1.9 %factor.1 = (f32[32,128]{1,0:T(8,128)}, f32[32,128]{1,0:T(8,128)S(1)}, bf16[128,256]{1,0:T(8,128)(2,1)S(1)}) custom-call(s32[3]{0:T(128)S(1)} %pad_add_fusion.ids_ref, f32[8,128]{1,0:T(8,128)S(1)} %slice_bitcast_fusion.gram_ref, f32[32,128]{1,0:T(8,128)S(1)} %add.23.refs_0_, f32[32,128]{1,0:T(8,128)S(1)} %collective-permute-done.1.refs_1_, ...), custom_call_target="tpu_custom_call" | custom-call | flops 20000000000 | bytes 10000000 | tf_op jit(solution)/shard_map/factor/pallas_call | solution.py:221
  82.4 0.2 collective-permute-done.8.other_ref
  82.6 0.0 copy-done.1
  82.6 0.0 copy-done.2
  82.6 4.0 %finish.1 = (f32[32,448]{1,0:T(8,128)}, bf16[128,14336]{1,0:T(8,128)(2,1)}) custom-call(s32[3]{0:T(128)S(1)} %pad_add_fusion.ids_ref, f32[16,2,7,8,128]{4,3,2,1,0:T(8,128)S(1)} %bitcast.14, f32[16,2,7,8,128]{4,3,2,1,0:T(8,128)S(1)} %collective-permute-done.8.other_ref, f32[32,128]{1,0:T(8,128)S(1)} %get-tuple-element.27.inverse_ref, ...), custom_call_target="tpu_custom_call" | custom-call | tf_op jit(solution)/shard_map/finish/pallas_call | solution.py:291
  (4 shorter events, 0.0 us)
Async XLA Ops:
  0.6 3.8 %copy-start = (bf16[1,128,14336]{2,1,0:T(8,128)(2,1)S(1)}, bf16[1,128,14336]{2,1,0:T(8,128)(2,1)}, u32[]{:S(2)}) copy-start(bf16[1,128,14336]{2,1,0:T(8,128)(2,1)} %param.4) | copy-start | bytes 11010052
  5.8 4.1 %collective-permute-start = (f32[32,128]{1,0:T(8,128)S(1)}, f32[32,128]{1,0:T(8,128)S(1)}, u32[]{:S(2)}, u32[]{:S(2)}) collective-permute-start(f32[32,128]{1,0:T(8,128)S(1)} %left_second.1), channel_id=1, source_target_pairs={{0,32},{32,0},{1,33},{33,1},{2,34},{34,2},{3,35},{35,3},{4,36},{36... | collective-permute-start | bytes 49160 | tf_op jit(solution)/shard_map/ppermute | solution.py:310
  10.0 3.8 %collective-permute-start.3 = (f32[32,128]{1,0:T(8,128)S(1)}, f32[32,128]{1,0:T(8,128)S(1)}, u32[]{:S(2)}, u32[]{:S(2)}) collective-permute-start(f32[32,128]{1,0:T(8,128)S(1)} %add.23.refs_0_), channel_id=1, source_target_pairs={{0,192},{64,128},{128,64},{192,0},{1,193},{65,129},{129,65},{193,1... | collective-permute-start | bytes 49160 | tf_op jit(solution)/shard_map/ppermute | solution.py:314
  11.0 4.1 %collective-permute-start.2 = (f32[32,128]{1,0:T(8,128)S(1)}, f32[32,128]{1,0:T(8,128)S(1)}, u32[]{:S(2)}, u32[]{:S(2)}) collective-permute-start(f32[32,128]{1,0:T(8,128)S(1)} %add.23.refs_0_), channel_id=1, source_target_pairs={{0,128},{64,192},{128,0},{192,64},{1,129},{65,193},{129,1},{193,65... | collective-permute-start | bytes 49160 | tf_op jit(solution)/shard_map/ppermute | solution.py:314
  11.3 3.7 %collective-permute-start.1 = (f32[32,128]{1,0:T(8,128)S(1)}, f32[32,128]{1,0:T(8,128)S(1)}, u32[]{:S(2)}, u32[]{:S(2)}) collective-permute-start(f32[32,128]{1,0:T(8,128)S(1)} %add.23.refs_0_), channel_id=1, source_target_pairs={{0,64},{64,0},{128,192},{192,128},{1,65},{65,1},{129,193},{193,129... | collective-permute-start | bytes 49160 | tf_op jit(solution)/shard_map/ppermute | solution.py:314
  17.3 4.1 %collective-permute-start.4 = (f32[16,2,8,8,128]{4,3,2,1,0:T(8,128)S(1)}, f32[16,2,8,8,128]{4,3,2,1,0:T(8,128)S(1)}, u32[]{:S(2)}, u32[]{:S(2)}) collective-permute-start(f32[16,2,8,8,128]{4,3,2,1,0:T(8,128)S(1)} %get-tuple-element.23), channel_id=1, source_target_pairs={{0,32},{32,0},{1,33},{33,1},{2,34},{34,2},{3,35},{35,3},{4,36},{36... | collective-permute-start | bytes 3145736 | tf_op jit(solution)/shard_map/ppermute | solution.py:310
  45.6 7.4 %collective-permute-start.7 = (f32[8,8,128]{2,1,0:T(8,128)S(1)}, f32[8,8,128]{2,1,0:T(8,128)S(1)}, u32[]{:S(2)}, u32[]{:S(2)}) collective-permute-start(f32[8,8,128]{2,1,0:T(8,128)S(1)} %reduce_sum.9), channel_id=1, source_target_pairs={{0,6},{2,4},{4,2},{6,0},{1,7},{3,5},{5,3},{7,1},{8,14},{10,12},{12... | collective-permute-start | bytes 98312 | tf_op jit(solution)/shard_map/ppermute | solution.py:314
  50.9 7.2 %collective-permute-start.6 = (f32[8,8,128]{2,1,0:T(8,128)S(1)}, f32[8,8,128]{2,1,0:T(8,128)S(1)}, u32[]{:S(2)}, u32[]{:S(2)}) collective-permute-start(f32[8,8,128]{2,1,0:T(8,128)S(1)} %reduce_sum.9), channel_id=1, source_target_pairs={{0,4},{2,6},{4,0},{6,2},{1,5},{3,7},{5,1},{7,3},{8,12},{10,14},{12... | collective-permute-start | bytes 98312 | tf_op jit(solution)/shard_map/ppermute | solution.py:314
  52.0 6.0 %collective-permute-start.5 = (f32[8,8,128]{2,1,0:T(8,128)S(1)}, f32[8,8,128]{2,1,0:T(8,128)S(1)}, u32[]{:S(2)}, u32[]{:S(2)}) collective-permute-start(f32[8,8,128]{2,1,0:T(8,128)S(1)} %reduce_sum.9), channel_id=1, source_target_pairs={{0,2},{2,0},{4,6},{6,4},{1,3},{3,1},{5,7},{7,5},{8,10},{10,8},{12,... | collective-permute-start | bytes 98312 | tf_op jit(solution)/shard_map/ppermute | solution.py:314
  59.1 18.0 %all-to-all-start.1 = ((f32[32,7,8,128]{3,2,1,0:T(8,128)}), f32[32,7,8,128]{3,2,1,0:T(8,128)S(1)}, u32[]{:S(2)}, u32[]{:S(2)}) async-start(f32[32,7,8,128]{3,2,1,0:T(8,128)} %broadcast_in_dim.4), calls=%async_computation.1 | async-start | bytes 1835008 | tf_op jit(solution)/shard_map/all_to_all | solution.py:306
  77.0 5.5 %copy-start.1 = (bf16[1,128,14336]{2,1,0:T(8,128)(2,1)S(1)}, bf16[1,128,14336]{2,1,0:T(8,128)(2,1)}, u32[]{:S(2)}) copy-start(bf16[1,128,14336]{2,1,0:T(8,128)(2,1)} %param.4) | copy-start | bytes 11010052
  77.0 5.5 %copy-start.2 = (bf16[1,128,14336]{2,1,0:T(8,128)(2,1)S(1)}, bf16[1,128,14336]{2,1,0:T(8,128)(2,1)}, u32[]{:S(2)}) copy-start(bf16[1,128,14336]{2,1,0:T(8,128)(2,1)} %param.3) | copy-start | bytes 11010052
  77.0 5.5 %collective-permute-start.8 = (f32[16,2,7,8,128]{4,3,2,1,0:T(8,128)S(1)}, f32[16,2,7,8,128]{4,3,2,1,0:T(8,128)S(1)}, u32[]{:S(2)}, u32[]{:S(2)}) collective-permute-start(f32[16,2,7,8,128]{4,3,2,1,0:T(8,128)S(1)} %bitcast.13), channel_id=1, source_target_pairs={{0,32},{32,0},{1,33},{33,1},{2,34},{34,2},{3,35},{35,3},{4,36},{36... | collective-permute-start | bytes 2752520 | tf_op jit(solution)/shard_map/ppermute | solution.py:310

commit v8 on v7

--- a/solution.py
+++ b/solution.py
@@ -128,7 +128,7 @@
     left = jnp.concatenate(three_parts(ordered), axis=0).astype(BF16)
     left = jnp.concatenate([left, left], axis=1)
 
-    @pl.loop(0, STEPS, unroll=2)
+    @pl.loop(0, STEPS, unroll=4)
     def _(step):
         cols = pl.ds(pl.multiple_of(step * STEP_WIDTH, 128), STEP_WIDTH)
         both = jnp.concatenate([grad_ref[:, cols], memory_ref[:, cols]], axis=0)

time: 86.8 us -> 86.5 us (level)
  no operation moved by 1% of the time
where the time goes in v8:
time: 86.5 us; the launch traced here: 86.3 us
  waiting for transfers between devices  24.2 us (28%)
  blocking collectives  24 us (28%)
  starting transfers between devices  23.2 us (27%)
  Pallas kernels  12.9 us (15%)
  local copies, waits for them, and re-layouts  1 us (1%)
    all_to_all x1, blocking collectives, exchange(): return lax.all_to_all(value, axes, 0, 0, tiled=True)  24 us
    all_to_all x1, waiting for transfers between devices, exchange(): return lax.all_to_all(value, axes, 0, 0, tiled=True)  14 us
    ppermute x6, starting transfers between devices, four(): lax.ppermute(value, axes, [(i, i ^ k) for i in range(4)])  10.6 us
    ppermute x3, starting transfers between devices, swap(): return lax.ppermute(value, 'c', [(0, 1), (1, 0)])  8.59 us
    ppermute x6, waiting for transfers between devices, four(): lax.ppermute(value, axes, [(i, i ^ k) for i in range(4)])  6.85 us
    pallas_call x1, Pallas kernels, finish(): pl.pallas_call(update_kernel, out_shape=(jax.ShapeDtypeStruct((RANK, WIDT...  3.96 us
    all_to_all x1, starting transfers between devices, exchange(): return lax.all_to_all(value, axes, 0, 0, tiled=True)  3.92 us
    pallas_call x1, Pallas kernels, left_sketch(): pl.pallas_call(first_kernel, out_shape=(jax.ShapeDtypeStruct((RANK, ROWS)...  3.73 us
  transfers between devices with their start and end apart: 10, of which 7 were waited for; matrix products, arithmetic and copies ran while one was open for 0% of the time, Pallas kernels for 2%

profile of v8, /device:TPU:1, one launch (start us, length us, event | category | flops | bytes accessed | tf_op | source)
XLA Modules:
  0.0 86.3 jit_solution(4899783554308224367)
XLA Ops:
  0.6 0.0 copy-start
  0.7 3.7 %left_first.1 = (f32[32,128]{1,0:T(8,128)S(1)}, bf16[128,14336]{1,0:T(8,128)(2,1)S(1)}, bf16[32,14336]{1,0:T(8,128)(2,1)S(1)}) custom-call(bf16[128,14336]{1,0:T(8,128)(2,1)} %bitcast.15, bf16[32,14336]{1,0:T(8,128)(2,1)} %sketch_hbm.1), custom_call_target="tpu_custom_call" | custom-call | flops 20000000000 | bytes 10000000 | tf_op jit(solution)/shard_map/left_first/pallas_call | solution.py:75
  4.4 0.1 pad_add_fusion.ids_ref
  4.5 0.0 copy-done
  4.5 1.4 %left_second.1 = f32[32,128]{1,0:T(8,128)S(1)} custom-call(f32[32,128]{1,0:T(8,128)S(1)} %get-tuple-element.17.first_ref, bf16[32,14336]{1,0:T(8,128)(2,1)S(1)} %get-tuple-element.18.sketch_ref, bf16[128,14336]{1,0:T(8,128)(2,1)S(1)} %bitcast.10), custom_call_target="tpu_custom_call" | custom-call | tf_op jit(solution)/shard_map/left_second/pallas_call | solution.py:89
  5.8 3.3 %collective-permute-start = (f32[32,128]{1,0:T(8,128)S(1)}, f32[32,128]{1,0:T(8,128)S(1)}, u32[]{:S(2)}, u32[]{:S(2)}) collective-permute-start(f32[32,128]{1,0:T(8,128)S(1)} %left_second.1), channel_id=1, source_target_pairs={{0,32},{32,0},{1,33},{33,1},{2,34},{34,2},{3,35},{35,3},{4,36},{36... | collective-permute-start | bytes 49160 | tf_op jit(solution)/shard_map/ppermute | solution.py:310
  9.1 0.8 collective-permute-done
  10.0 1.0 %collective-permute-start.3 = (f32[32,128]{1,0:T(8,128)S(1)}, f32[32,128]{1,0:T(8,128)S(1)}, u32[]{:S(2)}, u32[]{:S(2)}) collective-permute-start(f32[32,128]{1,0:T(8,128)S(1)} %add.23.refs_0_), channel_id=1, source_target_pairs={{0,192},{64,128},{128,64},{192,0},{1,193},{65,129},{129,65},{193,1... | collective-permute-start | bytes 49160 | tf_op jit(solution)/shard_map/ppermute | solution.py:314
  11.0 0.3 collective-permute-start.2
  11.3 1.9 %collective-permute-start.1 = (f32[32,128]{1,0:T(8,128)S(1)}, f32[32,128]{1,0:T(8,128)S(1)}, u32[]{:S(2)}, u32[]{:S(2)}) collective-permute-start(f32[32,128]{1,0:T(8,128)S(1)} %add.23.refs_0_), channel_id=1, source_target_pairs={{0,64},{64,0},{128,192},{192,128},{1,65},{65,1},{129,193},{193,129... | collective-permute-start | bytes 49160 | tf_op jit(solution)/shard_map/ppermute | solution.py:314
  13.2 0.5 collective-permute-done.3.refs_3_
  13.8 1.3 %collective-permute-done.2.refs_2_ = f32[32,128]{1,0:T(8,128)S(1)} collective-permute-done((f32[32,128]{1,0:T(8,128)S(1)}, f32[32,128]{1,0:T(8,128)S(1)}, u32[]{:S(2)}, u32[]{:S(2)}) %collective-permute-start.2) | collective-permute-done | bytes 16416 | tf_op jit(solution)/shard_map/ppermute | solution.py:314
  15.1 0.0 collective-permute-done.1.refs_1_
  15.1 1.9 %project.1 = (f32[16,2,8,8,128]{4,3,2,1,0:T(8,128)S(1)}, f32[16,2,8,8,128]{4,3,2,1,0:T(8,128)S(1)}) custom-call(s32[3]{0:T(128)S(1)} %pad_add_fusion.ids_ref, f32[32,128]{1,0:T(8,128)S(1)} %add.23.refs_0_, f32[32,128]{1,0:T(8,128)S(1)} %collective-permute-done.1.refs_1_, f32[32,128]{1,0:T(8,128)S(1)} %collective-permute-done.2.refs_2_, ...), custom_call_target="tpu_custom_call" | custom-call | tf_op jit(solution)/shard_map/project/pallas_call | solution.py:150
  17.0 1.9 %collective-permute-start.4 = (f32[16,2,8,8,128]{4,3,2,1,0:T(8,128)S(1)}, f32[16,2,8,8,128]{4,3,2,1,0:T(8,128)S(1)}, u32[]{:S(2)}, u32[]{:S(2)}) collective-permute-start(f32[16,2,8,8,128]{4,3,2,1,0:T(8,128)S(1)} %get-tuple-element.23), channel_id=1, source_target_pairs={{0,32},{32,0},{1,33},{33,1},{2,34},{34,2},{3,35},{35,3},{4,36},{36... | collective-permute-start | bytes 3145736 | tf_op jit(solution)/shard_map/ppermute | solution.py:310
  18.9 2.3 %collective-permute-done.4 = f32[16,2,8,8,128]{4,3,2,1,0:T(8,128)S(1)} collective-permute-done((f32[16,2,8,8,128]{4,3,2,1,0:T(8,128)S(1)}, f32[16,2,8,8,128]{4,3,2,1,0:T(8,128)S(1)}, u32[]{:S(2)}, u32[]{:S(2)}) %collective-permute-start.4) | collective-permute-done | bytes 1048608 | tf_op jit(solution)/shard_map/ppermute | solution.py:310
  21.1 0.2 add.24
  21.3 24.0 %all_to_all.10 = f32[32,8,8,128]{3,2,1,0:T(8,128)S(1)} all-to-all(f32[32,8,8,128]{3,2,1,0:T(8,128)S(1)} %bitcast.17), channel_id=1, replica_groups=mesh['y'=4,'c'=2,'x'=4,'z4'=2,'z2'=2,'z1'=2] {'y','x','z1'}, dimensions={0} | all-to-all | bytes 2097152 | tf_op jit(solution)/shard_map/all_to_all | solution.py:306
  45.3 0.1 reduce_sum.9
  45.4 5.2 %collective-permute-start.7 = (f32[8,8,128]{2,1,0:T(8,128)S(1)}, f32[8,8,128]{2,1,0:T(8,128)S(1)}, u32[]{:S(2)}, u32[]{:S(2)}) collective-permute-start(f32[8,8,128]{2,1,0:T(8,128)S(1)} %reduce_sum.9), channel_id=1, source_target_pairs={{0,6},{2,4},{4,2},{6,0},{1,7},{3,5},{5,3},{7,1},{8,14},{10,12},{12... | collective-permute-start | bytes 98312 | tf_op jit(solution)/shard_map/ppermute | solution.py:314
  50.6 1.2 %collective-permute-start.6 = (f32[8,8,128]{2,1,0:T(8,128)S(1)}, f32[8,8,128]{2,1,0:T(8,128)S(1)}, u32[]{:S(2)}, u32[]{:S(2)}) collective-permute-start(f32[8,8,128]{2,1,0:T(8,128)S(1)} %reduce_sum.9), channel_id=1, source_target_pairs={{0,4},{2,6},{4,0},{6,2},{1,5},{3,7},{5,1},{7,3},{8,12},{10,14},{12... | collective-permute-start | bytes 98312 | tf_op jit(solution)/shard_map/ppermute | solution.py:314
  51.7 1.0 %collective-permute-start.5 = (f32[8,8,128]{2,1,0:T(8,128)S(1)}, f32[8,8,128]{2,1,0:T(8,128)S(1)}, u32[]{:S(2)}, u32[]{:S(2)}) collective-permute-start(f32[8,8,128]{2,1,0:T(8,128)S(1)} %reduce_sum.9), channel_id=1, source_target_pairs={{0,2},{2,0},{4,6},{6,4},{1,3},{3,1},{5,7},{7,5},{8,10},{10,8},{12,... | collective-permute-start | bytes 98312 | tf_op jit(solution)/shard_map/ppermute | solution.py:314
  52.8 0.0 collective-permute-done.7
  52.8 5.0 %collective-permute-done.6 = f32[8,8,128]{2,1,0:T(8,128)S(1)} collective-permute-done((f32[8,8,128]{2,1,0:T(8,128)S(1)}, f32[8,8,128]{2,1,0:T(8,128)S(1)}, u32[]{:S(2)}, u32[]{:S(2)}) %collective-permute-start.6) | collective-permute-done | bytes 32800 | tf_op jit(solution)/shard_map/ppermute | solution.py:314
  57.8 0.0 collective-permute-done.5
  57.8 1.0 %broadcast_in_dim.4 = f32[32,7,8,128]{3,2,1,0:T(8,128)} broadcast(f32[7,8,128]{2,1,0:T(8,128)S(1)} %slice.8), dimensions={1,2,3} | broadcast | bytes 946176 | tf_op jit(solution)/shard_map/broadcast_in_dim | solution.py:319
  58.8 3.9 %all-to-all-start.1 = ((f32[32,7,8,128]{3,2,1,0:T(8,128)}), f32[32,7,8,128]{3,2,1,0:T(8,128)S(1)}, u32[]{:S(2)}, u32[]{:S(2)}) async-start(f32[32,7,8,128]{3,2,1,0:T(8,128)} %broadcast_in_dim.4), calls=%async_computation.1 | async-start | bytes 1835008 | tf_op jit(solution)/shard_map/all_to_all | solution.py:306
  62.7 14.0 %all-to-all-done.1 = f32[32,7,8,128]{3,2,1,0:T(8,128)S(1)} async-done(((f32[32,7,8,128]{3,2,1,0:T(8,128)}), f32[32,7,8,128]{3,2,1,0:T(8,128)S(1)}, u32[]{:S(2)}, u32[]{:S(2)}) %all-to-all-start.1) | async-done | bytes 917536 | tf_op jit(solution)/shard_map/all_to_all | solution.py:306
  76.8 0.0 copy-start.1
  76.8 0.0 copy-start.2
  76.8 3.4 %collective-permute-start.8 = (f32[16,2,7,8,128]{4,3,2,1,0:T(8,128)S(1)}, f32[16,2,7,8,128]{4,3,2,1,0:T(8,128)S(1)}, u32[]{:S(2)}, u32[]{:S(2)}) collective-permute-start(f32[16,2,7,8,128]{4,3,2,1,0:T(8,128)S(1)} %bitcast.13), channel_id=1, source_target_pairs={{0,32},{32,0},{1,33},{33,1},{2,34},{34,2},{3,35},{35,3},{4,36},{36... | collective-permute-start | bytes 2752520 | tf_op jit(solution)/shard_map/ppermute | solution.py:310
  80.2 1.9 %factor.1 = (f32[32,128]{1,0:T(8,128)}, f32[32,128]{1,0:T(8,128)S(1)}, bf16[128,256]{1,0:T(8,128)(2,1)S(1)}) custom-call(s32[3]{0:T(128)S(1)} %pad_add_fusion.ids_ref, f32[8,128]{1,0:T(8,128)S(1)} %slice_bitcast_fusion.gram_ref, f32[32,128]{1,0:T(8,128)S(1)} %add.23.refs_0_, f32[32,128]{1,0:T(8,128)S(1)} %collective-permute-done.1.refs_1_, ...), custom_call_target="tpu_custom_call" | custom-call | flops 20000000000 | bytes 10000000 | tf_op jit(solution)/shard_map/factor/pallas_call | solution.py:221
  82.1 0.2 collective-permute-done.8.other_ref
  82.3 0.0 copy-done.1
  82.3 0.0 copy-done.2
  82.3 4.0 %finish.1 = (f32[32,448]{1,0:T(8,128)}, bf16[128,14336]{1,0:T(8,128)(2,1)}) custom-call(s32[3]{0:T(128)S(1)} %pad_add_fusion.ids_ref, f32[16,2,7,8,128]{4,3,2,1,0:T(8,128)S(1)} %bitcast.14, f32[16,2,7,8,128]{4,3,2,1,0:T(8,128)S(1)} %collective-permute-done.8.other_ref, f32[32,128]{1,0:T(8,128)S(1)} %get-tuple-element.27.inverse_ref, ...), custom_call_target="tpu_custom_call" | custom-call | tf_op jit(solution)/shard_map/finish/pallas_call | solution.py:291
  (4 shorter events, 0.0 us)
Async XLA Ops:
  0.6 3.8 %copy-start = (bf16[1,128,14336]{2,1,0:T(8,128)(2,1)S(1)}, bf16[1,128,14336]{2,1,0:T(8,128)(2,1)}, u32[]{:S(2)}) copy-start(bf16[1,128,14336]{2,1,0:T(8,128)(2,1)} %param.4) | copy-start | bytes 11010052
  5.8 4.1 %collective-permute-start = (f32[32,128]{1,0:T(8,128)S(1)}, f32[32,128]{1,0:T(8,128)S(1)}, u32[]{:S(2)}, u32[]{:S(2)}) collective-permute-start(f32[32,128]{1,0:T(8,128)S(1)} %left_second.1), channel_id=1, source_target_pairs={{0,32},{32,0},{1,33},{33,1},{2,34},{34,2},{3,35},{35,3},{4,36},{36... | collective-permute-start | bytes 49160 | tf_op jit(solution)/shard_map/ppermute | solution.py:310
  10.0 3.8 %collective-permute-start.3 = (f32[32,128]{1,0:T(8,128)S(1)}, f32[32,128]{1,0:T(8,128)S(1)}, u32[]{:S(2)}, u32[]{:S(2)}) collective-permute-start(f32[32,128]{1,0:T(8,128)S(1)} %add.23.refs_0_), channel_id=1, source_target_pairs={{0,192},{64,128},{128,64},{192,0},{1,193},{65,129},{129,65},{193,1... | collective-permute-start | bytes 49160 | tf_op jit(solution)/shard_map/ppermute | solution.py:314
  11.0 4.1 %collective-permute-start.2 = (f32[32,128]{1,0:T(8,128)S(1)}, f32[32,128]{1,0:T(8,128)S(1)}, u32[]{:S(2)}, u32[]{:S(2)}) collective-permute-start(f32[32,128]{1,0:T(8,128)S(1)} %add.23.refs_0_), channel_id=1, source_target_pairs={{0,128},{64,192},{128,0},{192,64},{1,129},{65,193},{129,1},{193,65... | collective-permute-start | bytes 49160 | tf_op jit(solution)/shard_map/ppermute | solution.py:314
  11.3 3.7 %collective-permute-start.1 = (f32[32,128]{1,0:T(8,128)S(1)}, f32[32,128]{1,0:T(8,128)S(1)}, u32[]{:S(2)}, u32[]{:S(2)}) collective-permute-start(f32[32,128]{1,0:T(8,128)S(1)} %add.23.refs_0_), channel_id=1, source_target_pairs={{0,64},{64,0},{128,192},{192,128},{1,65},{65,1},{129,193},{193,129... | collective-permute-start | bytes 49160 | tf_op jit(solution)/shard_map/ppermute | solution.py:314
  17.0 4.1 %collective-permute-start.4 = (f32[16,2,8,8,128]{4,3,2,1,0:T(8,128)S(1)}, f32[16,2,8,8,128]{4,3,2,1,0:T(8,128)S(1)}, u32[]{:S(2)}, u32[]{:S(2)}) collective-permute-start(f32[16,2,8,8,128]{4,3,2,1,0:T(8,128)S(1)} %get-tuple-element.23), channel_id=1, source_target_pairs={{0,32},{32,0},{1,33},{33,1},{2,34},{34,2},{3,35},{35,3},{4,36},{36... | collective-permute-start | bytes 3145736 | tf_op jit(solution)/shard_map/ppermute | solution.py:310
  45.4 7.4 %collective-permute-start.7 = (f32[8,8,128]{2,1,0:T(8,128)S(1)}, f32[8,8,128]{2,1,0:T(8,128)S(1)}, u32[]{:S(2)}, u32[]{:S(2)}) collective-permute-start(f32[8,8,128]{2,1,0:T(8,128)S(1)} %reduce_sum.9), channel_id=1, source_target_pairs={{0,6},{2,4},{4,2},{6,0},{1,7},{3,5},{5,3},{7,1},{8,14},{10,12},{12... | collective-permute-start | bytes 98312 | tf_op jit(solution)/shard_map/ppermute | solution.py:314
  50.6 7.2 %collective-permute-start.6 = (f32[8,8,128]{2,1,0:T(8,128)S(1)}, f32[8,8,128]{2,1,0:T(8,128)S(1)}, u32[]{:S(2)}, u32[]{:S(2)}) collective-permute-start(f32[8,8,128]{2,1,0:T(8,128)S(1)} %reduce_sum.9), channel_id=1, source_target_pairs={{0,4},{2,6},{4,0},{6,2},{1,5},{3,7},{5,1},{7,3},{8,12},{10,14},{12... | collective-permute-start | bytes 98312 | tf_op jit(solution)/shard_map/ppermute | solution.py:314
  51.7 6.0 %collective-permute-start.5 = (f32[8,8,128]{2,1,0:T(8,128)S(1)}, f32[8,8,128]{2,1,0:T(8,128)S(1)}, u32[]{:S(2)}, u32[]{:S(2)}) collective-permute-start(f32[8,8,128]{2,1,0:T(8,128)S(1)} %reduce_sum.9), channel_id=1, source_target_pairs={{0,2},{2,0},{4,6},{6,4},{1,3},{3,1},{5,7},{7,5},{8,10},{10,8},{12,... | collective-permute-start | bytes 98312 | tf_op jit(solution)/shard_map/ppermute | solution.py:314
  58.8 18.0 %all-to-all-start.1 = ((f32[32,7,8,128]{3,2,1,0:T(8,128)}), f32[32,7,8,128]{3,2,1,0:T(8,128)S(1)}, u32[]{:S(2)}, u32[]{:S(2)}) async-start(f32[32,7,8,128]{3,2,1,0:T(8,128)} %broadcast_in_dim.4), calls=%async_computation.1 | async-start | bytes 1835008 | tf_op jit(solution)/shard_map/all_to_all | solution.py:306
  76.8 5.5 %copy-start.1 = (bf16[1,128,14336]{2,1,0:T(8,128)(2,1)S(1)}, bf16[1,128,14336]{2,1,0:T(8,128)(2,1)}, u32[]{:S(2)}) copy-start(bf16[1,128,14336]{2,1,0:T(8,128)(2,1)} %param.4) | copy-start | bytes 11010052
  76.8 5.5 %copy-start.2 = (bf16[1,128,14336]{2,1,0:T(8,128)(2,1)S(1)}, bf16[1,128,14336]{2,1,0:T(8,128)(2,1)}, u32[]{:S(2)}) copy-start(bf16[1,128,14336]{2,1,0:T(8,128)(2,1)} %param.3) | copy-start | bytes 11010052
  76.8 5.5 %collective-permute-start.8 = (f32[16,2,7,8,128]{4,3,2,1,0:T(8,128)S(1)}, f32[16,2,7,8,128]{4,3,2,1,0:T(8,128)S(1)}, u32[]{:S(2)}, u32[]{:S(2)}) collective-permute-start(f32[16,2,7,8,128]{4,3,2,1,0:T(8,128)S(1)} %bitcast.13), channel_id=1, source_target_pairs={{0,32},{32,0},{1,33},{33,1},{2,34},{34,2},{3,35},{35,3},{4,36},{36... | collective-permute-start | bytes 2752520 | tf_op jit(solution)/shard_map/ppermute | solution.py:310
